TPU v7x, 32 devices: a whole 2x2x4 slice. The times are simulated.
32 devices in a mesh: fsdp: 8 (over y, x, core), rep: 4 (over z).
Axes of the slice: x: 2, y: 2, z: 4, core: 2. Of those that a mesh axis runs over, the one named last changes fastest.
Arguments:
- tokens: bfloat16 [64, 237, 768], P(('fsdp', 'rep')), may hold values from -6 to 6
- out_grad: bfloat16 [64, 237, 768], P(('fsdp', 'rep')), may hold values from -6 to 6
- masked: int32 [64, 40], P(('fsdp', 'rep')), may hold values from 0 to 1, as said below
- lengths: int32 [64], P(('fsdp', 'rep')), may hold values from 8 to 40, as said below
- mask_vec: bfloat16 [768], P('fsdp'), may hold values from -6 to 6
- norm1_gain: bfloat16 [768], P('fsdp'), may hold values from 0.099609375 to 1.8984375
- norm1_shift: bfloat16 [768], P('fsdp'), may hold values from -4 to 4
- w_qkv: bfloat16 [768, 2304], P('fsdp'), may hold values from -0.21875 to 0.21875
- query_bias: bfloat16 [768], P('fsdp'), may hold values from -4 to 4
- value_bias: bfloat16 [768], P('fsdp'), may hold values from -4 to 4
- w_out: bfloat16 [768, 768], P('fsdp'), may hold values from -0.875 to 0.875
- out_bias: bfloat16 [768], P('fsdp'), may hold values from -4 to 4
- norm2_gain: bfloat16 [768], P('fsdp'), may hold values from 0.099609375 to 1.8984375
- norm2_shift: bfloat16 [768], P('fsdp'), may hold values from -4 to 4
- vision_up: bfloat16 [768, 3072], P('fsdp'), may hold values from -0.21875 to 0.21875
- vision_up_bias: bfloat16 [3072], P('fsdp'), may hold values from -4 to 4
- vision_down: bfloat16 [3072, 768], P('fsdp'), may hold values from -0.21875 to 0.21875
- vision_down_bias: bfloat16 [768], P('fsdp'), may hold values from -4 to 4
- text_up: bfloat16 [768, 3072], P('fsdp'), may hold values from -0.21875 to 0.21875
- text_up_bias: bfloat16 [3072], P('fsdp'), may hold values from -4 to 4
- text_down: bfloat16 [3072, 768], P('fsdp'), may hold values from -0.21875 to 0.21875
- text_down_bias: bfloat16 [768], P('fsdp'), may hold values from -4 to 4
Outputs:
- mixed: bfloat16 [64, 237, 768], P(('fsdp', 'rep'))
- grad_tokens: float32 [64, 237, 768], P(('fsdp', 'rep'))
- grad_mask_vec: float32 [768], P('fsdp')
- grad_norm1_gain: float32 [768], P('fsdp')
- grad_norm1_shift: float32 [768], P('fsdp')
- grad_w_qkv: float32 [768, 2304], P('fsdp')
- grad_query_bias: float32 [768], P('fsdp')
- grad_value_bias: float32 [768], P('fsdp')
- grad_w_out: float32 [768, 768], P('fsdp')
- grad_out_bias: float32 [768], P('fsdp')
- grad_norm2_gain: float32 [768], P('fsdp')
- grad_norm2_shift: float32 [768], P('fsdp')
- grad_vision_up: float32 [768, 3072], P('fsdp')
- grad_vision_up_bias: float32 [3072], P('fsdp')
- grad_vision_down: float32 [3072, 768], P('fsdp')
- grad_vision_down_bias: float32 [768], P('fsdp')
- grad_text_up: float32 [768, 3072], P('fsdp')
- grad_text_up_bias: float32 [3072], P('fsdp')
- grad_text_down: float32 [3072, 768], P('fsdp')
- grad_text_down_bias: float32 [768], P('fsdp')
Inputs may be any that keep to these rules, and one draw needn't show every extreme that they name: A caption fills the first lengths slots of its item; in every draw some item fills all 40 slots. Only slots below the item's length are masked; an item masks between 15 and 80 percent of its length, rounded down, and at least one slot.
All inputs are finite; a program needn't handle non-finite values.
Results may differ from a plain program's by a relative error of at most 0.017.
Values may be sent and summed in bfloat16 or wider, within the bound.
No kernel may reach another device: no remote copies, remote signals or barrier semaphores. Data moves between devices by JAX's collectives and lax.ppermute only.
A program may use at most 192 MiB of HBM per device.

v0:
```python
import functools
import math

import jax
import jax.numpy as jnp
from jax import lax
from jax.experimental import pallas as pl
from jax.experimental.pallas import tpu as pltpu
from jax.sharding import PartitionSpec as P

HEAD_DIM = 64
BF = jnp.bfloat16
F32 = jnp.float32
epsilon = 1e-06
VMEM_LIMIT = 58 * 1024 * 1024

ITEM = 256
SCALE = 0.2
TEXT_AT = 208


def cdiv(a, b):
    return -(-a // b)


def dot_nn(a, b):
    return lax.dot_general(a, b, (((1,), (0,)), ((), ())), preferred_element_type=F32)


def dot_nt(a, b):
    return lax.dot_general(a, b, (((1,), (1,)), ((), ())), preferred_element_type=F32)


def dot_tn(a, b):
    return lax.dot_general(a, b, (((0,), (0,)), ((), ())), preferred_element_type=F32)


def gelu_parts(upper):
    half = 0.5 * (1.0 + lax.erf(upper * math.sqrt(0.5)))
    slope = half + upper * (jnp.exp(-0.5 * upper * upper) * (1.0 / math.sqrt(2.0 * math.pi)))
    return upper * half, slope


def normalize(hidden):
    center = hidden - jnp.mean(hidden, axis=-1, keepdims=True)
    spread = jnp.mean(center * center, axis=-1, keepdims=True)
    scale = lax.rsqrt(spread + epsilon)
    return center * scale, scale


def start_rows(pieces, target, me, sems):
    block = target.shape[0] // 8
    copies = []
    for index, (slot, first, ref) in enumerate(pieces):
        row = pl.multiple_of((me ^ slot) * block + first, 16)
        copy = pltpu.make_async_copy(ref, target.at[pl.ds(row, ref.shape[0])], sems.at[index])
        copy.start()
        copies.append(copy)
    return copies


def mixed_in(tok, mask, vec, rows):
    keep = mask[rows, :]
    return keep * vec[0:1, :] + (1.0 - keep) * tok[rows, :].astype(F32)


def gate_kernel(count, *refs):
    del count, refs


def gate(arrays, after):
    count = len(arrays)
    return pl.pallas_call(
        functools.partial(gate_kernel, count),
        out_shape=[jax.ShapeDtypeStruct(a.shape, a.dtype) for a in arrays],
        in_specs=[pl.BlockSpec(memory_space=pl.ANY)] * (count + len(after)),
        out_specs=[pl.BlockSpec(memory_space=pl.ANY)] * count,
        input_output_aliases={i: i for i in range(count)},
        cost_estimate=pl.CostEstimate(flops=1000, bytes_accessed=1000, transcendentals=0),
    )(*arrays, *after)


def tick(token, after):
    return gate([token], after)[0]


def prep_kernel(text_rows, info, tokens, out_grad, w_out, down, up, text_up, *outs):
    tok, grad, grad_v, grad_t, sums, out_copy, down_copy, up_mine, up_other, strip0, te1, te2, te3, token = outs
    token[...] = jnp.zeros(token.shape, F32)
    items, row_count, width = tokens.shape
    patches = row_count - text_rows
    tail = ITEM - TEXT_AT - text_rows
    zeros = lambda n: jnp.zeros((n, width), F32)
    totals = [zeros(1), zeros(1)]
    texts = []
    for i in range(items):
        for source, target in ((tokens, tok), (out_grad, grad)):
            whole = source[i].astype(F32)
            patch, text = whole[:patches], whole[patches:]
            full = jnp.concatenate([patch, zeros(TEXT_AT - patches), text, zeros(tail)], axis=0)
            target[pl.ds(i * ITEM, ITEM), :] = full.astype(BF)
            if target is grad:
                grad_v[pl.ds(i * TEXT_AT, TEXT_AT), :] = full[:TEXT_AT].astype(BF)
                texts.append(text)
                totals[0] = totals[0] + jnp.sum(patch, axis=0, keepdims=True)
                totals[1] = totals[1] + jnp.sum(text, axis=0, keepdims=True)
    slots = jnp.concatenate(texts, axis=0).astype(BF)
    grad_t[...] = slots
    sums[0:1, :] = totals[0]
    sums[1:2, :] = totals[1]
    out_copy[...] = w_out[...]
    down_copy[...] = down[...]
    chip = info[0] // 2
    side = chip % 2
    block = up.shape[0]
    pair = 2 * down.shape[0]
    strip = lambda ref, c: ref[:, pl.ds(pl.multiple_of(c * pair, 128), pair)]
    for k in range(2):
        up_mine[:, k * pair : (k + 1) * pair] = strip(up, side + 2 * k)
        up_other[:, k * pair : (k + 1) * pair] = strip(up, 1 - side + 2 * k)
    strip0[...] = strip(text_up, chip)
    for k, target in ((1, te1), (2, te2), (3, te3)):
        target[pl.ds(0, block), :] = strip(text_up, chip ^ k)
        target[pl.ds(block, slots.shape[0]), :] = slots


def norm_kernel(info, tok, mask, even, odd, *refs):
    n1, vec, up_bias, shards = refs[-4:]
    me = info[0]
    total, width = tok.shape
    block = width // 8
    for slot in range(8):
        shards[me ^ slot] = (even, odd)[slot % 2][slot // 2]
    wide = jnp.concatenate([shards[b] for b in range(8)], axis=1)
    lane = lax.broadcasted_iota(jnp.int32, (1024, width), 0)
    to = lax.broadcasted_iota(jnp.int32, (1024, width), 1)
    spread = ((lane // 128) * block + lane % 128 == to) & (lane % 128 < block)
    vec[...] = dot_nn(wide, jnp.where(spread, 1.0, 0.0).astype(BF))
    hid = up_bias.shape[1] // 4
    for q in range(4):
        b = (q // 2) * 4 + q % 2 + ((me // 2) % 2) * 2
        for r in range(hid // 128):
            at = q * hid + r * 128
            up_bias[0:1, at : at + 128] = shards[b, 10 + r : 11 + r, :].astype(F32)

    @pl.loop(0, total // 64)
    def _(step):
        rows = pl.ds(pl.multiple_of(step * 64, 64), 64)
        normal, _unused = normalize(mixed_in(tok, mask, vec, rows))
        n1[rows, :] = (normal * vec[1:2, :] + vec[2:3, :]).astype(BF)


def qkv_kernel(slots, info, n1, vec, *refs):
    count = len(slots)
    pieces = refs[:count]
    qkv, weight, bias, sems = refs[-4:]
    width = n1.shape[1]
    copies = start_rows([(s, f, r) for (s, f), r in zip(slots, pieces)], weight, info[0], sems)
    bias[0:1, 0:width] = vec[3:4, :]
    bias[0:1, width : 2 * width] = jnp.zeros((1, width), F32)
    bias[0:1, 2 * width : 3 * width] = vec[4:5, :]
    for copy in copies:
        copy.wait()

    @pl.loop(0, 3 * width // 256)
    def _(step):
        cols = pl.ds(pl.multiple_of(step * 256, 256), 256)
        factor = jnp.where(step < width // 256, 0.125, 1.0).astype(F32)
        out = dot_nn(n1[...], weight[:, cols])
        qkv[:, cols] = ((out + bias[0:1, cols]) * factor).astype(BF)


def attn_kernel(info, qkv, *refs):
    probs, ctx = refs[-2:]
    total, width = ctx.shape
    items = total // ITEM
    pairs = width // 128
    patches = info[3]

    @pl.loop(0, items * pairs)
    def _(step):
        item, pair = step // pairs, step % pairs
        rows = pl.ds(pl.multiple_of(item * ITEM, ITEM), ITEM)
        lane = lambda part: pl.ds(pl.multiple_of(part * width + pair * 128, 128), 128)
        q2, k2, v2 = qkv[rows, lane(0)], qkv[rows, lane(1)], qkv[rows, lane(2)]
        low = lax.broadcasted_iota(jnp.int32, (ITEM, 128), 1) < HEAD_DIM
        zero = jnp.zeros_like(q2)
        both = jnp.concatenate([jnp.where(low, q2, zero), jnp.where(low, zero, q2)], axis=0)
        scores = dot_nt(both, k2)
        col = lax.broadcasted_iota(jnp.int32, (1, ITEM), 1)
        valid = (col < patches) | ((col >= TEXT_AT) & (col < TEXT_AT + info[1 + item]))
        scores = jnp.where(valid, scores, -1000000000.0)
        expo = jnp.exp(scores - jnp.max(scores, axis=-1, keepdims=True))
        prob = (expo * (1.0 / jnp.sum(expo, axis=-1, keepdims=True))).astype(BF)
        probs[step] = prob
        wide = jnp.concatenate([prob[:ITEM], prob[ITEM:]], axis=1)
        values = jnp.concatenate([jnp.where(low, v2, zero), jnp.where(low, zero, v2)], axis=0)
        ctx[rows, pl.ds(pl.multiple_of(pair * 128, 128), 128)] = dot_nn(wide, values).astype(BF)


def out_kernel(text_rows, info, tok, mask, vec, ctx, out_w, *refs):
    h1, n2t, *n2v = refs[-2 - tok.shape[0] // ITEM :]
    items = tok.shape[0] // ITEM
    texts = []
    for i in range(items):
        for at, size in ((0, TEXT_AT), (TEXT_AT, ITEM - TEXT_AT)):
            rows = pl.ds(i * ITEM + at, size)
            attended = dot_nn(ctx[rows, :], out_w[...]) + vec[5:6, :]
            hidden = mixed_in(tok, mask, vec, rows) + attended
            h1[rows, :] = hidden
            normal, _unused = normalize(hidden)
            second = normal * vec[6:7, :] + vec[7:8, :]
            if at == 0:
                n2v[i][...] = second.astype(BF)
            else:
                texts.append(second[:text_rows])
    n2t[...] = jnp.concatenate(texts, axis=0).astype(BF)


def pack_kernel(info, strip0, te1, te2, te3, grad_t, pack):
    block, hid = strip0.shape[0], strip0.shape[1] // 2
    rows = grad_t.shape[0]
    other = pl.ds(pl.multiple_of((1 - info[0] % 2) * hid, 128), hid)
    for k, ref in enumerate((strip0, te1, te2, te3)):
        at = (k // 2) * block
        pack[at : at + block, (k % 2) * hid : (k % 2 + 1) * hid] = ref[pl.ds(0, block), other]
        there = pl.ds(2 * block + k * rows, rows)
        pack[there, :] = grad_t[...] if k == 0 else ref[pl.ds(block, rows), :]


def up_rows(me, pieces, target, sems):
    block = target.shape[0] // 8
    copies = []
    for index, (base, ref) in enumerate(pieces):
        for k in range(2):
            row = pl.multiple_of((me ^ (base + 2 * k)) * block, 16)
            sem = sems.at[2 * index + k]
            copies.append(pltpu.make_async_copy(ref.at[k], target.at[pl.ds(row, block)], sem))
    for copy in copies:
        copy.start()
    return copies


def place_of(me):
    return (me // 4) * 2 + me % 2


def vision_kernel(pair, items, info, grad, up_bias, *refs):
    parts, refs = refs[:items], refs[items:]
    ups, downs = refs[:4], refs[4:6]
    branch, gn2, act, low, up_w, down_w, rows_in, sems = refs[-8:]
    me = info[0]
    block = downs[0].shape[1]
    copies = up_rows(me, list(zip((0, 4, 1, 5), ups)), up_w, sems)
    place = place_of(me)
    for j in range(4):
        row = pl.multiple_of((place ^ j) * block, 16)
        copy = pltpu.make_async_copy(downs[j % 2].at[j // 2], down_w.at[pl.ds(row, block)], sems.at[8 + j])
        copy.start()
        copies.append(copy)
    for copy in copies:
        copy.wait()
    mine = grad.at[(me // 2) % 2 ^ 1] if pair else grad
    for i, part in enumerate(parts):
        rows_in[pl.ds(i * TEXT_AT, TEXT_AT), :] = part[...]
    chunk = 512
    for step in range(down_w.shape[0] // chunk):
        cols = slice(step * chunk, (step + 1) * chunk)
        upper = dot_nn(rows_in[...], up_w[:, cols]) + up_bias[0:1, cols]
        active, slope = gelu_parts(upper)
        active = active.astype(BF)
        act[:, cols] = active
        back = (dot_nt(mine[...], down_w[cols, :]) * slope).astype(BF)
        low[:, cols] = back
        if step == 0:
            sum_branch = dot_nn(active, down_w[cols, :])
            sum_gn2 = dot_nt(back, up_w[:, cols])
        else:
            sum_branch = sum_branch + dot_nn(active, down_w[cols, :])
            sum_gn2 = sum_gn2 + dot_nt(back, up_w[:, cols])
    branch[...] = sum_branch.astype(branch.dtype)
    gn2[...] = sum_gn2.astype(gn2.dtype)


def vision_grad_kernel(items, info, *refs):
    ins = refs[:items], refs[items : 2 * items]
    grads, refs = refs[2 * items], refs[2 * items + 1 :]
    acts, lows = refs[:2], refs[2:4]
    up_keep, up_send, down_keep, down_send, bias_sums = refs[-11:-6]
    left_t, act_t, right, low, turn0, turn1 = refs[-6:]
    me = info[0]
    rows, width = items * ins[0][0].shape[0], ins[0][0].shape[1]
    block = width // 8
    half = down_keep.shape[1]
    place, core = place_of(me), me % 2
    for k in range(2):
        at = pl.ds(k * rows, rows)
        right[at, :] = grads[(me // 2) % 2 ^ k]
        low[at, :] = lows[k][...]
        turned = jnp.concatenate([ref[...] for ref in ins[k]], axis=0).T
        turn = (turn0, turn1)[k]
        for b in range(8):
            spot = pl.multiple_of((me ^ b) * block, 16)
            turn[pl.ds(spot, block), :] = turned[b * block : (b + 1) * block]
        left_t[:, at] = turn[...]
        act_t[:, at] = acts[k][...].T
    chunk = 512
    for step in range(4 * half // chunk):
        cols = slice(step * chunk, (step + 1) * chunk)
        grad_up = dot_nn(left_t[...], low[:, cols])
        bias_sums[0:1, cols] = jnp.sum(low[:, cols].astype(F32), axis=0, keepdims=True)
        grad_up = grad_up.astype(BF)
        for b in range(4):
            up_keep[b, :, cols] = grad_up[2 * b * block : (2 * b + 1) * block]
            up_send[b, :, cols] = grad_up[(2 * b + 1) * block : (2 * b + 2) * block]
    for q in range(4):
        grad_down = dot_nn(act_t[q * half : (q + 1) * half, :], right[...]).astype(BF)
        side = (q // 2) ^ (place // 2)

        @pl.when(core == q % 2)
        def _():
            down_keep[side] = grad_down

        @pl.when(core != q % 2)
        def _():
            down_send[side] = grad_down


def text_kernel(info, down, up_bias, strip0, te1, te2, te3, far, even, odd, *refs):
    grad0, refs = refs[0], refs[1:]
    branch_keep, branch_send, gn2_keep, gn2_send, up_keep, up_send, grad_down, bias_sums = refs[-12:-4]
    up_w, left, right, left_t = refs[-4:]
    me = info[0]
    width = down.shape[1]
    hid = down.shape[0]
    block = width // 8
    rows = even.shape[1]
    mine = pl.ds(pl.multiple_of((me % 2) * hid, 128), hid)
    spot = lambda slot: pl.ds(pl.multiple_of((me ^ slot) * block, 16), block)
    up_w[spot(0), :] = strip0[:, mine]
    for s, te in ((2, te1), (4, te2), (6, te3)):
        up_w[spot(s), :] = te[pl.ds(0, block), mine]
        right[pl.ds(s * rows, rows), :] = te[pl.ds(block, rows), :]
    up_w[spot(1), :] = far[pl.ds(0, block), pl.ds(0, hid)]
    up_w[spot(3), :] = far[pl.ds(0, block), pl.ds(hid, hid)]
    up_w[spot(5), :] = far[pl.ds(block, block), pl.ds(0, hid)]
    up_w[spot(7), :] = far[pl.ds(block, block), pl.ds(hid, hid)]
    right[pl.ds(0, rows), :] = grad0[...]
    for k in range(4):
        right[pl.ds((2 * k + 1) * rows, rows), :] = far[pl.ds(2 * block + k * rows, rows), :]
    for slot in range(8):
        left[pl.ds(slot * rows, rows), :] = (even, odd)[slot % 2][slot // 2]
    turned = left[...].T
    for b in range(8):
        left_t[spot(b), :] = turned[b * block : (b + 1) * block]
    upper = dot_nn(left[...], up_w[...]) + up_bias[...]
    active, slope = gelu_parts(upper)
    act = active.astype(BF)
    low = (dot_nt(right[...], down[...]) * slope).astype(BF)
    bias_sums[...] = jnp.sum(low.astype(F32), axis=0, keepdims=True)
    gn2 = dot_nt(low, up_w[...]).astype(BF)
    branch = dot_nn(act, down[...]).astype(BF)
    for s in range(4):
        gn2_keep[s] = gn2[2 * s * rows : (2 * s + 1) * rows]
        gn2_send[s] = gn2[(2 * s + 1) * rows : (2 * s + 2) * rows]
        branch_keep[s] = branch[2 * s * rows : (2 * s + 1) * rows]
        branch_send[s] = branch[(2 * s + 1) * rows : (2 * s + 2) * rows]
    grad_down[...] = dot_tn(act, right[...]).astype(BF)
    grad_up = dot_nn(left_t[...], low).astype(BF)
    for b in range(4):
        up_keep[b] = grad_up[2 * b * block : (2 * b + 1) * block]
        up_send[b] = grad_up[(2 * b + 1) * block : (2 * b + 2) * block]


def attn_bwd_kernel(text_rows, info, gn2v, gn2x, t0, t1, t2, t3, grad, h1, vec, qkv, probs, weight, *refs):
    gh1, low, stacked, sums, gn2, gctx = refs[-6:]
    total, width = h1.shape
    items = total // ITEM
    text = (
        t0[0].astype(F32) + t1[...].astype(F32) + t2[...].astype(F32) + t3[...].astype(F32)
    )
    for i in range(items):
        part = pl.ds(i * TEXT_AT, TEXT_AT)
        gn2[pl.ds(i * ITEM, TEXT_AT), :] = gn2v[part, :] + gn2x[part, :].astype(F32)
        gn2[pl.ds(i * ITEM + TEXT_AT, text_rows), :] = text[i * text_rows : (i + 1) * text_rows]
        pad = ITEM - TEXT_AT - text_rows
        gn2[pl.ds(i * ITEM + TEXT_AT + text_rows, pad), :] = jnp.zeros((pad, width), F32)
    sums[...] = jnp.zeros_like(sums)

    @pl.loop(0, total // 64)
    def _(step):
        rows = pl.ds(pl.multiple_of(step * 64, 64), 64)
        normal, scale = normalize(h1[rows, :])
        above = gn2[rows, :]
        inner = above * vec[6:7, :]
        back = scale * (
            inner
            - jnp.mean(inner, axis=-1, keepdims=True)
            - normal * jnp.mean(inner * normal, axis=-1, keepdims=True)
        )
        out = grad[rows, :].astype(F32)
        hidden = out + back
        gh1[rows, :] = hidden
        low[rows, :] = hidden.astype(BF)
        sums[0:1, :] += jnp.sum(above * normal, axis=0, keepdims=True)
        sums[1:2, :] += jnp.sum(above, axis=0, keepdims=True)
        sums[2:3, :] += jnp.sum(hidden.astype(BF).astype(F32), axis=0, keepdims=True)

    gctx[...] = dot_nt(low[...], weight[...]).astype(BF)
    pairs = width // 128

    @pl.loop(0, items * pairs)
    def _(step):
        item, pair = step // pairs, step % pairs
        rows = pl.ds(pl.multiple_of(item * ITEM, ITEM), ITEM)
        lane = lambda part: pl.ds(pl.multiple_of(part * width + pair * 128, 128), 128)
        q2, k2, v2 = qkv[rows, lane(0)], qkv[rows, lane(1)], qkv[rows, lane(2)]
        g2 = gctx[rows, pl.ds(pl.multiple_of(pair * 128, 128), 128)]
        lower = lax.broadcasted_iota(jnp.int32, (ITEM, 128), 1) < HEAD_DIM
        zero = jnp.zeros_like(q2)
        split = lambda a: jnp.concatenate([jnp.where(lower, a, zero), jnp.where(lower, zero, a)], axis=0)
        both_g = split(g2)
        prob_b = probs[step]
        prob = prob_b.astype(F32)
        gprob = dot_nt(both_g, v2)
        weighted = prob * gprob
        gscore = (weighted - prob * jnp.sum(weighted, axis=-1, keepdims=True)).astype(BF)
        stacked[rows, lane(2)] = dot_tn(prob_b, both_g).astype(BF)
        stacked[rows, lane(1)] = dot_tn(gscore, split(q2)).astype(BF)
        wide = jnp.concatenate([gscore[:ITEM], gscore[ITEM:]], axis=1)
        gquery = dot_nn(wide, split(k2)).astype(BF).astype(F32) * 0.125
        stacked[rows, lane(0)] = gquery.astype(BF)

    for part in (0, 2):
        cols = stacked[:, part * width : (part + 1) * width].astype(F32)
        sums[3 + part // 2 : 4 + part // 2, :] = jnp.sum(cols, axis=0, keepdims=True)


def attn_grad_kernel(last, info, left, *refs):
    me = info[0]
    width = left.shape[1]
    block = width // 8
    keep, send, left_t, other_t, right, sem = refs[-6:]
    others, stacked = (refs[:2], refs[2]) if last else ((), refs[0])
    first = 2 * width if last else 0
    copy = pltpu.make_async_copy(stacked.at[:, pl.ds(first, right.shape[1])], right, sem.at[0])
    copy.start()
    for source, target in ((left, left_t), (others[0], other_t)) if last else ((left, left_t),):
        turned = source[...].T
        for b in range(8):
            place = pl.multiple_of((me ^ b) * block, 16)
            target[pl.ds(place, block), :] = turned[b * block : (b + 1) * block]
    for part in (1, 0) if last else (0, 1):
        cols = slice(part * width, (part + 1) * width)
        if last and part == 1:
            value = dot_nn(other_t[...], others[1][...]).astype(BF)
        else:
            if part == 0:
                copy.wait()
            value = dot_nn(left_t[...], right[:, cols]).astype(BF)
        for b in range(4):
            keep[b, :, cols] = value[2 * b * block : (2 * b + 1) * block]
            send[b, :, cols] = value[(2 * b + 1) * block : (2 * b + 2) * block]


def last_kernel(slots, info, stacked, gh1, tok, mask, vec, *refs):
    count = len(slots)
    pieces = refs[:count]
    gtok, sums, weight, sems = refs[-4:]
    copies = start_rows([(s, f, r) for (s, f), r in zip(slots, pieces)], weight, info[0], sems)
    sums[...] = jnp.zeros_like(sums)
    for copy in copies:
        copy.wait()

    @pl.loop(0, tok.shape[0] // 128)
    def _(step):
        rows = pl.ds(pl.multiple_of(step * 128, 128), 128)
        above = dot_nt(stacked[rows, :], weight[...])
        normal, scale = normalize(mixed_in(tok, mask, vec, rows))
        inner = above * vec[1:2, :]
        back = scale * (
            inner
            - jnp.mean(inner, axis=-1, keepdims=True)
            - normal * jnp.mean(inner * normal, axis=-1, keepdims=True)
        )
        hidden = gh1[rows, :] + back
        keep = mask[rows, :]
        gtok[rows, :] = hidden * (1.0 - keep)
        sums[0:1, :] += jnp.sum(hidden * keep, axis=0, keepdims=True)
        sums[1:2, :] += jnp.sum(above * normal, axis=0, keepdims=True)
        sums[2:3, :] += jnp.sum(above, axis=0, keepdims=True)


def call(kernel, outs, scratch, args, pieces=(), us=1):
    in_specs = [pl.BlockSpec(memory_space=pltpu.SMEM)]
    in_specs += [pl.BlockSpec(memory_space=pltpu.VMEM)] * (len(args) - 1)
    in_specs += [pl.BlockSpec(memory_space=pl.ANY)] * len(pieces)
    return pl.pallas_call(
        kernel,
        out_shape=[jax.ShapeDtypeStruct(s, d) for s, d in outs],
        in_specs=in_specs,
        out_specs=[pl.BlockSpec(memory_space=pltpu.VMEM)] * len(outs),
        scratch_shapes=scratch,
        compiler_params=pltpu.CompilerParams(vmem_limit_bytes=VMEM_LIMIT),
        cost_estimate=pl.CostEstimate(flops=int(us * SCALE * 1.1e9), bytes_accessed=int(us * SCALE * 1e6), transcendentals=0),
    )(*args, *pieces)


def swap(array, mask):
    return lax.ppermute(array, "fsdp", [(i, i ^ mask) for i in range(8)])


def along_rep(array, pairs):
    return lax.ppermute(array, "rep", pairs)


def add(*terms):
    out = terms[0].astype(F32)
    for term in terms[1:]:
        out = out + term.astype(F32)
    return out.astype(BF)


def planned(
    tokens,
    out_grad,
    masked,
    lengths,
    mask_vec,
    norm1_gain,
    norm1_shift,
    w_qkv,
    query_bias,
    value_bias,
    w_out,
    out_bias,
    norm2_gain,
    norm2_shift,
    vision_up,
    vision_up_bias,
    vision_down,
    vision_down_bias,
    text_up,
    text_up_bias,
    text_down,
    text_down_bias,
):
    items, row_count, width = tokens.shape
    text_rows = masked.shape[1]
    patches = row_count - text_rows
    block = width // 8
    half = block // 2
    hid = vision_down.shape[0]
    pair = 2 * hid
    hidden = 8 * hid
    total = items * ITEM
    vision_rows = items * TEXT_AT
    slot_rows = items * text_rows
    te_rows = block + slot_rows
    me = lax.axis_index("fsdp").astype(jnp.int32)
    rep = lax.axis_index("rep").astype(jnp.int32)
    core, chip, side = me % 2, me // 2, (me // 2) % 2
    sem = lambda n: pltpu.SemaphoreType.DMA((n,))
    quad = lambda r, c: ((4, r, c), BF)

    names = (
        mask_vec,
        norm1_gain,
        norm1_shift,
        query_bias,
        value_bias,
        out_bias,
        norm2_gain,
        norm2_shift,
        vision_down_bias,
        text_down_bias,
    )
    own_vec = jnp.pad(jnp.stack(names), ((0, 0), (0, 128 - block)))
    own_vec = jnp.concatenate([own_vec, vision_up_bias.reshape(-1, 128)], axis=0)
    own_vec = jnp.pad(own_vec, ((0, 16 - own_vec.shape[0]), (0, 0)))[None]
    vx, vy, vxy = swap(own_vec, 2), swap(own_vec, 4), swap(own_vec, 6)
    qx, qy = swap(w_qkv, 2), swap(w_qkv, 4)
    mask = jnp.concatenate(
        [
            jnp.zeros((items, TEXT_AT), F32),
            masked.astype(F32),
            jnp.zeros((items, ITEM - TEXT_AT - text_rows), F32),
        ],
        axis=1,
    ).reshape(total, 1)
    info = jnp.concatenate([me[None], lengths, jnp.full((1,), patches, jnp.int32)])
    tok, grad, grad_v, grad_t, grad_sums, own_out, own_down, up_mine, up_other, strip0, te1, te2, te3, t = call(
        functools.partial(prep_kernel, text_rows),
        [
            ((total, width), BF),
            ((total, width), BF),
            ((vision_rows, width), BF),
            ((slot_rows, width), BF),
            ((2, width), F32),
            ((block, width), BF),
            ((hid, width), BF),
            ((block, 2 * pair), BF),
            ((block, 2 * pair), BF),
            ((block, pair), BF),
            ((te_rows, width), BF),
            ((te_rows, width), BF),
            ((te_rows, width), BF),
            ((8, 128), F32),
        ],
        [],
        [info, tokens, out_grad, w_out, vision_down, vision_up, text_up],
        us=5,
    )
    vec_four = gate([jnp.concatenate([own_vec, vx, vy, vxy], axis=0)], [t])[0]
    vec_arrays = [vec_four, swap(vec_four, 1)]
    part1, part2 = gate([qx[:half], qy[half:]], [tok, vec_arrays[1]])

    far1, far2 = swap(part1, 4), swap(part2, 2)
    near = [swap(a, 1) for a in (w_qkv, qx, qy)]
    n1, vec, up_bias = call(
        norm_kernel,
        [((total, width), BF), ((16, width), F32), ((1, 4 * hid), F32)],
        [pltpu.VMEM((8, 16, 128), BF)],
        [info, tok, mask, *vec_arrays],
        [part1],
        us=5,
    )
    far1, far2, up_other, own_down, own_out = gate([far1, far2, up_other, own_down, own_out], [n1, *near])
    out_all = lax.all_gather(own_out, "fsdp", tiled=True)
    pairs = [[0, 2], [1, 3], [4, 6], [5, 7]]
    grad_pair = lax.all_gather(grad_v, "fsdp", axis_index_groups=pairs)
    attn = [(0, 0, w_qkv), (2, 0, qx), (4, 0, qy), (6, 0, far1), (6, half, far2)]
    attn += [(1, 0, near[0]), (3, 0, near[1]), (5, 0, near[2]), (7, 0, swap(far1, 1)), (7, half, swap(far2, 1))]
    attn_slots = tuple((p[0], p[1]) for p in attn)
    attn_arrays = [p[2] for p in attn]

    up_x, down_y = swap(up_other, 2), swap(own_down, 4)
    (qkv,) = call(
        functools.partial(qkv_kernel, attn_slots),
        [((total, 3 * width), BF)],
        [pltpu.VMEM((width, 3 * width), BF), pltpu.VMEM((1, 3 * width), F32), sem(len(attn))],
        [info, n1, vec],
        attn_arrays,
        us=8,
    )
    t = tick(t, [qkv, up_x])

    up_x, te1, te2, te3 = gate([up_x, te1, te2, te3], [t])
    up_two = jnp.stack([up_mine, up_x])
    up_y, up_c = swap(up_two, 4), swap(up_two, 1)
    te1, te3 = swap(te1, 2), swap(te3, 6)
    probs, ctx = call(
        attn_kernel,
        [((items * width // 128, 2 * ITEM, ITEM), BF), ((total, width), BF)],
        [],
        [info, qkv],
        [t],
        us=10,
    )
    t = tick(t, [ctx, up_y, up_c, te1, te3, down_y])

    up_y, te1, te2, te3, down_y = gate([up_y, te1, te2, te3, down_y], [t])
    te2 = swap(te2, 4)
    down_two = jnp.stack([own_down, down_y])
    up_yc, down_c = swap(up_y, 1), swap(down_two, 1)
    h1, n2t, *n2v = call(
        functools.partial(out_kernel, text_rows),
        [((total, width), F32), ((slot_rows, width), BF)] + [((TEXT_AT, width), BF)] * items,
        [],
        [info, tok, mask, vec, ctx, out_all],
        [t],
        us=5,
    )
    t = tick(t, [n2t, te2, up_yc, down_c, grad_pair])

    te1, te2, te3, n2t, *n2v = gate([te1, te2, te3, n2t, *n2v], [t])
    (pack,) = call(
        pack_kernel,
        [((2 * block + 4 * slot_rows, width), BF)],
        [],
        [info, strip0, te1, te2, te3, grad_t],
    )
    text_in = [swap(n2t, 2), swap(n2t, 4), swap(n2t, 6)]
    n2x = [swap(n2v[0], 2)]
    far = swap(pack, 1)
    weights = [up_two, up_y, up_c, up_yc, down_two, down_c]

    def vision(rows_in, grads, kind, after):
        return call(
            functools.partial(vision_kernel, kind == BF, items),
            [
                ((vision_rows, width), kind),
                ((vision_rows, width), kind),
                ((vision_rows, 4 * hid), BF),
                ((vision_rows, 4 * hid), BF),
            ],
            [
                pltpu.VMEM((width, 4 * hid), BF),
                pltpu.VMEM((4 * hid, width), BF),
                pltpu.VMEM((vision_rows, width), BF),
                sem(12),
            ],
            [info, grads, up_bias, *rows_in],
            [*weights, *after],
            us=9,
        )

    branch_own, gn2_own, act_own, low_own = vision(n2v, grad_v, F32, [pack])
    t = tick(t, [gn2_own, *text_in, n2x[0], far])

    far, *text_in = gate([far, *text_in], [t])
    text_four = jnp.stack([n2t, *text_in])
    text_odd = swap(text_four, 1)
    n2x += [swap(a, 2) for a in gate(n2v[1:], [t])]
    branch_keep, branch_send, gn2_keep, gn2_send, tu_keep, tu_send, td, text_bias_sum = call(
        text_kernel,
        [
            quad(slot_rows, width),
            quad(slot_rows, width),
            quad(slot_rows, width),
            quad(slot_rows, width),
            quad(block, hid),
            quad(block, hid),
            ((hid, width), BF),
            ((1, hid), F32),
        ],
        [
            pltpu.VMEM((width, hid), BF),
            pltpu.VMEM((8 * slot_rows, width), BF),
            pltpu.VMEM((8 * slot_rows, width), BF),
            pltpu.VMEM((width, 8 * slot_rows), BF),
        ],
        [
            info,
            text_down,
            text_up_bias.astype(F32).reshape(1, hid),
            strip0,
            te1,
            te2,
            te3,
            far,
            text_four,
            text_odd,
            grad_t,
        ],
        us=6,
    )
    t = tick(t, [gn2_keep, *n2x])
    tu_keep, tu_send, td = lax.psum((tu_keep, tu_send, td), "rep")

    gn2_send, *n2x = gate([gn2_send, *n2x], [t])
    gn2_sum = add(gn2_keep, swap(gn2_send, 1))
    gn2_text = [gn2_sum] + [swap(gn2_sum[s], 2 * s) for s in (1, 2, 3)]
    branch_x, gn2_x, act_x, low_x = vision(n2x, grad_pair, BF, [gn2_sum])
    t = tick(t, [gn2_x, *gn2_text[1:]])

    (gn2_x,) = gate([gn2_x], [t])
    gn2_back = swap(gn2_x, 2)
    vu_keep, vu_send, vd_keep, vd_send, vu_bias_sum = call(
        functools.partial(vision_grad_kernel, items),
        [
            quad(block, 4 * hid),
            quad(block, 4 * hid),
            ((2, hid, width), BF),
            ((2, hid, width), BF),
            ((1, 4 * hid), F32),
        ],
        [
            pltpu.VMEM((width, 2 * vision_rows), BF),
            pltpu.VMEM((4 * hid, 2 * vision_rows), BF),
            pltpu.VMEM((2 * vision_rows, width), BF),
            pltpu.VMEM((2 * vision_rows, 4 * hid), BF),
            pltpu.VMEM((width, vision_rows), BF),
            pltpu.VMEM((width, vision_rows), BF),
        ],
        [info, *n2v, *n2x, grad_pair, act_own, act_x, low_own, low_x],
        [t],
        us=12,
    )
    t = tick(t, [vu_bias_sum, gn2_back])

    vu_send, vd_send, branch_x, branch_send, gn2_back = gate([vu_send, vd_send, branch_x, branch_send, gn2_back], [t])
    vu_got, vd_got = swap(vu_send, 1), swap(vd_send, 1)
    vd_near, vd_far = add(vd_keep[0], vd_got[0]), add(vd_keep[1], vd_got[1])
    vu_far = [add(vu_keep[k], vu_got[k]) for k in (2, 3)]
    vd_y, vu_y1 = swap(vd_far, 4), swap(vu_far[1], 4)
    branch_back = swap(branch_x, 2)
    branch_got = swap(branch_send, 1)
    gh1, low_attn, stacked, sums_two = call(
        functools.partial(attn_bwd_kernel, text_rows),
        [((total, width), F32), ((total, width), BF), ((total, 3 * width), BF), ((8, width), F32)],
        [pltpu.VMEM((total, width), F32), pltpu.VMEM((total, width), BF)],
        [info, gn2_own, gn2_back, *gn2_text, grad, h1, vec, qkv, probs, out_all],
        [vd_far, *vu_far],
        us=18,
    )
    t = tick(t, [stacked, vd_y, vu_y1, branch_back, branch_got])

    vd_y, vu_y1, vu_far0, branch_got = gate([vd_y, vu_y1, vu_far[0], branch_got], [t])
    vd_sum = add(vd_near, vd_y)
    vu_x = swap(add(vu_keep[1], vu_got[1], vu_y1), 2)
    vu_y0 = swap(vu_far0, 4)

    def attn_grads(last, after):
        return call(
            functools.partial(attn_grad_kernel, last),
            [quad(block, 2 * width), quad(block, 2 * width)],
            [
                pltpu.VMEM((width, total), BF),
                pltpu.VMEM((width, total), BF),
                pltpu.VMEM((total, (1 if last else 2) * width), BF),
                sem(1),
            ],
            [info, n1, ctx, low_attn] if last else [info, n1],
            [stacked, *after],
            us=5,
        )

    a_keep, a_send = attn_grads(False, [t])
    t = tick(t, [a_keep, vu_x, vu_y0])
    a_send, vu_x, vu_y0 = gate([a_send, vu_x, vu_y0], [t])
    a_got = swap(a_send, 1)
    branch_sum = add(branch_keep, branch_got)
    vu_both = jnp.stack([add(vu_keep[0], vu_got[0], vu_y0), vu_x])
    vu, vd = lax.psum((vu_both, vd_sum), "rep", axis_index_groups=[[1, 0, 2, 3]])
    b_keep, b_send = attn_grads(True, [t])
    t = tick(t, [b_keep, a_got])
    a_got, b_send, branch_sum = gate([a_got, b_send, branch_sum], [t])
    b_got = swap(b_send, 1)

    def begin(keep, got, one):
        i = one // 2
        return add(jnp.stack([keep[i], keep[3]]), jnp.stack([got[i], got[3]]))

    a_first, b_first = begin(a_keep, a_got, 2), begin(b_keep, b_got, 4)
    a_there, b_there = swap(a_first, 2), swap(b_first, 4)
    branch_t = [branch_sum] + [swap(branch_sum[s], 2 * s) for s in (1, 2, 3)]
    gtok, sums_one = call(
        functools.partial(last_kernel, attn_slots),
        [((total, width), F32), ((8, width), F32)],
        [pltpu.VMEM((width, 3 * width), BF), sem(len(attn))],
        [info, stacked, gh1, tok, mask, vec],
        attn_arrays + [a_first, b_first, vu_both, vd_sum],
        us=12,
    )
    t = tick(t, [sums_one, a_there, b_there, *branch_t[1:]])

    a_there, b_there = gate([a_there, b_there], [t])
    a_next, b_next = add(a_keep[2], a_got[2], a_there[1]), add(b_keep[1], b_got[1], b_there[1])
    a_beyond, b_beyond = swap(a_next, 4), swap(b_next, 2)
    (sums_one,) = gate([sums_one], [tick(t, [a_next, b_next])])
    vu_sum = vu_bias_sum.reshape(2, 1, pair)
    vu_sum = jnp.where(
        side == 0,
        jnp.concatenate([vu_sum, jnp.zeros_like(vu_sum)], axis=1),
        jnp.concatenate([jnp.zeros_like(vu_sum), vu_sum], axis=1),
    )
    count, rows = len(names), hid // block
    vec_rows = count + 2 * rows
    vu_sum = vu_sum.reshape(8, rows, block).transpose(1, 0, 2).reshape(-1, width)
    flat = jnp.concatenate(
        [sums_one[0:3], sums_two[3:5], sums_two[2:3], sums_two[0:2], grad_sums, vu_sum], axis=0
    )
    for m in (1, 2, 4):
        flat = flat + swap(flat, m)
    own_sums = lax.dynamic_slice_in_dim(flat, me * block, block, axis=1)
    own_sums = jnp.concatenate([own_sums, text_bias_sum.reshape(-1, block)], axis=0)
    ga = add(a_keep[0], a_got[0], a_there[0], a_beyond)
    gb = add(b_keep[0], b_got[0], b_there[0], b_beyond)

    inner = (rep == 1) | (rep == 2)

    def rep_sum(array):
        part = add(array, along_rep(array, [(0, 1), (3, 2)]))
        whole = add(part, along_rep(part, [(1, 2), (2, 1)]))
        return jnp.where(inner, whole, along_rep(whole, [(1, 0), (2, 3)]))

    plane_sums = [ga, gb]
    own_sums = own_sums.reshape(-1)
    own_sums = jnp.pad(own_sums, (0, 8 * 2 * width - own_sums.shape[0])).reshape(8, 2 * width)
    ga, gb = rep_sum(jnp.concatenate([ga, own_sums.astype(BF)], axis=0)), rep_sum(gb)
    last_sums = [ga, gb]
    tu_keep, tu_send, td = gate([tu_keep, tu_send, td], plane_sums)
    tu_got = swap(tu_send, 1)
    tu_wide = jnp.where(
        core == 0,
        jnp.concatenate([tu_keep, tu_got], axis=-1),
        jnp.concatenate([tu_got, tu_keep], axis=-1),
    )
    tu_all = [tu_wide[0]] + [swap(tu_wide[s], 2 * s) for s in (1, 2, 3)]
    tu_x = [jnp.where(side == 0, tu_all[k], tu_all[k ^ 1]) for k in range(4)]
    tu_y = [jnp.where(me // 4 == 0, tu_x[k], tu_x[k ^ 2]) for k in range(4)]
    grad_text_up = jnp.concatenate(tu_y, axis=1).astype(F32)
    grad_text_down = td.astype(F32)

    ga = ga.astype(F32)
    mine = ga[block:].reshape(-1)[: vec_rows * block].reshape(vec_rows, block)
    ga = ga[:block]
    vec_grad = [mine[i] for i in range(count)]
    vu_bias_grad = mine[count : count + rows].reshape(-1)
    tu_bias_grad = mine[count + rows : count + 2 * rows].reshape(-1)

    vu, vd = gate([vu, vd], last_sums)
    gb = gb.astype(F32)
    grad_w_qkv = jnp.concatenate([ga, gb[:, :width]], axis=1)
    grad_w_out = gb[:, width:]
    vu_s = [jnp.where(side == 0, vu[k], vu[1 - k]) for k in range(2)]
    grad_vision_up = jnp.concatenate(
        [vu_s[0][:, :pair], vu_s[1][:, :pair], vu_s[0][:, pair:], vu_s[1][:, pair:]], axis=1
    ).astype(F32)
    grad_vision_down = vd.astype(F32)
    h1 = h1.reshape(items, ITEM, width)
    branch_v = (branch_own + branch_back.astype(F32)).reshape(items, TEXT_AT, width)[:, :patches]
    mixed_v = h1[:, :patches] + branch_v + vec[8][None, None]
    branch_t = branch_t[0][0].astype(F32) + sum(b.astype(F32) for b in branch_t[1:])
    branch_t = branch_t.reshape(items, text_rows, width)
    mixed_t = h1[:, TEXT_AT : TEXT_AT + text_rows] + branch_t + vec[9][None, None]
    mixed = jnp.concatenate([mixed_v.astype(BF), mixed_t.astype(BF)], axis=1)
    gtok = gtok.reshape(items, ITEM, width)
    grad_tokens = jnp.concatenate(
        [gtok[:, :patches], gtok[:, TEXT_AT : TEXT_AT + text_rows]], axis=1
    )
    return (
        mixed,
        grad_tokens,
        vec_grad[0],
        vec_grad[1],
        vec_grad[2],
        grad_w_qkv,
        vec_grad[3],
        vec_grad[4],
        grad_w_out,
        vec_grad[5],
        vec_grad[6],
        vec_grad[7],
        grad_vision_up,
        vu_bias_grad,
        grad_vision_down,
        vec_grad[8],
        grad_text_up,
        tu_bias_grad,
        grad_text_down,
        vec_grad[9],
    )


def layer_norm(hidden, gain, shift):
    center = hidden - jnp.mean(hidden, axis=-1, keepdims=True)
    spread = jnp.mean(center * center, axis=-1, keepdims=True)
    return center * lax.rsqrt(spread + epsilon) * gain + shift


def exact_gelu(values):
    return jax.nn.gelu(values, approximate=False)


def expert_forward(rows_in, up_matrix, up_shift, down_matrix, down_shift):
    upper = jnp.dot(rows_in, up_matrix, preferred_element_type=jnp.float32) + up_shift.astype(
        jnp.float32
    )
    active, gelu_pull = jax.vjp(exact_gelu, upper)
    active_b = active.astype(jnp.bfloat16)
    result = jnp.dot(active_b, down_matrix, preferred_element_type=jnp.float32) + down_shift.astype(
        jnp.float32
    )
    return (result, active_b, gelu_pull)


def expert_backward(rows_in, active_b, gelu_pull, up_matrix, down_matrix, grad_b):
    grad_down = jnp.einsum("rf,rd->fd", active_b, grad_b, preferred_element_type=jnp.float32)
    grad_down_shift = jnp.sum(grad_b.astype(jnp.float32), axis=0)
    grad_active = jnp.einsum("rd,fd->rf", grad_b, down_matrix, preferred_element_type=jnp.float32)
    (grad_upper,) = gelu_pull(grad_active)
    upper_b = grad_upper.astype(jnp.bfloat16)
    grad_up = jnp.einsum("rd,rf->df", rows_in, upper_b, preferred_element_type=jnp.float32)
    grad_up_shift = jnp.sum(upper_b.astype(jnp.float32), axis=0)
    grad_rows = jnp.einsum("rf,df->rd", upper_b, up_matrix, preferred_element_type=jnp.float32)
    return (grad_up, grad_up_shift, grad_down, grad_down_shift, grad_rows)


def general(
    tokens,
    out_grad,
    masked,
    lengths,
    mask_vec,
    norm1_gain,
    norm1_shift,
    w_qkv,
    query_bias,
    value_bias,
    w_out,
    out_bias,
    norm2_gain,
    norm2_shift,
    vision_up,
    vision_up_bias,
    vision_down,
    vision_down_bias,
    text_up,
    text_up_bias,
    text_down,
    text_down_bias,
):
    item_count, row_count, model_width = tokens.shape
    slot_count = masked.shape[1]
    patches = row_count - slot_count
    head_count = model_width // HEAD_DIM
    split_shape = (item_count, row_count, head_count, HEAD_DIM)

    def fetch_attention():
        return (
            lax.all_gather(mask_vec, "fsdp", axis=0, tiled=True),
            lax.all_gather(norm1_gain, "fsdp", axis=0, tiled=True),
            lax.all_gather(norm1_shift, "fsdp", axis=0, tiled=True),
            lax.all_gather(w_qkv, "fsdp", axis=0, tiled=True),
            lax.all_gather(query_bias, "fsdp", axis=0, tiled=True),
            lax.all_gather(value_bias, "fsdp", axis=0, tiled=True),
            lax.all_gather(w_out, "fsdp", axis=0, tiled=True),
            lax.all_gather(out_bias, "fsdp", axis=0, tiled=True),
        )

    def fetch_feedforward():
        return (
            lax.all_gather(norm2_gain, "fsdp", axis=0, tiled=True),
            lax.all_gather(norm2_shift, "fsdp", axis=0, tiled=True),
            lax.all_gather(vision_up, "fsdp", axis=0, tiled=True),
            lax.all_gather(vision_up_bias, "fsdp", axis=0, tiled=True),
            lax.all_gather(vision_down, "fsdp", axis=0, tiled=True),
            lax.all_gather(vision_down_bias, "fsdp", axis=0, tiled=True),
            lax.all_gather(text_up, "fsdp", axis=0, tiled=True),
            lax.all_gather(text_up_bias, "fsdp", axis=0, tiled=True),
            lax.all_gather(text_down, "fsdp", axis=0, tiled=True),
            lax.all_gather(text_down_bias, "fsdp", axis=0, tiled=True),
        )

    attn_full = fetch_attention()
    full_mask, gain_one, shift_one, qkv_matrix, query_shift, value_shift, out_matrix, out_shift = (
        attn_full
    )
    mask_rows = jnp.concatenate(
        [jnp.zeros((item_count, patches), jnp.float32), masked.astype(jnp.float32)], axis=1
    )[:, :, None]
    hidden0 = mask_rows * full_mask.astype(jnp.float32) + (1.0 - mask_rows) * tokens.astype(
        jnp.float32
    )
    normed1, first_pull = jax.vjp(
        layer_norm, hidden0, gain_one.astype(jnp.float32), shift_one.astype(jnp.float32)
    )
    first_in = normed1.astype(jnp.bfloat16).reshape(item_count * row_count, model_width)
    projected = jnp.dot(first_in, qkv_matrix, preferred_element_type=jnp.float32)
    query_b = (
        ((projected[:, :model_width] + query_shift.astype(jnp.float32)) * 0.125)
        .astype(jnp.bfloat16)
        .reshape(split_shape)
    )
    key_b = projected[:, model_width : 2 * model_width].astype(jnp.bfloat16).reshape(split_shape)
    value_b = (
        (projected[:, 2 * model_width :] + value_shift.astype(jnp.float32))
        .astype(jnp.bfloat16)
        .reshape(split_shape)
    )
    key_index = jnp.arange(row_count, dtype=jnp.int32)
    valid_keys = (key_index[None, :] < patches + lengths[:, None])[:, None, None, :]

    def scores_of():
        raw_scores = jnp.einsum(
            "iqhd,ikhd->ihqk", query_b, key_b, preferred_element_type=jnp.float32
        )
        return jnp.where(valid_keys, raw_scores, -1000000000.0)

    scores = scores_of()
    top_score = jnp.max(scores, axis=-1, keepdims=True)
    expo = jnp.exp(scores - top_score)
    totals = jnp.sum(expo, axis=-1, keepdims=True)
    probs = expo / totals
    log_total = top_score + jnp.log(totals)
    context = jnp.einsum(
        "ihqk,ikhd->iqhd", probs.astype(jnp.bfloat16), value_b, preferred_element_type=jnp.float32
    )
    context_b = context.reshape(item_count * row_count, model_width).astype(jnp.bfloat16)
    attended = jnp.dot(
        context_b, out_matrix, preferred_element_type=jnp.float32
    ) + out_shift.astype(jnp.float32)
    hidden1 = hidden0 + attended.reshape(item_count, row_count, model_width)
    ffn_full = fetch_feedforward()
    (
        gain_two,
        shift_two,
        vision_upm,
        vision_upb,
        vision_downm,
        vision_downb,
        text_upm,
        text_upb,
        text_downm,
        text_downb,
    ) = ffn_full
    normed2, second_pull = jax.vjp(
        layer_norm, hidden1, gain_two.astype(jnp.float32), shift_two.astype(jnp.float32)
    )
    second_in = normed2.astype(jnp.bfloat16)
    patch_in = second_in[:, :patches].reshape(-1, model_width)
    text_in = second_in[:, patches:].reshape(-1, model_width)
    vision_out, vision_act, vision_pull = expert_forward(
        patch_in, vision_upm, vision_upb, vision_downm, vision_downb
    )
    text_out, text_act, text_pull = expert_forward(
        text_in, text_upm, text_upb, text_downm, text_downb
    )
    mixed = hidden1 + jnp.concatenate(
        [
            vision_out.reshape(item_count, patches, model_width),
            text_out.reshape(item_count, slot_count, model_width),
        ],
        axis=1,
    )
    cotangent = out_grad.astype(jnp.float32)
    branch_b = cotangent.astype(jnp.bfloat16)
    ffn_back = fetch_feedforward()
    vision_grads = expert_backward(
        patch_in,
        vision_act,
        vision_pull,
        ffn_back[2],
        ffn_back[4],
        branch_b[:, :patches].reshape(-1, model_width),
    )
    text_grads = expert_backward(
        text_in,
        text_act,
        text_pull,
        ffn_back[6],
        ffn_back[8],
        branch_b[:, patches:].reshape(-1, model_width),
    )
    grad_normed2 = jnp.concatenate(
        [
            vision_grads[4].reshape(item_count, patches, model_width),
            text_grads[4].reshape(item_count, slot_count, model_width),
        ],
        axis=1,
    )
    grad_hidden1_norm, grad_gain_two, grad_shift_two = second_pull(grad_normed2)
    grad_hidden1 = cotangent + grad_hidden1_norm
    attn_back = fetch_attention()
    grad_attn_b = grad_hidden1.reshape(-1, model_width).astype(jnp.bfloat16)
    grad_out_matrix = jnp.einsum(
        "rd,re->de", context_b, grad_attn_b, preferred_element_type=jnp.float32
    )
    grad_out_shift = jnp.sum(grad_attn_b.astype(jnp.float32), axis=0)
    grad_context = jnp.einsum(
        "re,de->rd", grad_attn_b, attn_back[6], preferred_element_type=jnp.float32
    )
    grad_context_b = grad_context.astype(jnp.bfloat16).reshape(split_shape)
    again_probs = jnp.exp(scores_of() - log_total)
    grad_probs = jnp.einsum(
        "iqhd,ikhd->ihqk", grad_context_b, value_b, preferred_element_type=jnp.float32
    )
    grad_value = jnp.einsum(
        "ihqk,iqhd->ikhd",
        again_probs.astype(jnp.bfloat16),
        grad_context_b,
        preferred_element_type=jnp.float32,
    )
    row_inner = jnp.sum(again_probs * grad_probs, axis=-1, keepdims=True)
    grad_scores_b = (again_probs * (grad_probs - row_inner)).astype(jnp.bfloat16)
    grad_query = jnp.einsum(
        "ihqk,ikhd->iqhd", grad_scores_b, key_b, preferred_element_type=jnp.float32
    )
    grad_key = jnp.einsum(
        "ihqk,iqhd->ikhd", grad_scores_b, query_b, preferred_element_type=jnp.float32
    )
    grad_query_b = grad_query.astype(jnp.bfloat16) * jnp.bfloat16(0.125)
    stacked = jnp.concatenate(
        [
            grad_query_b.reshape(-1, model_width),
            grad_key.astype(jnp.bfloat16).reshape(-1, model_width),
            grad_value.astype(jnp.bfloat16).reshape(-1, model_width),
        ],
        axis=1,
    )
    grad_qkv = jnp.einsum("rd,re->de", first_in, stacked, preferred_element_type=jnp.float32)
    grad_query_shift = jnp.sum(stacked[:, :model_width].astype(jnp.float32), axis=0)
    grad_value_shift = jnp.sum(stacked[:, 2 * model_width :].astype(jnp.float32), axis=0)
    grad_normed1 = jnp.einsum(
        "re,de->rd", stacked, attn_back[3], preferred_element_type=jnp.float32
    )
    grad_hidden0_norm, grad_gain_one, grad_shift_one = first_pull(
        grad_normed1.reshape(item_count, row_count, model_width)
    )
    grad_hidden0 = grad_hidden1 + grad_hidden0_norm
    grad_tokens = grad_hidden0 * (1.0 - mask_rows)
    grad_mask = jnp.sum(grad_hidden0 * mask_rows, axis=(0, 1))
    ffn_share = (
        lax.psum_scatter(grad_gain_two, "fsdp", scatter_dimension=0, tiled=True),
        lax.psum_scatter(grad_shift_two, "fsdp", scatter_dimension=0, tiled=True),
        lax.psum_scatter(vision_grads[0], "fsdp", scatter_dimension=0, tiled=True),
        lax.psum_scatter(vision_grads[1], "fsdp", scatter_dimension=0, tiled=True),
        lax.psum_scatter(vision_grads[2], "fsdp", scatter_dimension=0, tiled=True),
        lax.psum_scatter(vision_grads[3], "fsdp", scatter_dimension=0, tiled=True),
        lax.psum_scatter(text_grads[0], "fsdp", scatter_dimension=0, tiled=True),
        lax.psum_scatter(text_grads[1], "fsdp", scatter_dimension=0, tiled=True),
        lax.psum_scatter(text_grads[2], "fsdp", scatter_dimension=0, tiled=True),
        lax.psum_scatter(text_grads[3], "fsdp", scatter_dimension=0, tiled=True),
    )
    attn_share = (
        lax.psum_scatter(grad_mask, "fsdp", scatter_dimension=0, tiled=True),
        lax.psum_scatter(grad_gain_one, "fsdp", scatter_dimension=0, tiled=True),
        lax.psum_scatter(grad_shift_one, "fsdp", scatter_dimension=0, tiled=True),
        lax.psum_scatter(grad_qkv, "fsdp", scatter_dimension=0, tiled=True),
        lax.psum_scatter(grad_query_shift, "fsdp", scatter_dimension=0, tiled=True),
        lax.psum_scatter(grad_value_shift, "fsdp", scatter_dimension=0, tiled=True),
        lax.psum_scatter(grad_out_matrix, "fsdp", scatter_dimension=0, tiled=True),
        lax.psum_scatter(grad_out_shift, "fsdp", scatter_dimension=0, tiled=True),
    )
    quarter = (
        lax.psum_scatter(
            attn_share[0].astype(jnp.bfloat16), "rep", scatter_dimension=0, tiled=True
        ).astype(jnp.float32),
        lax.psum_scatter(
            attn_share[1].astype(jnp.bfloat16), "rep", scatter_dimension=0, tiled=True
        ).astype(jnp.float32),
        lax.psum_scatter(
            attn_share[2].astype(jnp.bfloat16), "rep", scatter_dimension=0, tiled=True
        ).astype(jnp.float32),
        lax.psum_scatter(
            attn_share[3].astype(jnp.bfloat16), "rep", scatter_dimension=0, tiled=True
        ).astype(jnp.float32),
        lax.psum_scatter(
            attn_share[4].astype(jnp.bfloat16), "rep", scatter_dimension=0, tiled=True
        ).astype(jnp.float32),
        lax.psum_scatter(
            attn_share[5].astype(jnp.bfloat16), "rep", scatter_dimension=0, tiled=True
        ).astype(jnp.float32),
        lax.psum_scatter(
            attn_share[6].astype(jnp.bfloat16), "rep", scatter_dimension=0, tiled=True
        ).astype(jnp.float32),
        lax.psum_scatter(
            attn_share[7].astype(jnp.bfloat16), "rep", scatter_dimension=0, tiled=True
        ).astype(jnp.float32),
        lax.psum_scatter(
            ffn_share[0].astype(jnp.bfloat16), "rep", scatter_dimension=0, tiled=True
        ).astype(jnp.float32),
        lax.psum_scatter(
            ffn_share[1].astype(jnp.bfloat16), "rep", scatter_dimension=0, tiled=True
        ).astype(jnp.float32),
        lax.psum_scatter(
            ffn_share[2].astype(jnp.bfloat16), "rep", scatter_dimension=0, tiled=True
        ).astype(jnp.float32),
        lax.psum_scatter(
            ffn_share[3].astype(jnp.bfloat16), "rep", scatter_dimension=0, tiled=True
        ).astype(jnp.float32),
        lax.psum_scatter(
            ffn_share[4].astype(jnp.bfloat16), "rep", scatter_dimension=0, tiled=True
        ).astype(jnp.float32),
        lax.psum_scatter(
            ffn_share[5].astype(jnp.bfloat16), "rep", scatter_dimension=0, tiled=True
        ).astype(jnp.float32),
        lax.psum_scatter(
            ffn_share[6].astype(jnp.bfloat16), "rep", scatter_dimension=0, tiled=True
        ).astype(jnp.float32),
        lax.psum_scatter(
            ffn_share[7].astype(jnp.bfloat16), "rep", scatter_dimension=0, tiled=True
        ).astype(jnp.float32),
        lax.psum_scatter(
            ffn_share[8].astype(jnp.bfloat16), "rep", scatter_dimension=0, tiled=True
        ).astype(jnp.float32),
        lax.psum_scatter(
            ffn_share[9].astype(jnp.bfloat16), "rep", scatter_dimension=0, tiled=True
        ).astype(jnp.float32),
    )
    summed = (
        lax.all_gather(quarter[0].astype(jnp.bfloat16), "rep", axis=0, tiled=True).astype(
            jnp.float32
        ),
        lax.all_gather(quarter[1].astype(jnp.bfloat16), "rep", axis=0, tiled=True).astype(
            jnp.float32
        ),
        lax.all_gather(quarter[2].astype(jnp.bfloat16), "rep", axis=0, tiled=True).astype(
            jnp.float32
        ),
        lax.all_gather(quarter[3].astype(jnp.bfloat16), "rep", axis=0, tiled=True).astype(
            jnp.float32
        ),
        lax.all_gather(quarter[4].astype(jnp.bfloat16), "rep", axis=0, tiled=True).astype(
            jnp.float32
        ),
        lax.all_gather(quarter[5].astype(jnp.bfloat16), "rep", axis=0, tiled=True).astype(
            jnp.float32
        ),
        lax.all_gather(quarter[6].astype(jnp.bfloat16), "rep", axis=0, tiled=True).astype(
            jnp.float32
        ),
        lax.all_gather(quarter[7].astype(jnp.bfloat16), "rep", axis=0, tiled=True).astype(
            jnp.float32
        ),
        lax.all_gather(quarter[8].astype(jnp.bfloat16), "rep", axis=0, tiled=True).astype(
            jnp.float32
        ),
        lax.all_gather(quarter[9].astype(jnp.bfloat16), "rep", axis=0, tiled=True).astype(
            jnp.float32
        ),
        lax.all_gather(quarter[10].astype(jnp.bfloat16), "rep", axis=0, tiled=True).astype(
            jnp.float32
        ),
        lax.all_gather(quarter[11].astype(jnp.bfloat16), "rep", axis=0, tiled=True).astype(
            jnp.float32
        ),
        lax.all_gather(quarter[12].astype(jnp.bfloat16), "rep", axis=0, tiled=True).astype(
            jnp.float32
        ),
        lax.all_gather(quarter[13].astype(jnp.bfloat16), "rep", axis=0, tiled=True).astype(
            jnp.float32
        ),
        lax.all_gather(quarter[14].astype(jnp.bfloat16), "rep", axis=0, tiled=True).astype(
            jnp.float32
        ),
        lax.all_gather(quarter[15].astype(jnp.bfloat16), "rep", axis=0, tiled=True).astype(
            jnp.float32
        ),
        lax.all_gather(quarter[16].astype(jnp.bfloat16), "rep", axis=0, tiled=True).astype(
            jnp.float32
        ),
        lax.all_gather(quarter[17].astype(jnp.bfloat16), "rep", axis=0, tiled=True).astype(
            jnp.float32
        ),
    )
    return (
        mixed.astype(jnp.bfloat16),
        grad_tokens,
        summed[0],
        summed[1],
        summed[2],
        summed[3],
        summed[4],
        summed[5],
        summed[6],
        summed[7],
        summed[8],
        summed[9],
        summed[10],
        summed[11],
        summed[12],
        summed[13],
        summed[14],
        summed[15],
        summed[16],
        summed[17],
    )


def solution(mesh):
    if mesh.shape["fsdp"] == 8 and mesh.shape["rep"] == 4:
        body = planned
    else:
        body = general
    return jax.shard_map(
        body,
        mesh=mesh,
        in_specs=(
            P(("fsdp", "rep"), None, None),
            P(("fsdp", "rep"), None, None),
            P(("fsdp", "rep"), None),
            P(("fsdp", "rep")),
            P("fsdp"),
            P("fsdp"),
            P("fsdp"),
            P("fsdp", None),
            P("fsdp"),
            P("fsdp"),
            P("fsdp", None),
            P("fsdp"),
            P("fsdp"),
            P("fsdp"),
            P("fsdp", None),
            P("fsdp"),
            P("fsdp", None),
            P("fsdp"),
            P("fsdp", None),
            P("fsdp"),
            P("fsdp", None),
            P("fsdp"),
        ),
        out_specs=(
            P(("fsdp", "rep"), None, None),
            P(("fsdp", "rep"), None, None),
            P("fsdp"),
            P("fsdp"),
            P("fsdp"),
            P("fsdp", None),
            P("fsdp"),
            P("fsdp"),
            P("fsdp", None),
            P("fsdp"),
            P("fsdp"),
            P("fsdp"),
            P("fsdp", None),
            P("fsdp"),
            P("fsdp", None),
            P("fsdp"),
            P("fsdp", None),
            P("fsdp"),
            P("fsdp", None),
            P("fsdp"),
        ),
        check_vma=False,
    )
```

profile of v0, /device:TPU:0, one launch (start us, length us, event | category | flops | bytes accessed | tf_op | source)
XLA Modules:
  0.0 350.0 jit_solution(6012123955597522757)
XLA Ops:
  7.3 3.0 collective-permute-start.5
  10.3 1.5 collective-permute-start.4
  11.8 1.5 stack.97
  14.6 2.9 collective-permute-start.2
  17.5 2.1 copy.117.tokens
  21.1 4.3 %shard_map.365 = (bf16[512,768]{1,0:T(8,128)(2,1)}, bf16[512,768]{1,0:T(8,128)(2,1)}, bf16[416,768]{1,0:T(8,128)(2,1)}, bf16[80,768]{1,0:T(8,128)(2,1)}, f32[2,7...) custom-call(s32[4]{0:T(128)} %pad_add_fusion.info, ...), custom_call_target="tpu_custom_call" | custom-call | flops 1100000000 | bytes 1000000 | tf_op jit(solution)/shard_map/pallas_call | solution.py:498
  30.9 4.8 %shard_map.368 = (bf16[512,768]{1,0:T(8,128)(2,1)}, f32[16,768]{1,0:T(8,128)}, f32[1,1536]{1,0:T(1,128)}) custom-call(s32[4]{0:T(128)} %pad_add_fusion.info, bf16[512,768]{1,0:T(8,128)(2,1)} %get-tuple-element.125.refs_2_.tok, f32[512,1]{1,0:T(8,128)} %bitcast.125, bf16[4,16,128]{2,1,0:T(8,128)(2,1)} %shard_map.366.even, bf16[4,16,128]{2,1,0:T(8,128)(2,1)} %copy-done.80, ...), custom_call_target="tpu_custom_call" | custom-call | flops 1100000000 | bytes 1000000 | tf_op jit(solution)/shard_map/pallas_call | solution.py:498
  35.7 1.3 collective-permute-done.6.refs_0_
  39.5 1.5 collective-permute-start.18
  41.8 8.0 %shard_map.370.refs_1_.qkv = bf16[512,2304]{1,0:T(8,128)(2,1)} custom-call(s32[4]{0:T(128)} %pad_add_fusion.info, bf16[512,768]{1,0:T(8,128)(2,1)} %get-tuple-element.129.refs_5_.n1.left, f32[16,768]{1,0:T(8,128)} %get-tuple-element.128.vec, bf16[96,2304]{1,0:T(8,128)(2,1)} %refs_0_.3, bf16[96,2304]{1,0:T(8,128)(2,1)} %copy-done.24, ...), custom_call_target="tpu_custom_call" | custom-call | flops 1760000000 | bytes 1600000 | tf_op jit(solution)/shard_map/pallas_call | solution.py:498
  54.6 1.5 collective-permute-start.17
  56.2 11.4 %shard_map.372 = (bf16[12,512,256]{2,1,0:T(8,128)(2,1)}, bf16[512,768]{1,0:T(8,128)(2,1)}) custom-call(s32[4]{0:T(128)} %pad_add_fusion.info, bf16[512,2304]{1,0:T(8,128)(2,1)} %shard_map.370.refs_1_.qkv, f32[8,128]{1,0:T(8,128)} %shard_map.371.refs_0_.refs_4_), custom_call_target="tpu_custom_call" | custom-call | flops 2200000000 | bytes 2000000 | tf_op jit(solution)/shard_map/pallas_call | solution.py:498
  67.6 4.4 %collective-permute-done.17.refs_5_.refs_3_ = bf16[176,768]{1,0:T(8,128)(2,1)S(1)} collective-permute-done((bf16[176,768]{1,0:T(8,128)(2,1)}, bf16[176,768]{1,0:T(8,128)(2,1)S(1)}, u32[]{:S(2)}, u32[]{:S(2)}) %collective-permute-start.17) | collective-permute-done | bytes 270368 | tf_op jit(solution)/shard_map/ppermute | solution.py:510
  72.0 5.9 %collective-permute-done.14.refs_2_.refs_0_ = bf16[2,96,1536]{2,1,0:T(8,128)(2,1)S(1)} collective-permute-done((bf16[2,96,1536]{2,1,0:T(8,128)(2,1)S(1)}, bf16[2,96,1536]{2,1,0:T(8,128)(2,1)S(1)}, u32[]{:S(2)}, u32[]{:S(2)}) %collective-permute-start.14) | collective-permute-done | bytes 589856 | tf_op jit(solution)/shard_map/ppermute | solution.py:510
  82.0 1.5 collective-permute-start.19
  83.5 4.5 %shard_map.375 = (f32[512,768]{1,0:T(8,128)}, bf16[80,768]{1,0:T(8,128)(2,1)}, bf16[208,768]{1,0:T(8,128)(2,1)}, bf16[208,768]{1,0:T(8,128)(2,1)}) custom-call(s32[4]{0:T(128)} %pad_add_fusion.info, bf16[512,768]{1,0:T(8,128)(2,1)} %get-tuple-element.125.refs_2_.tok, f32[512,1]{1,0:T(8,128)} %bitcast.126, f32[16,768]{1,0:T(8,128)} %get-tuple-element.128.vec, ...), custom_call_target="tpu_custom_call" | custom-call | flops 1100000000 | bytes 1000000 | tf_op jit(solution)/shard_map/pallas_call | solution.py:498
  88.0 8.9 %all-gather.6.cloned.1.call-done = bf16[832,768]{1,0:T(8,128)(2,1)} async-done(((bf16[416,768]{1,0:T(8,128)(2,1)}), bf16[832,768]{1,0:T(8,128)(2,1)}) %all-gather.6.cloned.1.call-update) | async-done | bytes 1277968 | tf_op jit(solution)/shard_map/all_gather | solution.py:631
  97.8 2.2 shard_map.379.refs_8_
  100.4 1.7 collective-permute-start.23
  102.1 1.5 collective-permute-start.24
  103.9 10.0 %shard_map.380 = (f32[416,768]{1,0:T(8,128)}, f32[416,768]{1,0:T(8,128)}, bf16[416,1536]{1,0:T(8,128)(2,1)}, bf16[416,1536]{1,0:T(8,128)(2,1)}) custom-call(s32[4]{0:T(128)} %pad_add_fusion.info, bf16[416,768]{1,0:T(8,128)(2,1)} %get-tuple-element.148.grad, f32[1,1536]{1,0:T(1,128)} %get-tuple-element.149.up_bias, ...), custom_call_target="tpu_custom_call" | custom-call | flops 1980000000 | bytes 1800000 | tf_op jit(solution)/shard_map/pallas_call | solution.py:498
  113.9 2.2 collective-permute-done.25.refs_4_.refs_3_
  121.1 6.3 %shard_map.383 = (bf16[4,80,768]{2,1,0:T(8,128)(2,1)}, bf16[4,80,768]{2,1,0:T(8,128)(2,1)}, bf16[4,80,768]{2,1,0:T(8,128)(2,1)}, bf16[4,80,768]{2,1,0:T(8,128)(2...) custom-call(s32[4]{0:T(128)} %pad_add_fusion.info, ...), custom_call_target="tpu_custom_call" | custom-call | flops 1320000000 | bytes 1200000 | tf_op jit(solution)/shard_map/pallas_call | solution.py:498
  127.5 1.8 collective-permute-done.28.refs_3_.refs_2_
  130.0 2.1 collective-permute-done.29
  133.3 2.5 collective-permute-start.32
  135.8 10.3 %shard_map.387 = (bf16[416,768]{1,0:T(8,128)(2,1)}, bf16[416,768]{1,0:T(8,128)(2,1)}, bf16[416,1536]{1,0:T(8,128)(2,1)}, bf16[416,1536]{1,0:T(8,128)(2,1)}) custom-call(s32[4]{0:T(128)} %pad_add_fusion.info, bf16[2,416,768]{2,1,0:T(8,128)(2,1)} %bitcast.119, f32[1,1536]{1,0:T(1,128)} %get-tuple-element.149.up_bias, ...), custom_call_target="tpu_custom_call" | custom-call | flops 1980000000 | bytes 1800000 | tf_op jit(solution)/shard_map/pallas_call | solution.py:498
  147.4 12.3 %shard_map.389 = (bf16[4,96,1536]{2,1,0:T(8,128)(2,1)}, bf16[4,96,1536]{2,1,0:T(8,128)(2,1)}, bf16[2,384,768]{2,1,0:T(8,128)(2,1)}, bf16[2,384,768]{2,1,0:T(8,128)(2,1)}, f32[1,1536]{1,0:T(1,128)}) custom-call(s32[4]{0:T(128)} %pad_add_fusion.info, bf16[208,768]{1,0:T(8,128)(2,1)} %get-tuple-element.159.refs_0_, ...), custom_call_target="tpu_custom_call" | custom-call | flops 2640000000 | bytes 2400000 | tf_op jit(solution)/shard_map/pallas_call | solution.py:498
  159.8 2.9 collective-permute-done.33.refs_2_.refs_4_
  167.2 1.4 fusion.3.refs_0_
  169.1 2.1 fusion.10
  171.2 1.6 collective-permute-start.38
  172.7 18.1 %shard_map.393 = (f32[512,768]{1,0:T(8,128)}, bf16[512,768]{1,0:T(8,128)(2,1)}, bf16[512,2304]{1,0:T(8,128)(2,1)}, f32[8,768]{1,0:T(8,128)}) custom-call(s32[4]{0:T(128)} %pad_add_fusion.info, f32[416,768]{1,0:T(8,128)} %get-tuple-element.168.refs_1_.gn2v, bf16[416,768]{1,0:T(8,128)(2,1)} %get-tuple-element.189.gn2x, bf16[4,80,768]{2,1,0:T(8,128)(2,1)} %copy-done.45, ...), custom_call_target="tpu_custom_call" | custom-call | flops 3960000000 | bytes 3600000 | tf_op jit(solution)/shard_map/pallas_call | solution.py:498
  192.3 1.3 fusion.8
  193.6 1.5 collective-permute-start.40
  195.9 1.4 convert_add_fusion
  198.4 5.4 %shard_map.395 = (bf16[4,96,1536]{2,1,0:T(8,128)(2,1)}, bf16[4,96,1536]{2,1,0:T(8,128)(2,1)}) custom-call(s32[4]{0:T(128)} %pad_add_fusion.info, bf16[512,768]{1,0:T(8,128)(2,1)} %get-tuple-element.129.refs_5_.n1.left, bf16[512,2304]{1,0:T(8,128)(2,1)} %get-tuple-element.196.refs_1_.refs_0_.refs_2_.stacked, f32[8,128]{1,0:T(8,128)} %shard_map.394.refs_1_.refs_4_.refs_0_), custom_call_target="tpu_custom_call" | custom-call | flops 1100000000 | bytes 1000000 | tf_op jit(solution)/shard_map/pallas_call | solution.py:498
  204.7 3.2 fusion.1
  209.1 2.2 fusion.2.refs_13_
  211.3 5.3 %shard_map.399 = (bf16[4,96,1536]{2,1,0:T(8,128)(2,1)}, bf16[4,96,1536]{2,1,0:T(8,128)(2,1)}) custom-call(s32[4]{0:T(128)} %pad_add_fusion.info, bf16[512,768]{1,0:T(8,128)(2,1)} %get-tuple-element.129.refs_5_.n1.left, bf16[512,768]{1,0:T(8,128)(2,1)} %get-tuple-element.137.refs_1_.ctx.refs_0_, bf16[512,768]{1,0:T(8,128)(2,1)} %get-tuple-element.203.refs_1_, ...), custom_call_target="tpu_custom_call" | custom-call | flops 1100000000 | bytes 1000000 | tf_op jit(solution)/shard_map/pallas_call | solution.py:498
  223.3 1.3 collective-permute-start.48
  225.5 1.7 slice_bitcast_fusion.9
  227.3 1.5 collective-permute-start.43
  230.7 11.5 %shard_map.402 = (f32[512,768]{1,0:T(8,128)}, f32[8,768]{1,0:T(8,128)}) custom-call(s32[4]{0:T(128)} %pad_add_fusion.info, bf16[512,2304]{1,0:T(8,128)(2,1)} %get-tuple-element.196.refs_1_.refs_0_.refs_2_.stacked, f32[512,768]{1,0:T(8,128)} %get-tuple-element.209.gh1, bf16[512,768]{1,0:T(8,128)(2,1)} %get-tuple-element.125.refs_2_.tok, f32[512,1]{1,0:T(8,128)} %bitcast.127, ...), custom_call_target="tpu_custom_call" | custom-call | flops 2640000000 | bytes 2400000 | tf_op jit(solution)/shard_map/pallas_call | solution.py:498
  242.5 1.9 collective-permute-done.44.refs_5_
  246.2 1.9 fusion.11.refs_1_
  248.2 1.8 fusion.12.refs_2_
  253.1 1.5 collective-permute-start.56
  256.1 1.8 pad_maximum_fusion.3
  258.9 4.8 %collective-permute-done.51 = f32[14,768]{1,0:T(8,128)} collective-permute-done((f32[14,768]{1,0:T(8,128)}, f32[14,768]{1,0:T(8,128)}, u32[]{:S(2)}, u32[]{:S(2)}) %collective-permute-start.51) | collective-permute-done | bytes 43040 | tf_op jit(solution)/shard_map/ppermute | solution.py:510
  264.5 1.4 collective-permute-start.52
  265.9 1.7 pad_maximum_fusion
  268.8 2.0 fusion.5.refs_4_
  270.8 5.2 %collective-permute-done.49 = bf16[96,1536]{1,0:T(8,128)(2,1)S(1)} collective-permute-done((bf16[96,1536]{1,0:T(8,128)(2,1)S(1)}, bf16[96,1536]{1,0:T(8,128)(2,1)S(1)}, u32[]{:S(2)}, u32[]{:S(2)}) %collective-permute-start.49) | collective-permute-done | bytes 294944 | tf_op jit(solution)/shard_map/ppermute | solution.py:510
  276.0 1.8 fusion.6.refs_3_
  278.8 3.4 collective-permute-start.57
  282.2 2.2 convert_element_type.375
  284.4 1.3 collective-permute-start.53
  286.0 1.6 collective-permute-start.61
  288.2 1.3 collective-permute-start.63
  290.4 6.9 %collective-permute-done.53 = bf16[104,1536]{1,0:T(8,128)(2,1)S(1)} collective-permute-done((bf16[104,1536]{1,0:T(8,128)(2,1)S(1)}, bf16[104,1536]{1,0:T(8,128)(2,1)S(1)}, u32[]{:S(2)}, u32[]{:S(2)}) %collective-permute-start.53) | collective-permute-done | bytes 319520 | tf_op jit(solution)/shard_map/ppermute | solution.py:514
  299.3 1.3 collective-permute-start.59
  302.0 25.4 %collective-permute-done.59 = bf16[96,1536]{1,0:T(8,128)(2,1)S(1)} collective-permute-done((bf16[96,1536]{1,0:T(8,128)(2,1)S(1)}, bf16[96,1536]{1,0:T(8,128)(2,1)S(1)}, u32[]{:S(2)}, u32[]{:S(2)}) %collective-permute-start.59) | collective-permute-done | bytes 294944 | tf_op jit(solution)/shard_map/ppermute | solution.py:514
  328.2 9.1 %collective-permute-done.55 = bf16[104,1536]{1,0:T(8,128)(2,1)S(1)} collective-permute-done((bf16[104,1536]{1,0:T(8,128)(2,1)S(1)}, bf16[104,1536]{1,0:T(8,128)(2,1)S(1)}, u32[]{:S(2)}, u32[]{:S(2)}) %collective-permute-start.55) | collective-permute-done | bytes 319520 | tf_op jit(solution)/shard_map/ppermute | solution.py:514
  (390 shorter events, 72.2 us)
Async XLA Ops:
  7.2 76.3 %all-gather.4.cloned.1.call-start = ((), (), s32[]{:S(2)}) async-start(), calls=%async_computation | async-start | bytes 1327104 | tf_op jit(solution)/shard_map/all_gather | solution.py:629
  7.3 18.2 %collective-permute-start.5 = (bf16[96,2304]{1,0:T(8,128)(2,1)}, bf16[96,2304]{1,0:T(8,128)(2,1)S(1)}, u32[]{:S(2)}, u32[]{:S(2)}) collective-permute-start(bf16[96,2304]{1,0:T(8,128)(2,1)} %refs_0_.3), channel_id=1, source_target_pairs={{0,16},{4,20},{8,24},{12,28},{16,0},{20,4},{24,8},{28,12},{1,17},{... | collective-permute-start | bytes 1327112 | tf_op jit(solution)/shard_map/ppermute | solution.py:510
  10.3 15.7 %collective-permute-start.4 = (bf16[96,2304]{1,0:T(8,128)(2,1)}, bf16[96,2304]{1,0:T(8,128)(2,1)S(1)}, u32[]{:S(2)}, u32[]{:S(2)}) collective-permute-start(bf16[96,2304]{1,0:T(8,128)(2,1)} %refs_0_.3), channel_id=1, source_target_pairs={{0,8},{4,12},{8,0},{12,4},{16,24},{20,28},{24,16},{28,20},{1,9},{5... | collective-permute-start | bytes 1327112 | tf_op jit(solution)/shard_map/ppermute | solution.py:510
  14.0 11.4 %collective-permute-start = (bf16[1,16,128]{2,1,0:T(8,128)(2,1)S(1)}, bf16[1,16,128]{2,1,0:T(8,128)(2,1)S(1)}, u32[]{:S(2)}, u32[]{:S(2)}) collective-permute-start(bf16[1,16,128]{2,1,0:T(8,128)(2,1)S(1)} %pad_bitcast_fusion), channel_id=1, source_target_pairs={{0,8},{4,12},{8,0},{12,4},{16,24},{20,28},{24,16},{28,20},{1,9},{5... | collective-permute-start | bytes 12296 | tf_op jit(solution)/shard_map/ppermute | solution.py:510
  14.6 11.5 %collective-permute-start.1 = (bf16[1,16,128]{2,1,0:T(8,128)(2,1)S(1)}, bf16[1,16,128]{2,1,0:T(8,128)(2,1)S(1)}, u32[]{:S(2)}, u32[]{:S(2)}) collective-permute-start(bf16[1,16,128]{2,1,0:T(8,128)(2,1)S(1)} %pad_bitcast_fusion), channel_id=1, source_target_pairs={{0,16},{4,20},{8,24},{12,28},{16,0},{20,4},{24,8},{28,12},{1,17},{... | collective-permute-start | bytes 12296 | tf_op jit(solution)/shard_map/ppermute | solution.py:510
  14.6 11.4 %collective-permute-start.2 = (bf16[1,16,128]{2,1,0:T(8,128)(2,1)S(1)}, bf16[1,16,128]{2,1,0:T(8,128)(2,1)S(1)}, u32[]{:S(2)}, u32[]{:S(2)}) collective-permute-start(bf16[1,16,128]{2,1,0:T(8,128)(2,1)S(1)} %pad_bitcast_fusion), channel_id=1, source_target_pairs={{0,24},{4,28},{8,16},{12,20},{16,8},{20,12},{24,0},{28,4},{1,25},{... | collective-permute-start | bytes 12296 | tf_op jit(solution)/shard_map/ppermute | solution.py:510
  25.4 10.3 %collective-permute-start.8 = (bf16[96,2304]{1,0:T(8,128)(2,1)S(1)}, bf16[96,2304]{1,0:T(8,128)(2,1)S(1)}, u32[]{:S(2)}, u32[]{:S(2)}) collective-permute-start(bf16[96,2304]{1,0:T(8,128)(2,1)S(1)} %copy-done.44), channel_id=1, source_target_pairs={{0,4},{4,0},{8,12},{12,8},{16,20},{20,16},{24,28},{28,24},{1,5},{5... | collective-permute-start | bytes 1327112 | tf_op jit(solution)/shard_map/ppermute | solution.py:510
  25.5 11.8 %collective-permute-start.10 = (bf16[96,2304]{1,0:T(8,128)(2,1)S(1)}, bf16[96,2304]{1,0:T(8,128)(2,1)S(1)}, u32[]{:S(2)}, u32[]{:S(2)}) collective-permute-start(bf16[96,2304]{1,0:T(8,128)(2,1)S(1)} %collective-permute-done.5.refs_2_), channel_id=1, source_target_pairs={{0,4},{4,0},{8,12},{12,8},{16,20},{20,16},{24,28},{28,24},{1,5},{5... | collective-permute-start | bytes 1327112 | tf_op jit(solution)/shard_map/ppermute | solution.py:510
  26.0 11.3 %collective-permute-start.9 = (bf16[96,2304]{1,0:T(8,128)(2,1)S(1)}, bf16[96,2304]{1,0:T(8,128)(2,1)S(1)}, u32[]{:S(2)}, u32[]{:S(2)}) collective-permute-start(bf16[96,2304]{1,0:T(8,128)(2,1)S(1)} %collective-permute-done.4.refs_1_), channel_id=1, source_target_pairs={{0,4},{4,0},{8,12},{12,8},{16,20},{20,16},{24,28},{28,24},{1,5},{5... | collective-permute-start | bytes 1327112 | tf_op jit(solution)/shard_map/ppermute | solution.py:510
  29.4 7.7 %collective-permute-start.6 = (bf16[48,2304]{1,0:T(8,128)(2,1)}, bf16[48,2304]{1,0:T(8,128)(2,1)S(1)}, u32[]{:S(2)}, u32[]{:S(2)}) collective-permute-start(bf16[48,2304]{1,0:T(8,128)(2,1)} %get-tuple-element.127.refs_0_), channel_id=1, source_target_pairs={{0,16},{4,20},{8,24},{12,28},{16,0},{20,4},{24,8},{28,12},{1,17},{... | collective-permute-start | bytes 663560 | tf_op jit(solution)/shard_map/ppermute | solution.py:510
  29.9 7.4 %collective-permute-start.7 = (bf16[48,2304]{1,0:T(8,128)(2,1)}, bf16[48,2304]{1,0:T(8,128)(2,1)S(1)}, u32[]{:S(2)}, u32[]{:S(2)}) collective-permute-start(bf16[48,2304]{1,0:T(8,128)(2,1)} %get-tuple-element.130), channel_id=1, source_target_pairs={{0,8},{4,12},{8,0},{12,4},{16,24},{20,28},{24,16},{28,20},{1,9},{5... | collective-permute-start | bytes 663560 | tf_op jit(solution)/shard_map/ppermute | solution.py:510
  38.3 58.6 %all-gather.6.cloned.1.call-start = ((), (), s32[]{:S(2)}) async-start(), calls=%async_computation.1 | async-start | bytes 1916928 | tf_op jit(solution)/shard_map/all_gather | solution.py:631
  38.4 2.6 collective-permute-start.11
  38.5 2.6 collective-permute-start.12
  39.0 10.9 %collective-permute-start.13 = (bf16[96,1536]{1,0:T(8,128)(2,1)}, bf16[96,1536]{1,0:T(8,128)(2,1)S(1)}, u32[]{:S(2)}, u32[]{:S(2)}) collective-permute-start(bf16[96,1536]{1,0:T(8,128)(2,1)} %get-tuple-element.136), channel_id=1, source_target_pairs={{0,8},{4,12},{8,0},{12,4},{16,24},{20,28},{24,16},{28,20},{1,9},{5... | collective-permute-start | bytes 884744 | tf_op jit(solution)/shard_map/ppermute | solution.py:510
  39.5 32.5 %collective-permute-start.18 = (bf16[384,768]{1,0:T(8,128)(2,1)}, bf16[384,768]{1,0:T(8,128)(2,1)S(1)}, u32[]{:S(2)}, u32[]{:S(2)}) collective-permute-start(bf16[384,768]{1,0:T(8,128)(2,1)} %get-tuple-element.146), channel_id=1, source_target_pairs={{0,16},{4,20},{8,24},{12,28},{16,0},{20,4},{24,8},{28,12},{1,17},{... | collective-permute-start | bytes 1769480 | tf_op jit(solution)/shard_map/ppermute | solution.py:510
  52.5 25.4 %collective-permute-start.14 = (bf16[2,96,1536]{2,1,0:T(8,128)(2,1)S(1)}, bf16[2,96,1536]{2,1,0:T(8,128)(2,1)S(1)}, u32[]{:S(2)}, u32[]{:S(2)}) collective-permute-start(bf16[2,96,1536]{2,1,0:T(8,128)(2,1)S(1)} %pad_maximum_fusion.4.refs_2_), channel_id=1, source_target_pairs={{0,16},{4,20},{8,24},{12,28},{16,0},{20,4},{24,8},{28,12},{1,17},{... | collective-permute-start | bytes 1769480 | tf_op jit(solution)/shard_map/ppermute | solution.py:510
  53.5 24.4 %collective-permute-start.15 = (bf16[2,96,1536]{2,1,0:T(8,128)(2,1)S(1)}, bf16[2,96,1536]{2,1,0:T(8,128)(2,1)S(1)}, u32[]{:S(2)}, u32[]{:S(2)}) collective-permute-start(bf16[2,96,1536]{2,1,0:T(8,128)(2,1)S(1)} %pad_maximum_fusion.4.refs_2_), channel_id=1, source_target_pairs={{0,4},{4,0},{8,12},{12,8},{16,20},{20,16},{24,28},{28,24},{1,5},{5... | collective-permute-start | bytes 1769480 | tf_op jit(solution)/shard_map/ppermute | solution.py:510
  53.5 14.1 %collective-permute-start.16 = (bf16[176,768]{1,0:T(8,128)(2,1)S(1)}, bf16[176,768]{1,0:T(8,128)(2,1)S(1)}, u32[]{:S(2)}, u32[]{:S(2)}) collective-permute-start(bf16[176,768]{1,0:T(8,128)(2,1)S(1)} %copy-done.75), channel_id=1, source_target_pairs={{0,8},{4,12},{8,0},{12,4},{16,24},{20,28},{24,16},{28,20},{1,9},{5... | collective-permute-start | bytes 811016 | tf_op jit(solution)/shard_map/ppermute | solution.py:510
  54.6 17.4 %collective-permute-start.17 = (bf16[176,768]{1,0:T(8,128)(2,1)}, bf16[176,768]{1,0:T(8,128)(2,1)S(1)}, u32[]{:S(2)}, u32[]{:S(2)}) collective-permute-start(bf16[176,768]{1,0:T(8,128)(2,1)} %get-tuple-element.145), channel_id=1, source_target_pairs={{0,24},{4,28},{8,16},{12,20},{16,8},{20,12},{24,0},{28,4},{1,25},{... | collective-permute-start | bytes 811016 | tf_op jit(solution)/shard_map/ppermute | solution.py:510
  56.1 221.7 %all-reduce.10.cloned.1.call-start = ((), (), s32[]{:S(2)}) async-start(), calls=%async_computation.2 | async-start | bytes 2359296 | tf_op jit(solution)/shard_map/psum | solution.py:749
  81.4 15.6 %collective-permute-start.21 = (bf16[2,384,768]{2,1,0:T(8,128)(2,1)S(1)}, bf16[2,384,768]{2,1,0:T(8,128)(2,1)}, u32[]{:S(2)}, u32[]{:S(2)}) collective-permute-start(bf16[2,384,768]{2,1,0:T(8,128)(2,1)S(1)} %pad_maximum_fusion.1.refs_6_), channel_id=1, source_target_pairs={{0,4},{4,0},{8,12},{12,8},{16,20},{20,16},{24,28},{28,24},{1,5},{5... | collective-permute-start | bytes 3538952 | tf_op jit(solution)/shard_map/ppermute | solution.py:510
  81.5 15.5 %collective-permute-start.20 = (bf16[2,96,1536]{2,1,0:T(8,128)(2,1)S(1)}, bf16[2,96,1536]{2,1,0:T(8,128)(2,1)S(1)}, u32[]{:S(2)}, u32[]{:S(2)}) collective-permute-start(bf16[2,96,1536]{2,1,0:T(8,128)(2,1)S(1)} %copy-done.40), channel_id=1, source_target_pairs={{0,4},{4,0},{8,12},{12,8},{16,20},{20,16},{24,28},{28,24},{1,5},{5... | collective-permute-start | bytes 1769480 | tf_op jit(solution)/shard_map/ppermute | solution.py:510
  82.0 15.0 %collective-permute-start.19 = (bf16[176,768]{1,0:T(8,128)(2,1)S(1)}, bf16[176,768]{1,0:T(8,128)(2,1)S(1)}, u32[]{:S(2)}, u32[]{:S(2)}) collective-permute-start(bf16[176,768]{1,0:T(8,128)(2,1)S(1)} %copy-done.61), channel_id=1, source_target_pairs={{0,16},{4,20},{8,24},{12,28},{16,0},{20,4},{24,8},{28,12},{1,17},{... | collective-permute-start | bytes 811016 | tf_op jit(solution)/shard_map/ppermute | solution.py:510
  100.0 16.1 %collective-permute-start.22 = (bf16[512,768]{1,0:T(8,128)(2,1)}, bf16[512,768]{1,0:T(8,128)(2,1)S(1)}, u32[]{:S(2)}, u32[]{:S(2)}) collective-permute-start(bf16[512,768]{1,0:T(8,128)(2,1)} %shard_map.379.refs_8_), channel_id=1, source_target_pairs={{0,4},{4,0},{8,12},{12,8},{16,20},{20,16},{24,28},{28,24},{1,5},{5... | collective-permute-start | bytes 2359304 | tf_op jit(solution)/shard_map/ppermute | solution.py:510
  100.0 16.1 %collective-permute-start.26 = (bf16[208,768]{1,0:T(8,128)(2,1)S(1)}, bf16[208,768]{1,0:T(8,128)(2,1)S(1)}, u32[]{:S(2)}, u32[]{:S(2)}) collective-permute-start(bf16[208,768]{1,0:T(8,128)(2,1)S(1)} %copy-done.72), channel_id=1, source_target_pairs={{0,8},{4,12},{8,0},{12,4},{16,24},{20,28},{24,16},{28,20},{1,9},{5... | collective-permute-start | bytes 958472 | tf_op jit(solution)/shard_map/ppermute | solution.py:510
  100.4 13.5 %collective-permute-start.23 = (bf16[80,768]{1,0:T(8,128)(2,1)S(1)}, bf16[80,768]{1,0:T(8,128)(2,1)S(1)}, u32[]{:S(2)}, u32[]{:S(2)}) collective-permute-start(bf16[80,768]{1,0:T(8,128)(2,1)S(1)} %copy-done.60), channel_id=1, source_target_pairs={{0,8},{4,12},{8,0},{12,4},{16,24},{20,28},{24,16},{28,20},{1,9},{5... | collective-permute-start | bytes 368648 | tf_op jit(solution)/shard_map/ppermute | solution.py:510
  102.1 11.8 %collective-permute-start.24 = (bf16[80,768]{1,0:T(8,128)(2,1)S(1)}, bf16[80,768]{1,0:T(8,128)(2,1)S(1)}, u32[]{:S(2)}, u32[]{:S(2)}) collective-permute-start(bf16[80,768]{1,0:T(8,128)(2,1)S(1)} %copy-done.60), channel_id=1, source_target_pairs={{0,16},{4,20},{8,24},{12,28},{16,0},{20,4},{24,8},{28,12},{1,17},{... | collective-permute-start | bytes 368648 | tf_op jit(solution)/shard_map/ppermute | solution.py:510
  103.6 12.6 %collective-permute-start.25 = (bf16[80,768]{1,0:T(8,128)(2,1)S(1)}, bf16[80,768]{1,0:T(8,128)(2,1)S(1)}, u32[]{:S(2)}, u32[]{:S(2)}) collective-permute-start(bf16[80,768]{1,0:T(8,128)(2,1)S(1)} %copy-done.60), channel_id=1, source_target_pairs={{0,24},{4,28},{8,16},{12,20},{16,8},{20,12},{24,0},{28,4},{1,25},{... | collective-permute-start | bytes 368648 | tf_op jit(solution)/shard_map/ppermute | solution.py:510
  119.2 10.1 %collective-permute-start.28 = (bf16[208,768]{1,0:T(8,128)(2,1)}, bf16[208,768]{1,0:T(8,128)(2,1)S(1)}, u32[]{:S(2)}, u32[]{:S(2)}) collective-permute-start(bf16[208,768]{1,0:T(8,128)(2,1)} %shard_map.384), channel_id=1, source_target_pairs={{0,8},{4,12},{8,0},{12,4},{16,24},{20,28},{24,16},{28,20},{1,9},{5... | collective-permute-start | bytes 958472 | tf_op jit(solution)/shard_map/ppermute | solution.py:510
  132.3 13.8 %collective-permute-start.30 = (bf16[80,768]{1,0:T(8,128)(2,1)S(1)}, bf16[80,768]{1,0:T(8,128)(2,1)S(1)}, u32[]{:S(2)}, u32[]{:S(2)}) collective-permute-start(bf16[80,768]{1,0:T(8,128)(2,1)S(1)} %get-tuple-element.257), channel_id=1, source_target_pairs={{0,8},{4,12},{8,0},{12,4},{16,24},{20,28},{24,16},{28,20},{1,9},{5... | collective-permute-start | bytes 368648 | tf_op jit(solution)/shard_map/ppermute | solution.py:510
  132.9 13.2 %collective-permute-start.31 = (bf16[80,768]{1,0:T(8,128)(2,1)S(1)}, bf16[80,768]{1,0:T(8,128)(2,1)S(1)}, u32[]{:S(2)}, u32[]{:S(2)}) collective-permute-start(bf16[80,768]{1,0:T(8,128)(2,1)S(1)} %get-tuple-element.256), channel_id=1, source_target_pairs={{0,16},{4,20},{8,24},{12,28},{16,0},{20,4},{24,8},{28,12},{1,17},{... | collective-permute-start | bytes 368648 | tf_op jit(solution)/shard_map/ppermute | solution.py:510
  133.3 12.8 %collective-permute-start.32 = (bf16[80,768]{1,0:T(8,128)(2,1)S(1)}, bf16[80,768]{1,0:T(8,128)(2,1)S(1)}, u32[]{:S(2)}, u32[]{:S(2)}) collective-permute-start(bf16[80,768]{1,0:T(8,128)(2,1)S(1)} %get-tuple-element.255), channel_id=1, source_target_pairs={{0,24},{4,28},{8,16},{12,20},{16,8},{20,12},{24,0},{28,4},{1,25},{... | collective-permute-start | bytes 368648 | tf_op jit(solution)/shard_map/ppermute | solution.py:510
  146.9 15.8 %collective-permute-start.33 = (bf16[416,768]{1,0:T(8,128)(2,1)}, bf16[416,768]{1,0:T(8,128)(2,1)S(1)}, u32[]{:S(2)}, u32[]{:S(2)}) collective-permute-start(bf16[416,768]{1,0:T(8,128)(2,1)} %shard_map.390), channel_id=1, source_target_pairs={{0,8},{4,12},{8,0},{12,4},{16,24},{20,28},{24,16},{28,20},{1,9},{5... | collective-permute-start | bytes 1916936 | tf_op jit(solution)/shard_map/ppermute | solution.py:510
  163.5 3.7 %collective-permute-start.35 = (bf16[2,384,768]{2,1,0:T(8,128)(2,1)}, bf16[2,384,768]{2,1,0:T(8,128)(2,1)}, u32[]{:S(2)}, u32[]{:S(2)}) collective-permute-start(bf16[2,384,768]{2,1,0:T(8,128)(2,1)} %get-tuple-element.193), channel_id=1, source_target_pairs={{0,4},{4,0},{8,12},{12,8},{16,20},{20,16},{24,28},{28,24},{1,5},{5... | collective-permute-start | bytes 3538952 | tf_op jit(solution)/shard_map/ppermute | solution.py:510
  163.5 5.6 %collective-permute-start.36 = (bf16[4,96,1536]{2,1,0:T(8,128)(2,1)}, bf16[4,96,1536]{2,1,0:T(8,128)(2,1)}, u32[]{:S(2)}, u32[]{:S(2)}) collective-permute-start(bf16[4,96,1536]{2,1,0:T(8,128)(2,1)} %get-tuple-element.195), channel_id=1, source_target_pairs={{0,4},{4,0},{8,12},{12,8},{16,20},{20,16},{24,28},{28,24},{1,5},{5... | collective-permute-start | bytes 3538952 | tf_op jit(solution)/shard_map/ppermute | solution.py:510
  166.5 24.4 %collective-permute-start.34 = (bf16[416,768]{1,0:T(8,128)(2,1)}, bf16[416,768]{1,0:T(8,128)(2,1)S(1)}, u32[]{:S(2)}, u32[]{:S(2)}) collective-permute-start(bf16[416,768]{1,0:T(8,128)(2,1)} %get-tuple-element.188), channel_id=1, source_target_pairs={{0,8},{4,12},{8,0},{12,4},{16,24},{20,28},{24,16},{28,20},{1,9},{5... | collective-permute-start | bytes 1916936 | tf_op jit(solution)/shard_map/ppermute | solution.py:510
  167.2 23.7 %collective-permute-start.39 = (bf16[4,80,768]{2,1,0:T(8,128)(2,1)}, bf16[4,80,768]{2,1,0:T(8,128)(2,1)S(1)}, u32[]{:S(2)}, u32[]{:S(2)}) collective-permute-start(bf16[4,80,768]{2,1,0:T(8,128)(2,1)} %get-tuple-element.197), channel_id=1, source_target_pairs={{0,4},{4,0},{8,12},{12,8},{16,20},{20,16},{24,28},{28,24},{1,5},{5... | collective-permute-start | bytes 1474568 | tf_op jit(solution)/shard_map/ppermute | solution.py:510
  168.6 22.4 %collective-permute-start.37 = (bf16[384,768]{1,0:T(8,128)(2,1)S(1)}, bf16[384,768]{1,0:T(8,128)(2,1)S(1)}, u32[]{:S(2)}, u32[]{:S(2)}) collective-permute-start(bf16[384,768]{1,0:T(8,128)(2,1)S(1)} %fusion.3.refs_0_), channel_id=1, source_target_pairs={{0,16},{4,20},{8,24},{12,28},{16,0},{20,4},{24,8},{28,12},{1,17},{... | collective-permute-start | bytes 1769480 | tf_op jit(solution)/shard_map/ppermute | solution.py:510
  171.2 19.8 %collective-permute-start.38 = (bf16[96,1536]{1,0:T(8,128)(2,1)S(1)}, bf16[96,1536]{1,0:T(8,128)(2,1)S(1)}, u32[]{:S(2)}, u32[]{:S(2)}) collective-permute-start(bf16[96,1536]{1,0:T(8,128)(2,1)S(1)} %get-tuple-element.237.refs_2_), channel_id=1, source_target_pairs={{0,16},{4,20},{8,24},{12,28},{16,0},{20,4},{24,8},{28,12},{1,17},{... | collective-permute-start | bytes 884744 | tf_op jit(solution)/shard_map/ppermute | solution.py:510
  193.6 10.2 %collective-permute-start.40 = (bf16[96,1536]{1,0:T(8,128)(2,1)S(1)}, bf16[96,1536]{1,0:T(8,128)(2,1)S(1)}, u32[]{:S(2)}, u32[]{:S(2)}) collective-permute-start(bf16[96,1536]{1,0:T(8,128)(2,1)S(1)} %fusion.8), channel_id=1, source_target_pairs={{0,8},{4,12},{8,0},{12,4},{16,24},{20,28},{24,16},{28,20},{1,9},{5... | collective-permute-start | bytes 884744 | tf_op jit(solution)/shard_map/ppermute | solution.py:510
  195.2 8.7 %collective-permute-start.41 = (bf16[96,1536]{1,0:T(8,128)(2,1)S(1)}, bf16[96,1536]{1,0:T(8,128)(2,1)S(1)}, u32[]{:S(2)}, u32[]{:S(2)}) collective-permute-start(bf16[96,1536]{1,0:T(8,128)(2,1)S(1)} %copy-done.50), channel_id=1, source_target_pairs={{0,16},{4,20},{8,24},{12,28},{16,0},{20,4},{24,8},{28,12},{1,17},{... | collective-permute-start | bytes 884744 | tf_op jit(solution)/shard_map/ppermute | solution.py:510
  204.7 12.0 %collective-permute-start.42 = (bf16[4,96,1536]{2,1,0:T(8,128)(2,1)}, bf16[4,96,1536]{2,1,0:T(8,128)(2,1)S(1)}, u32[]{:S(2)}, u32[]{:S(2)}) collective-permute-start(bf16[4,96,1536]{2,1,0:T(8,128)(2,1)} %get-tuple-element.202), channel_id=1, source_target_pairs={{0,4},{4,0},{8,12},{12,8},{16,20},{20,16},{24,28},{28,24},{1,5},{5... | collective-permute-start | bytes 3538952 | tf_op jit(solution)/shard_map/ppermute | solution.py:510
  217.7 3.7 %collective-permute-start.46 = (bf16[4,96,1536]{2,1,0:T(8,128)(2,1)}, bf16[4,96,1536]{2,1,0:T(8,128)(2,1)S(1)}, u32[]{:S(2)}, u32[]{:S(2)}) collective-permute-start(bf16[4,96,1536]{2,1,0:T(8,128)(2,1)} %get-tuple-element.211), channel_id=1, source_target_pairs={{0,4},{4,0},{8,12},{12,8},{16,20},{20,16},{24,28},{28,24},{1,5},{5... | collective-permute-start | bytes 3538952 | tf_op jit(solution)/shard_map/ppermute | solution.py:510
  220.8 23.6 %collective-permute-start.47 = (bf16[2,96,1536]{2,1,0:T(8,128)(2,1)}, bf16[2,96,1536]{2,1,0:T(8,128)(2,1)S(1)}, u32[]{:S(2)}, u32[]{:S(2)}) collective-permute-start(bf16[2,96,1536]{2,1,0:T(8,128)(2,1)} %add_convert_fusion.2.refs_10_), channel_id=1, source_target_pairs={{0,8},{4,12},{8,0},{12,4},{16,24},{20,28},{24,16},{28,20},{1,9},{5... | collective-permute-start | bytes 1769480 | tf_op jit(solution)/shard_map/ppermute | solution.py:510
  223.3 21.1 %collective-permute-start.48 = (bf16[2,96,1536]{2,1,0:T(8,128)(2,1)}, bf16[2,96,1536]{2,1,0:T(8,128)(2,1)S(1)}, u32[]{:S(2)}, u32[]{:S(2)}) collective-permute-start(bf16[2,96,1536]{2,1,0:T(8,128)(2,1)} %add_convert_fusion.1.refs_11_), channel_id=1, source_target_pairs={{0,16},{4,20},{8,24},{12,28},{16,0},{20,4},{24,8},{28,12},{1,17},{... | collective-permute-start | bytes 1769480 | tf_op jit(solution)/shard_map/ppermute | solution.py:510
  227.3 15.3 %collective-permute-start.43 = (bf16[80,768]{1,0:T(8,128)(2,1)}, bf16[80,768]{1,0:T(8,128)(2,1)}, u32[]{:S(2)}, u32[]{:S(2)}) collective-permute-start(bf16[80,768]{1,0:T(8,128)(2,1)} %get-tuple-element.252), channel_id=1, source_target_pairs={{0,8},{4,12},{8,0},{12,4},{16,24},{20,28},{24,16},{28,20},{1,9},{5... | collective-permute-start | bytes 368648 | tf_op jit(solution)/shard_map/ppermute | solution.py:510
  228.8 15.6 %collective-permute-start.44 = (bf16[80,768]{1,0:T(8,128)(2,1)}, bf16[80,768]{1,0:T(8,128)(2,1)}, u32[]{:S(2)}, u32[]{:S(2)}) collective-permute-start(bf16[80,768]{1,0:T(8,128)(2,1)} %get-tuple-element.254), channel_id=1, source_target_pairs={{0,16},{4,20},{8,24},{12,28},{16,0},{20,4},{24,8},{28,12},{1,17},{... | collective-permute-start | bytes 368648 | tf_op jit(solution)/shard_map/ppermute | solution.py:510
  229.5 14.9 %collective-permute-start.45 = (bf16[80,768]{1,0:T(8,128)(2,1)}, bf16[80,768]{1,0:T(8,128)(2,1)}, u32[]{:S(2)}, u32[]{:S(2)}) collective-permute-start(bf16[80,768]{1,0:T(8,128)(2,1)} %get-tuple-element.253), channel_id=1, source_target_pairs={{0,24},{4,28},{8,16},{12,20},{16,8},{20,12},{24,0},{28,4},{1,25},{... | collective-permute-start | bytes 368648 | tf_op jit(solution)/shard_map/ppermute | solution.py:510
  242.2 96.5 %all-reduce.12.cloned.1.call-start = ((), (), s32[]{:S(2)}) async-start(), calls=%async_computation.3 | async-start | bytes 2359296 | tf_op jit(solution)/shard_map/psum | solution.py:825
  253.1 15.7 %collective-permute-start.56 = (bf16[96,1536]{1,0:T(8,128)(2,1)S(1)}, bf16[96,1536]{1,0:T(8,128)(2,1)}, u32[]{:S(2)}, u32[]{:S(2)}) collective-permute-start(bf16[96,1536]{1,0:T(8,128)(2,1)S(1)} %copy-done.56), channel_id=1, source_target_pairs={{0,8},{4,12},{8,0},{12,4},{16,24},{20,28},{24,16},{28,20},{1,9},{5... | collective-permute-start | bytes 884744 | tf_op jit(solution)/shard_map/ppermute | solution.py:510
  255.2 8.5 %collective-permute-start.51 = (f32[14,768]{1,0:T(8,128)}, f32[14,768]{1,0:T(8,128)}, u32[]{:S(2)}, u32[]{:S(2)}) collective-permute-start(f32[14,768]{1,0:T(8,128)} %add.218), channel_id=1, source_target_pairs={{0,8},{4,12},{8,0},{12,4},{16,24},{20,28},{24,16},{28,20},{1,9},{5... | collective-permute-start | bytes 129032 | tf_op jit(solution)/shard_map/ppermute | solution.py:510
  264.5 4.2 %collective-permute-start.52 = (f32[14,768]{1,0:T(8,128)S(1)}, f32[14,768]{1,0:T(8,128)S(1)}, u32[]{:S(2)}, u32[]{:S(2)}) collective-permute-start(f32[14,768]{1,0:T(8,128)S(1)} %add.219), channel_id=1, source_target_pairs={{0,16},{4,20},{8,24},{12,28},{16,0},{20,4},{24,8},{28,12},{1,17},{... | collective-permute-start | bytes 129032 | tf_op jit(solution)/shard_map/ppermute | solution.py:510
  267.6 8.3 %collective-permute-start.49 = (bf16[96,1536]{1,0:T(8,128)(2,1)S(1)}, bf16[96,1536]{1,0:T(8,128)(2,1)S(1)}, u32[]{:S(2)}, u32[]{:S(2)}) collective-permute-start(bf16[96,1536]{1,0:T(8,128)(2,1)S(1)} %copy-done.55), channel_id=1, source_target_pairs={{0,16},{4,20},{8,24},{12,28},{16,0},{20,4},{24,8},{28,12},{1,17},{... | collective-permute-start | bytes 884744 | tf_op jit(solution)/shard_map/ppermute | solution.py:510
  277.8 8.0 %collective-permute-start.60 = (bf16[4,96,384]{2,1,0:T(8,128)(2,1)}, bf16[4,96,384]{2,1,0:T(8,128)(2,1)S(1)}, u32[]{:S(2)}, u32[]{:S(2)}) collective-permute-start(bf16[4,96,384]{2,1,0:T(8,128)(2,1)} %get-tuple-element.228), channel_id=1, source_target_pairs={{0,4},{4,0},{8,12},{12,8},{16,20},{20,16},{24,28},{28,24},{1,5},{5... | collective-permute-start | bytes 884744 | tf_op jit(solution)/shard_map/ppermute | solution.py:510
  278.8 10.8 %collective-permute-start.57 = (bf16[96,1536]{1,0:T(8,128)(2,1)S(1)}, bf16[96,1536]{1,0:T(8,128)(2,1)S(1)}, u32[]{:S(2)}, u32[]{:S(2)}) collective-permute-start(bf16[96,1536]{1,0:T(8,128)(2,1)S(1)} %copy-done.26), channel_id=1, source_target_pairs={{0,1},{3,2},{4,5},{7,6},{8,9},{11,10},{12,13},{15,14},{16,17},{19,... | collective-permute-start | bytes 884744 | tf_op jit(solution)/shard_map/ppermute | solution.py:514
  284.4 12.8 %collective-permute-start.53 = (bf16[104,1536]{1,0:T(8,128)(2,1)S(1)}, bf16[104,1536]{1,0:T(8,128)(2,1)S(1)}, u32[]{:S(2)}, u32[]{:S(2)}) collective-permute-start(bf16[104,1536]{1,0:T(8,128)(2,1)S(1)} %pad_maximum_fusion.7), channel_id=1, source_target_pairs={{0,1},{3,2},{4,5},{7,6},{8,9},{11,10},{12,13},{15,14},{16,17},{19,... | collective-permute-start | bytes 958472 | tf_op jit(solution)/shard_map/ppermute | solution.py:514
  286.0 12.0 %collective-permute-start.61 = (bf16[96,768]{1,0:T(8,128)(2,1)S(1)}, bf16[96,768]{1,0:T(8,128)(2,1)S(1)}, u32[]{:S(2)}, u32[]{:S(2)}) collective-permute-start(bf16[96,768]{1,0:T(8,128)(2,1)S(1)} %get-tuple-element.247), channel_id=1, source_target_pairs={{0,8},{4,12},{8,0},{12,4},{16,24},{20,28},{24,16},{28,20},{1,9},{5... | collective-permute-start | bytes 442376 | tf_op jit(solution)/shard_map/ppermute | solution.py:510
  287.5 10.5 %collective-permute-start.62 = (bf16[96,768]{1,0:T(8,128)(2,1)S(1)}, bf16[96,768]{1,0:T(8,128)(2,1)S(1)}, u32[]{:S(2)}, u32[]{:S(2)}) collective-permute-start(bf16[96,768]{1,0:T(8,128)(2,1)S(1)} %get-tuple-element.249), channel_id=1, source_target_pairs={{0,16},{4,20},{8,24},{12,28},{16,0},{20,4},{24,8},{28,12},{1,17},{... | collective-permute-start | bytes 442376 | tf_op jit(solution)/shard_map/ppermute | solution.py:510
  288.2 9.8 %collective-permute-start.63 = (bf16[96,768]{1,0:T(8,128)(2,1)S(1)}, bf16[96,768]{1,0:T(8,128)(2,1)S(1)}, u32[]{:S(2)}, u32[]{:S(2)}) collective-permute-start(bf16[96,768]{1,0:T(8,128)(2,1)S(1)} %get-tuple-element.248), channel_id=1, source_target_pairs={{0,24},{4,28},{8,16},{12,20},{16,8},{20,12},{24,0},{28,4},{1,25},{... | collective-permute-start | bytes 442376 | tf_op jit(solution)/shard_map/ppermute | solution.py:510
  289.7 9.5 %collective-permute-start.58 = (bf16[96,1536]{1,0:T(8,128)(2,1)S(1)}, bf16[96,1536]{1,0:T(8,128)(2,1)S(1)}, u32[]{:S(2)}, u32[]{:S(2)}) collective-permute-start(bf16[96,1536]{1,0:T(8,128)(2,1)S(1)} %add_convert_fusion.9), channel_id=1, source_target_pairs={{1,2},{2,1},{5,6},{6,5},{9,10},{10,9},{13,14},{14,13},{17,18},{18,... | collective-permute-start | bytes 884744 | tf_op jit(solution)/shard_map/ppermute | solution.py:514
  297.3 3.3 collective-permute-start.54
  299.3 28.1 %collective-permute-start.59 = (bf16[96,1536]{1,0:T(8,128)(2,1)S(1)}, bf16[96,1536]{1,0:T(8,128)(2,1)S(1)}, u32[]{:S(2)}, u32[]{:S(2)}) collective-permute-start(bf16[96,1536]{1,0:T(8,128)(2,1)S(1)} %add_convert_fusion.8), channel_id=1, source_target_pairs={{1,0},{2,3},{5,4},{6,7},{9,8},{10,11},{13,12},{14,15},{17,16},{18,... | collective-permute-start | bytes 884744 | tf_op jit(solution)/shard_map/ppermute | solution.py:514
  300.7 36.6 %collective-permute-start.55 = (bf16[104,1536]{1,0:T(8,128)(2,1)S(1)}, bf16[104,1536]{1,0:T(8,128)(2,1)S(1)}, u32[]{:S(2)}, u32[]{:S(2)}) collective-permute-start(bf16[104,1536]{1,0:T(8,128)(2,1)S(1)} %add_convert_fusion.6), channel_id=1, source_target_pairs={{1,0},{2,3},{5,4},{6,7},{9,8},{10,11},{13,12},{14,15},{17,16},{18,... | collective-permute-start | bytes 958472 | tf_op jit(solution)/shard_map/ppermute | solution.py:514
  (92 other events, 247.9 us)
Sparse Core Ops, SparseCore 0:
  38.5 35.1 all-gather.3
  75.8 21.1 all-gather.5
  166.5 55.6 all-reduce.9
  258.2 69.3 all-reduce.11
where the time goes:
time: 356 us; the launch traced here: 350 us
  Pallas kernels  114 us (32%)
  waiting for transfers between devices  83.8 us (24%)
  starting transfers between devices  55.2 us (16%)
  other arithmetic  44.4 us (12%)
  local copies, waits for them, and re-layouts  37.2 us (10%)
  between operations  15.2 us (4%)
    pallas_call x14, Pallas kernels, call(): pl.pallas_call(kernel, out_shape=[jax.ShapeDtypeStruct(s, d) for s, d in...  114 us
    ppermute x58, starting transfers between devices, swap(): return lax.ppermute(array, 'fsdp', [(i, i ^ mask) for i in range(8)])  46.1 us
    ppermute x6, waiting for transfers between devices, along_rep(): return lax.ppermute(array, 'rep', pairs)  41.4 us
    ppermute x58, waiting for transfers between devices, swap(): return lax.ppermute(array, 'fsdp', [(i, i ^ mask) for i in range(8)])  33.4 us
    unnamed x183, local copies, waits for them, and re-layouts  23.4 us
    convert_element_type x16, other arithmetic, add(): return out.astype(BF)  17.9 us
    all_gather x1, waiting for transfers between devices, planned(): grad_pair = lax.all_gather(grad_v, 'fsdp', axis_index_groups=pairs)  8.88 us
    ppermute x6, starting transfers between devices, along_rep(): return lax.ppermute(array, 'rep', pairs)  8.7 us
  transfers between devices with their start and end apart: 68, of which 18 were waited for; matrix products, arithmetic and copies ran while one was open for 17% of the time, Pallas kernels for 32%

commit v1 on v0

--- a/solution.py
+++ b/solution.py
@@ -15,7 +15,7 @@
 VMEM_LIMIT = 58 * 1024 * 1024
 
 ITEM = 256
-SCALE = 0.2
+SCALE = 0.3
 TEXT_AT = 208
 
 
@@ -834,7 +834,6 @@
 
     a_first, b_first = begin(a_keep, a_got, 2), begin(b_keep, b_got, 4)
     a_there, b_there = swap(a_first, 2), swap(b_first, 4)
-    branch_t = [branch_sum] + [swap(branch_sum[s], 2 * s) for s in (1, 2, 3)]
     gtok, sums_one = call(
         functools.partial(last_kernel, attn_slots),
         [((total, width), F32), ((8, width), F32)],
@@ -843,7 +842,7 @@
         attn_arrays + [a_first, b_first, vu_both, vd_sum],
         us=12,
     )
-    t = tick(t, [sums_one, a_there, b_there, *branch_t[1:]])
+    t = tick(t, [sums_one, a_there, b_there])
 
     a_there, b_there = gate([a_there, b_there], [t])
     a_next, b_next = add(a_keep[2], a_got[2], a_there[1]), add(b_keep[1], b_got[1], b_there[1])
@@ -880,7 +879,8 @@
     own_sums = jnp.pad(own_sums, (0, 8 * 2 * width - own_sums.shape[0])).reshape(8, 2 * width)
     ga, gb = rep_sum(jnp.concatenate([ga, own_sums.astype(BF)], axis=0)), rep_sum(gb)
     last_sums = [ga, gb]
-    tu_keep, tu_send, td = gate([tu_keep, tu_send, td], plane_sums)
+    tu_keep, tu_send, td, branch_sum, branch_back = gate([tu_keep, tu_send, td, branch_sum, branch_back], plane_sums)
+    branch_t = [branch_sum] + [swap(branch_sum[s], 2 * s) for s in (1, 2, 3)]
     tu_got = swap(tu_send, 1)
     tu_wide = jnp.where(
         core == 0,

time: 356 us -> 348 us (0.978)
  waiting for transfers between devices: 83.8 us -> 76.5 us
  other arithmetic: 44.4 us -> 39.1 us
  local copies, waits for them, and re-layouts: 37.2 us -> 41 us
    unnamed x183 -> x193, local copies, waits for them, and re-layouts: 23.4 us -> 25.8 us
  transfers between devices with their start and end apart: 68 -> 68, of which waited for: 18 -> 21; matrix products, arithmetic and copies ran while one was open for 17% -> 15% of each run, Pallas kernels for 32% -> 33%
where the time goes in v1:
time: 348 us; the launch traced here: 342 us
  Pallas kernels  114 us (33%)
  waiting for transfers between devices  76.5 us (22%)
  starting transfers between devices  56 us (16%)
  local copies, waits for them, and re-layouts  41 us (12%)
  other arithmetic  39.1 us (11%)
  between operations  15.2 us (4%)
    pallas_call x14, Pallas kernels, call(): pl.pallas_call(kernel, out_shape=[jax.ShapeDtypeStruct(s, d) for s, d in...  114 us
    ppermute x58, starting transfers between devices, swap(): return lax.ppermute(array, 'fsdp', [(i, i ^ mask) for i in range(8)])  45 us
    ppermute x6, waiting for transfers between devices, along_rep(): return lax.ppermute(array, 'rep', pairs)  40.2 us
    ppermute x58, waiting for transfers between devices, swap(): return lax.ppermute(array, 'fsdp', [(i, i ^ mask) for i in range(8)])  30.1 us
    unnamed x193, local copies, waits for them, and re-layouts  25.8 us
    convert_element_type x16, other arithmetic, add(): return out.astype(BF)  17.4 us
    ppermute x6, starting transfers between devices, along_rep(): return lax.ppermute(array, 'rep', pairs)  10.8 us
  transfers between devices with their start and end apart: 68, of which 21 were waited for; matrix products, arithmetic and copies ran while one was open for 15% of the time, Pallas kernels for 33%

profile of v1, /device:TPU:0, one launch (start us, length us, event | category | flops | bytes accessed | tf_op | source)
XLA Modules:
  0.0 342.3 jit_solution(1391510987697115545)
XLA Ops:
  7.3 3.0 collective-permute-start.4
  10.3 1.5 collective-permute-start.5
  11.8 1.5 stack.97
  14.6 2.9 collective-permute-start.2
  17.5 2.1 copy.119.tokens
  21.1 4.3 %shard_map.365 = (bf16[512,768]{1,0:T(8,128)(2,1)}, bf16[512,768]{1,0:T(8,128)(2,1)}, bf16[416,768]{1,0:T(8,128)(2,1)}, bf16[80,768]{1,0:T(8,128)(2,1)}, f32[2,7...) custom-call(s32[4]{0:T(128)} %pad_add_fusion.info, ...), custom_call_target="tpu_custom_call" | custom-call | flops 1650000000 | bytes 1500000 | tf_op jit(solution)/shard_map/pallas_call | solution.py:498
  30.9 4.7 %shard_map.368 = (bf16[512,768]{1,0:T(8,128)(2,1)}, f32[16,768]{1,0:T(8,128)}, f32[1,1536]{1,0:T(1,128)}) custom-call(s32[4]{0:T(128)} %pad_add_fusion.info, bf16[512,768]{1,0:T(8,128)(2,1)} %get-tuple-element.127.refs_2_.tok, f32[512,1]{1,0:T(8,128)} %bitcast.127, bf16[4,16,128]{2,1,0:T(8,128)(2,1)} %shard_map.366.even, bf16[4,16,128]{2,1,0:T(8,128)(2,1)} %copy-done.82, ...), custom_call_target="tpu_custom_call" | custom-call | flops 1650000000 | bytes 1500000 | tf_op jit(solution)/shard_map/pallas_call | solution.py:498
  35.7 1.4 collective-permute-done.6.refs_0_
  39.5 1.6 collective-permute-start.18
  41.8 8.0 %shard_map.370.refs_1_.qkv = bf16[512,2304]{1,0:T(8,128)(2,1)} custom-call(s32[4]{0:T(128)} %pad_add_fusion.info, bf16[512,768]{1,0:T(8,128)(2,1)} %get-tuple-element.131.refs_5_.n1.left, f32[16,768]{1,0:T(8,128)} %get-tuple-element.130.vec, bf16[96,2304]{1,0:T(8,128)(2,1)} %refs_0_.3, bf16[96,2304]{1,0:T(8,128)(2,1)} %copy-done.79, ...), custom_call_target="tpu_custom_call" | custom-call | flops 2640000000 | bytes 2400000 | tf_op jit(solution)/shard_map/pallas_call | solution.py:498
  54.7 1.5 collective-permute-start.17
  56.2 11.4 %shard_map.372 = (bf16[12,512,256]{2,1,0:T(8,128)(2,1)}, bf16[512,768]{1,0:T(8,128)(2,1)}) custom-call(s32[4]{0:T(128)} %pad_add_fusion.info, bf16[512,2304]{1,0:T(8,128)(2,1)} %shard_map.370.refs_1_.qkv, f32[8,128]{1,0:T(8,128)} %shard_map.371.refs_0_.refs_4_), custom_call_target="tpu_custom_call" | custom-call | flops 3300000000 | bytes 3000000 | tf_op jit(solution)/shard_map/pallas_call | solution.py:498
  67.6 4.5 %collective-permute-done.17.refs_5_.refs_3_ = bf16[176,768]{1,0:T(8,128)(2,1)S(1)} collective-permute-done((bf16[176,768]{1,0:T(8,128)(2,1)S(1)}, bf16[176,768]{1,0:T(8,128)(2,1)S(1)}, u32[]{:S(2)}, u32[]{:S(2)}) %collective-permute-start.17) | collective-permute-done | bytes 270368 | tf_op jit(solution)/shard_map/ppermute | solution.py:510
  72.1 5.8 %collective-permute-done.14.refs_2_.refs_0_ = bf16[2,96,1536]{2,1,0:T(8,128)(2,1)S(1)} collective-permute-done((bf16[2,96,1536]{2,1,0:T(8,128)(2,1)S(1)}, bf16[2,96,1536]{2,1,0:T(8,128)(2,1)S(1)}, u32[]{:S(2)}, u32[]{:S(2)}) %collective-permute-start.14) | collective-permute-done | bytes 589856 | tf_op jit(solution)/shard_map/ppermute | solution.py:510
  80.0 1.2 pad_maximum_fusion.1.refs_6_
  81.8 1.6 collective-permute-start.19
  83.4 4.5 %shard_map.375 = (f32[512,768]{1,0:T(8,128)}, bf16[80,768]{1,0:T(8,128)(2,1)}, bf16[208,768]{1,0:T(8,128)(2,1)}, bf16[208,768]{1,0:T(8,128)(2,1)}) custom-call(s32[4]{0:T(128)} %pad_add_fusion.info, bf16[512,768]{1,0:T(8,128)(2,1)} %get-tuple-element.127.refs_2_.tok, f32[512,1]{1,0:T(8,128)} %bitcast.128, f32[16,768]{1,0:T(8,128)} %get-tuple-element.130.vec, ...), custom_call_target="tpu_custom_call" | custom-call | flops 1650000000 | bytes 1500000 | tf_op jit(solution)/shard_map/pallas_call | solution.py:498
  87.9 6.1 %all-gather.6.cloned.1.call-done = bf16[832,768]{1,0:T(8,128)(2,1)} async-done(((bf16[416,768]{1,0:T(8,128)(2,1)}), bf16[832,768]{1,0:T(8,128)(2,1)}) %all-gather.6.cloned.1.call-update) | async-done | bytes 1277968 | tf_op jit(solution)/shard_map/all_gather | solution.py:631
  95.2 2.2 shard_map.379.refs_8_
  97.7 1.7 collective-permute-start.23
  99.4 1.5 collective-permute-start.24
  101.2 10.0 %shard_map.380 = (f32[416,768]{1,0:T(8,128)}, f32[416,768]{1,0:T(8,128)}, bf16[416,1536]{1,0:T(8,128)(2,1)}, bf16[416,1536]{1,0:T(8,128)(2,1)}) custom-call(s32[4]{0:T(128)} %pad_add_fusion.info, bf16[416,768]{1,0:T(8,128)(2,1)} %get-tuple-element.150.grad, f32[1,1536]{1,0:T(1,128)} %get-tuple-element.151.up_bias, ...), custom_call_target="tpu_custom_call" | custom-call | flops 2969999872 | bytes 2699999 | tf_op jit(solution)/shard_map/pallas_call | solution.py:498
  111.3 2.2 collective-permute-done.25.refs_4_.refs_3_
  118.5 6.3 %shard_map.383 = (bf16[4,80,768]{2,1,0:T(8,128)(2,1)}, bf16[4,80,768]{2,1,0:T(8,128)(2,1)}, bf16[4,80,768]{2,1,0:T(8,128)(2,1)}, bf16[4,80,768]{2,1,0:T(8,128)(2...) custom-call(s32[4]{0:T(128)} %pad_add_fusion.info, ...), custom_call_target="tpu_custom_call" | custom-call | flops 1980000000 | bytes 1799999 | tf_op jit(solution)/shard_map/pallas_call | solution.py:498
  124.8 1.8 collective-permute-done.28.refs_3_.refs_2_
  127.3 2.1 collective-permute-done.29
  130.7 2.4 collective-permute-start.32
  133.1 10.3 %shard_map.387 = (bf16[416,768]{1,0:T(8,128)(2,1)}, bf16[416,768]{1,0:T(8,128)(2,1)}, bf16[416,1536]{1,0:T(8,128)(2,1)}, bf16[416,1536]{1,0:T(8,128)(2,1)}) custom-call(s32[4]{0:T(128)} %pad_add_fusion.info, bf16[2,416,768]{2,1,0:T(8,128)(2,1)} %bitcast.119, f32[1,1536]{1,0:T(1,128)} %get-tuple-element.151.up_bias, ...), custom_call_target="tpu_custom_call" | custom-call | flops 2969999872 | bytes 2699999 | tf_op jit(solution)/shard_map/pallas_call | solution.py:498
  144.8 12.3 %shard_map.389 = (bf16[4,96,1536]{2,1,0:T(8,128)(2,1)}, bf16[4,96,1536]{2,1,0:T(8,128)(2,1)}, bf16[2,384,768]{2,1,0:T(8,128)(2,1)}, bf16[2,384,768]{2,1,0:T(8,128)(2,1)}, f32[1,1536]{1,0:T(1,128)}) custom-call(s32[4]{0:T(128)} %pad_add_fusion.info, bf16[208,768]{1,0:T(8,128)(2,1)} %get-tuple-element.161.refs_0_, ...), custom_call_target="tpu_custom_call" | custom-call | flops 3960000000 | bytes 3599999 | tf_op jit(solution)/shard_map/pallas_call | solution.py:498
  157.2 2.9 collective-permute-done.33.refs_2_.refs_4_
  162.0 2.0 collective-permute-done.34
  164.0 1.6 fusion.3.refs_0_
  167.3 1.5 collective-permute-start.37
  168.8 18.2 %shard_map.393 = (f32[512,768]{1,0:T(8,128)}, bf16[512,768]{1,0:T(8,128)(2,1)}, bf16[512,2304]{1,0:T(8,128)(2,1)}, f32[8,768]{1,0:T(8,128)}) custom-call(s32[4]{0:T(128)} %pad_add_fusion.info, f32[416,768]{1,0:T(8,128)} %get-tuple-element.170.refs_1_.gn2v, bf16[416,768]{1,0:T(8,128)(2,1)} %get-tuple-element.193.gn2x, bf16[4,80,768]{2,1,0:T(8,128)(2,1)} %copy-done.39, ...), custom_call_target="tpu_custom_call" | custom-call | flops 5939999744 | bytes 5399999 | tf_op jit(solution)/shard_map/pallas_call | solution.py:498
  190.8 5.3 %shard_map.395 = (bf16[4,96,1536]{2,1,0:T(8,128)(2,1)}, bf16[4,96,1536]{2,1,0:T(8,128)(2,1)}) custom-call(s32[4]{0:T(128)} %pad_add_fusion.info, bf16[512,768]{1,0:T(8,128)(2,1)} %get-tuple-element.131.refs_5_.n1.left, bf16[512,2304]{1,0:T(8,128)(2,1)} %get-tuple-element.200.refs_1_.refs_0_.refs_2_.stacked, f32[8,128]{1,0:T(8,128)} %shard_map.394.refs_1_.refs_4_.refs_0_), custom_call_target="tpu_custom_call" | custom-call | flops 1650000000 | bytes 1500000 | tf_op jit(solution)/shard_map/pallas_call | solution.py:498
  196.2 1.9 collective-permute-done.40.refs_2_.refs_1_
  200.1 1.9 add_convert_fusion.4.refs_2_
  202.0 2.4 fusion.2.refs_13_
  205.2 5.3 %shard_map.399 = (bf16[4,96,1536]{2,1,0:T(8,128)(2,1)}, bf16[4,96,1536]{2,1,0:T(8,128)(2,1)}) custom-call(s32[4]{0:T(128)} %pad_add_fusion.info, bf16[512,768]{1,0:T(8,128)(2,1)} %get-tuple-element.131.refs_5_.n1.left, bf16[512,768]{1,0:T(8,128)(2,1)} %get-tuple-element.139.refs_1_.ctx.refs_0_, bf16[512,768]{1,0:T(8,128)(2,1)} %get-tuple-element.208.refs_1_, ...), custom_call_target="tpu_custom_call" | custom-call | flops 1650000000 | bytes 1500000 | tf_op jit(solution)/shard_map/pallas_call | solution.py:498
  214.6 1.5 collective-permute-start.43
  219.9 11.5 %shard_map.402 = (f32[512,768]{1,0:T(8,128)}, f32[8,768]{1,0:T(8,128)}) custom-call(s32[4]{0:T(128)} %pad_add_fusion.info, bf16[512,2304]{1,0:T(8,128)(2,1)} %get-tuple-element.200.refs_1_.refs_0_.refs_2_.stacked, f32[512,768]{1,0:T(8,128)} %get-tuple-element.216.gh1, bf16[512,768]{1,0:T(8,128)(2,1)} %get-tuple-element.127.refs_2_.tok, f32[512,1]{1,0:T(8,128)} %bitcast.129, ...), custom_call_target="tpu_custom_call" | custom-call | flops 3960000000 | bytes 3599999 | tf_op jit(solution)/shard_map/pallas_call | solution.py:498
  231.5 1.4 collective-permute-done.45.refs_3_.refs_1_
  233.8 1.9 fusion.11.refs_1_
  235.7 1.8 fusion.12.refs_2_
  239.3 2.4 slice.331
  244.1 1.4 slice.345
  245.5 1.7 slice.346
  248.3 1.4 collective-permute-start.47
  251.5 1.7 pad_maximum_fusion
  254.9 2.6 collective-permute-done.47
  257.6 1.3 fusion.5.refs_6_
  258.9 3.6 %collective-permute-start.57 = (bf16[96,1536]{1,0:T(8,128)(2,1)S(1)}, bf16[96,1536]{1,0:T(8,128)(2,1)S(1)}, u32[]{:S(2)}, u32[]{:S(2)}) collective-permute-start(bf16[96,1536]{1,0:T(8,128)(2,1)S(1)} %fusion.5.refs_6_), channel_id=1, source_target_pairs={{0,1},{3,2},{4,5},{7,6},{8,9},{11,10},{12,13},{15,14},{16,17},{19,... | collective-permute-start | bytes 884744 | tf_op jit(solution)/shard_map/ppermute | solution.py:514
  262.5 1.9 fusion.6.refs_5_
  264.6 1.2 copy-done.40
  265.8 1.2 convert_add_fusion
  268.1 1.4 collective-permute-start.48
  273.8 3.2 collective-permute-start.54
  277.3 1.8 pad_maximum_fusion.3
  280.8 2.1 collective-permute-start.63
  283.7 4.0 %collective-permute-done.54 = bf16[104,1536]{1,0:T(8,128)(2,1)S(1)} collective-permute-done((bf16[104,1536]{1,0:T(8,128)(2,1)S(1)}, bf16[104,1536]{1,0:T(8,128)(2,1)S(1)}, u32[]{:S(2)}, u32[]{:S(2)}) %collective-permute-start.54) | collective-permute-done | bytes 319520 | tf_op jit(solution)/shard_map/ppermute | solution.py:514
  289.8 1.3 collective-permute-start.59
  291.2 1.3 collective-permute-start.56
  292.5 28.4 %collective-permute-done.59 = bf16[96,1536]{1,0:T(8,128)(2,1)S(1)} collective-permute-done((bf16[96,1536]{1,0:T(8,128)(2,1)S(1)}, bf16[96,1536]{1,0:T(8,128)(2,1)S(1)}, u32[]{:S(2)}, u32[]{:S(2)}) %collective-permute-start.59) | collective-permute-done | bytes 294944 | tf_op jit(solution)/shard_map/ppermute | solution.py:514
  321.7 7.8 %collective-permute-done.56 = bf16[104,1536]{1,0:T(8,128)(2,1)S(1)} collective-permute-done((bf16[104,1536]{1,0:T(8,128)(2,1)S(1)}, bf16[104,1536]{1,0:T(8,128)(2,1)S(1)}, u32[]{:S(2)}, u32[]{:S(2)}) %collective-permute-start.56) | collective-permute-done | bytes 319520 | tf_op jit(solution)/shard_map/ppermute | solution.py:514
  (400 shorter events, 73.7 us)
Async XLA Ops:
  7.2 76.2 %all-gather.4.cloned.1.call-start = ((), (), s32[]{:S(2)}) async-start(), calls=%async_computation | async-start | bytes 1327104 | tf_op jit(solution)/shard_map/all_gather | solution.py:629
  7.3 18.7 %collective-permute-start.4 = (bf16[96,2304]{1,0:T(8,128)(2,1)}, bf16[96,2304]{1,0:T(8,128)(2,1)S(1)}, u32[]{:S(2)}, u32[]{:S(2)}) collective-permute-start(bf16[96,2304]{1,0:T(8,128)(2,1)} %refs_0_.3), channel_id=1, source_target_pairs={{0,8},{4,12},{8,0},{12,4},{16,24},{20,28},{24,16},{28,20},{1,9},{5... | collective-permute-start | bytes 1327112 | tf_op jit(solution)/shard_map/ppermute | solution.py:510
  10.3 15.2 %collective-permute-start.5 = (bf16[96,2304]{1,0:T(8,128)(2,1)}, bf16[96,2304]{1,0:T(8,128)(2,1)S(1)}, u32[]{:S(2)}, u32[]{:S(2)}) collective-permute-start(bf16[96,2304]{1,0:T(8,128)(2,1)} %refs_0_.3), channel_id=1, source_target_pairs={{0,16},{4,20},{8,24},{12,28},{16,0},{20,4},{24,8},{28,12},{1,17},{... | collective-permute-start | bytes 1327112 | tf_op jit(solution)/shard_map/ppermute | solution.py:510
  14.0 11.4 %collective-permute-start = (bf16[1,16,128]{2,1,0:T(8,128)(2,1)S(1)}, bf16[1,16,128]{2,1,0:T(8,128)(2,1)S(1)}, u32[]{:S(2)}, u32[]{:S(2)}) collective-permute-start(bf16[1,16,128]{2,1,0:T(8,128)(2,1)S(1)} %pad_bitcast_fusion), channel_id=1, source_target_pairs={{0,8},{4,12},{8,0},{12,4},{16,24},{20,28},{24,16},{28,20},{1,9},{5... | collective-permute-start | bytes 12296 | tf_op jit(solution)/shard_map/ppermute | solution.py:510
  14.6 11.5 %collective-permute-start.1 = (bf16[1,16,128]{2,1,0:T(8,128)(2,1)S(1)}, bf16[1,16,128]{2,1,0:T(8,128)(2,1)S(1)}, u32[]{:S(2)}, u32[]{:S(2)}) collective-permute-start(bf16[1,16,128]{2,1,0:T(8,128)(2,1)S(1)} %pad_bitcast_fusion), channel_id=1, source_target_pairs={{0,16},{4,20},{8,24},{12,28},{16,0},{20,4},{24,8},{28,12},{1,17},{... | collective-permute-start | bytes 12296 | tf_op jit(solution)/shard_map/ppermute | solution.py:510
  14.6 11.5 %collective-permute-start.2 = (bf16[1,16,128]{2,1,0:T(8,128)(2,1)S(1)}, bf16[1,16,128]{2,1,0:T(8,128)(2,1)S(1)}, u32[]{:S(2)}, u32[]{:S(2)}) collective-permute-start(bf16[1,16,128]{2,1,0:T(8,128)(2,1)S(1)} %pad_bitcast_fusion), channel_id=1, source_target_pairs={{0,24},{4,28},{8,16},{12,20},{16,8},{20,12},{24,0},{28,4},{1,25},{... | collective-permute-start | bytes 12296 | tf_op jit(solution)/shard_map/ppermute | solution.py:510
  25.4 10.2 %collective-permute-start.8 = (bf16[96,2304]{1,0:T(8,128)(2,1)S(1)}, bf16[96,2304]{1,0:T(8,128)(2,1)S(1)}, u32[]{:S(2)}, u32[]{:S(2)}) collective-permute-start(bf16[96,2304]{1,0:T(8,128)(2,1)S(1)} %copy-done.90), channel_id=1, source_target_pairs={{0,4},{4,0},{8,12},{12,8},{16,20},{20,16},{24,28},{28,24},{1,5},{5... | collective-permute-start | bytes 1327112 | tf_op jit(solution)/shard_map/ppermute | solution.py:510
  25.5 11.8 %collective-permute-start.10 = (bf16[96,2304]{1,0:T(8,128)(2,1)S(1)}, bf16[96,2304]{1,0:T(8,128)(2,1)S(1)}, u32[]{:S(2)}, u32[]{:S(2)}) collective-permute-start(bf16[96,2304]{1,0:T(8,128)(2,1)S(1)} %collective-permute-done.5.refs_2_), channel_id=1, source_target_pairs={{0,4},{4,0},{8,12},{12,8},{16,20},{20,16},{24,28},{28,24},{1,5},{5... | collective-permute-start | bytes 1327112 | tf_op jit(solution)/shard_map/ppermute | solution.py:510
  26.0 11.3 %collective-permute-start.9 = (bf16[96,2304]{1,0:T(8,128)(2,1)S(1)}, bf16[96,2304]{1,0:T(8,128)(2,1)S(1)}, u32[]{:S(2)}, u32[]{:S(2)}) collective-permute-start(bf16[96,2304]{1,0:T(8,128)(2,1)S(1)} %collective-permute-done.4.refs_1_), channel_id=1, source_target_pairs={{0,4},{4,0},{8,12},{12,8},{16,20},{20,16},{24,28},{28,24},{1,5},{5... | collective-permute-start | bytes 1327112 | tf_op jit(solution)/shard_map/ppermute | solution.py:510
  29.4 7.7 %collective-permute-start.6 = (bf16[48,2304]{1,0:T(8,128)(2,1)}, bf16[48,2304]{1,0:T(8,128)(2,1)S(1)}, u32[]{:S(2)}, u32[]{:S(2)}) collective-permute-start(bf16[48,2304]{1,0:T(8,128)(2,1)} %get-tuple-element.129.refs_0_), channel_id=1, source_target_pairs={{0,16},{4,20},{8,24},{12,28},{16,0},{20,4},{24,8},{28,12},{1,17},{... | collective-permute-start | bytes 663560 | tf_op jit(solution)/shard_map/ppermute | solution.py:510
  29.9 7.4 %collective-permute-start.7 = (bf16[48,2304]{1,0:T(8,128)(2,1)}, bf16[48,2304]{1,0:T(8,128)(2,1)S(1)}, u32[]{:S(2)}, u32[]{:S(2)}) collective-permute-start(bf16[48,2304]{1,0:T(8,128)(2,1)} %get-tuple-element.132), channel_id=1, source_target_pairs={{0,8},{4,12},{8,0},{12,4},{16,24},{20,28},{24,16},{28,20},{1,9},{5... | collective-permute-start | bytes 663560 | tf_op jit(solution)/shard_map/ppermute | solution.py:510
  38.3 55.7 %all-gather.6.cloned.1.call-start = ((), (), s32[]{:S(2)}) async-start(), calls=%async_computation.1 | async-start | bytes 1916928 | tf_op jit(solution)/shard_map/all_gather | solution.py:631
  38.4 2.6 collective-permute-start.11
  39.0 10.8 %collective-permute-start.13 = (bf16[96,1536]{1,0:T(8,128)(2,1)}, bf16[96,1536]{1,0:T(8,128)(2,1)S(1)}, u32[]{:S(2)}, u32[]{:S(2)}) collective-permute-start(bf16[96,1536]{1,0:T(8,128)(2,1)} %get-tuple-element.138), channel_id=1, source_target_pairs={{0,8},{4,12},{8,0},{12,4},{16,24},{20,28},{24,16},{28,20},{1,9},{5... | collective-permute-start | bytes 884744 | tf_op jit(solution)/shard_map/ppermute | solution.py:510
  39.5 32.6 %collective-permute-start.18 = (bf16[384,768]{1,0:T(8,128)(2,1)}, bf16[384,768]{1,0:T(8,128)(2,1)S(1)}, u32[]{:S(2)}, u32[]{:S(2)}) collective-permute-start(bf16[384,768]{1,0:T(8,128)(2,1)} %get-tuple-element.148), channel_id=1, source_target_pairs={{0,16},{4,20},{8,24},{12,28},{16,0},{20,4},{24,8},{28,12},{1,17},{... | collective-permute-start | bytes 1769480 | tf_op jit(solution)/shard_map/ppermute | solution.py:510
  52.5 25.4 %collective-permute-start.14 = (bf16[2,96,1536]{2,1,0:T(8,128)(2,1)S(1)}, bf16[2,96,1536]{2,1,0:T(8,128)(2,1)S(1)}, u32[]{:S(2)}, u32[]{:S(2)}) collective-permute-start(bf16[2,96,1536]{2,1,0:T(8,128)(2,1)S(1)} %pad_maximum_fusion.4.refs_2_), channel_id=1, source_target_pairs={{0,16},{4,20},{8,24},{12,28},{16,0},{20,4},{24,8},{28,12},{1,17},{... | collective-permute-start | bytes 1769480 | tf_op jit(solution)/shard_map/ppermute | solution.py:510
  53.4 24.5 %collective-permute-start.15 = (bf16[2,96,1536]{2,1,0:T(8,128)(2,1)S(1)}, bf16[2,96,1536]{2,1,0:T(8,128)(2,1)S(1)}, u32[]{:S(2)}, u32[]{:S(2)}) collective-permute-start(bf16[2,96,1536]{2,1,0:T(8,128)(2,1)S(1)} %pad_maximum_fusion.4.refs_2_), channel_id=1, source_target_pairs={{0,4},{4,0},{8,12},{12,8},{16,20},{20,16},{24,28},{28,24},{1,5},{5... | collective-permute-start | bytes 1769480 | tf_op jit(solution)/shard_map/ppermute | solution.py:510
  53.4 211.0 %all-reduce.10.cloned.1.call-start = ((), (), s32[]{:S(2)}) async-start(), calls=%async_computation.2 | async-start | bytes 2359296 | tf_op jit(solution)/shard_map/psum | solution.py:749
  53.5 14.1 %collective-permute-start.16 = (bf16[176,768]{1,0:T(8,128)(2,1)S(1)}, bf16[176,768]{1,0:T(8,128)(2,1)S(1)}, u32[]{:S(2)}, u32[]{:S(2)}) collective-permute-start(bf16[176,768]{1,0:T(8,128)(2,1)S(1)} %copy-done.70), channel_id=1, source_target_pairs={{0,8},{4,12},{8,0},{12,4},{16,24},{20,28},{24,16},{28,20},{1,9},{5... | collective-permute-start | bytes 811016 | tf_op jit(solution)/shard_map/ppermute | solution.py:510
  54.7 17.4 %collective-permute-start.17 = (bf16[176,768]{1,0:T(8,128)(2,1)S(1)}, bf16[176,768]{1,0:T(8,128)(2,1)S(1)}, u32[]{:S(2)}, u32[]{:S(2)}) collective-permute-start(bf16[176,768]{1,0:T(8,128)(2,1)S(1)} %copy-done.71), channel_id=1, source_target_pairs={{0,24},{4,28},{8,16},{12,20},{16,8},{20,12},{24,0},{28,4},{1,25},{... | collective-permute-start | bytes 811016 | tf_op jit(solution)/shard_map/ppermute | solution.py:510
  81.2 12.8 %collective-permute-start.21 = (bf16[2,384,768]{2,1,0:T(8,128)(2,1)S(1)}, bf16[2,384,768]{2,1,0:T(8,128)(2,1)S(1)}, u32[]{:S(2)}, u32[]{:S(2)}) collective-permute-start(bf16[2,384,768]{2,1,0:T(8,128)(2,1)S(1)} %pad_maximum_fusion.1.refs_6_), channel_id=1, source_target_pairs={{0,4},{4,0},{8,12},{12,8},{16,20},{20,16},{24,28},{28,24},{1,5},{5... | collective-permute-start | bytes 3538952 | tf_op jit(solution)/shard_map/ppermute | solution.py:510
  81.3 12.7 %collective-permute-start.20 = (bf16[2,96,1536]{2,1,0:T(8,128)(2,1)S(1)}, bf16[2,96,1536]{2,1,0:T(8,128)(2,1)}, u32[]{:S(2)}, u32[]{:S(2)}) collective-permute-start(bf16[2,96,1536]{2,1,0:T(8,128)(2,1)S(1)} %copy-done.37), channel_id=1, source_target_pairs={{0,4},{4,0},{8,12},{12,8},{16,20},{20,16},{24,28},{28,24},{1,5},{5... | collective-permute-start | bytes 1769480 | tf_op jit(solution)/shard_map/ppermute | solution.py:510
  81.8 12.2 %collective-permute-start.19 = (bf16[176,768]{1,0:T(8,128)(2,1)}, bf16[176,768]{1,0:T(8,128)(2,1)S(1)}, u32[]{:S(2)}, u32[]{:S(2)}) collective-permute-start(bf16[176,768]{1,0:T(8,128)(2,1)} %get-tuple-element.154), channel_id=1, source_target_pairs={{0,16},{4,20},{8,24},{12,28},{16,0},{20,4},{24,8},{28,12},{1,17},{... | collective-permute-start | bytes 811016 | tf_op jit(solution)/shard_map/ppermute | solution.py:510
  97.3 16.1 %collective-permute-start.22 = (bf16[512,768]{1,0:T(8,128)(2,1)}, bf16[512,768]{1,0:T(8,128)(2,1)S(1)}, u32[]{:S(2)}, u32[]{:S(2)}) collective-permute-start(bf16[512,768]{1,0:T(8,128)(2,1)} %shard_map.379.refs_8_), channel_id=1, source_target_pairs={{0,4},{4,0},{8,12},{12,8},{16,20},{20,16},{24,28},{28,24},{1,5},{5... | collective-permute-start | bytes 2359304 | tf_op jit(solution)/shard_map/ppermute | solution.py:510
  97.3 16.1 %collective-permute-start.26 = (bf16[208,768]{1,0:T(8,128)(2,1)S(1)}, bf16[208,768]{1,0:T(8,128)(2,1)S(1)}, u32[]{:S(2)}, u32[]{:S(2)}) collective-permute-start(bf16[208,768]{1,0:T(8,128)(2,1)S(1)} %copy-done.67), channel_id=1, source_target_pairs={{0,8},{4,12},{8,0},{12,4},{16,24},{20,28},{24,16},{28,20},{1,9},{5... | collective-permute-start | bytes 958472 | tf_op jit(solution)/shard_map/ppermute | solution.py:510
  97.7 13.5 %collective-permute-start.23 = (bf16[80,768]{1,0:T(8,128)(2,1)S(1)}, bf16[80,768]{1,0:T(8,128)(2,1)S(1)}, u32[]{:S(2)}, u32[]{:S(2)}) collective-permute-start(bf16[80,768]{1,0:T(8,128)(2,1)S(1)} %copy-done.57), channel_id=1, source_target_pairs={{0,8},{4,12},{8,0},{12,4},{16,24},{20,28},{24,16},{28,20},{1,9},{5... | collective-permute-start | bytes 368648 | tf_op jit(solution)/shard_map/ppermute | solution.py:510
  99.4 11.8 %collective-permute-start.24 = (bf16[80,768]{1,0:T(8,128)(2,1)S(1)}, bf16[80,768]{1,0:T(8,128)(2,1)S(1)}, u32[]{:S(2)}, u32[]{:S(2)}) collective-permute-start(bf16[80,768]{1,0:T(8,128)(2,1)S(1)} %copy-done.57), channel_id=1, source_target_pairs={{0,16},{4,20},{8,24},{12,28},{16,0},{20,4},{24,8},{28,12},{1,17},{... | collective-permute-start | bytes 368648 | tf_op jit(solution)/shard_map/ppermute | solution.py:510
  100.9 12.6 %collective-permute-start.25 = (bf16[80,768]{1,0:T(8,128)(2,1)S(1)}, bf16[80,768]{1,0:T(8,128)(2,1)S(1)}, u32[]{:S(2)}, u32[]{:S(2)}) collective-permute-start(bf16[80,768]{1,0:T(8,128)(2,1)S(1)} %copy-done.57), channel_id=1, source_target_pairs={{0,24},{4,28},{8,16},{12,20},{16,8},{20,12},{24,0},{28,4},{1,25},{... | collective-permute-start | bytes 368648 | tf_op jit(solution)/shard_map/ppermute | solution.py:510
  116.5 10.1 %collective-permute-start.28 = (bf16[208,768]{1,0:T(8,128)(2,1)}, bf16[208,768]{1,0:T(8,128)(2,1)S(1)}, u32[]{:S(2)}, u32[]{:S(2)}) collective-permute-start(bf16[208,768]{1,0:T(8,128)(2,1)} %shard_map.384), channel_id=1, source_target_pairs={{0,8},{4,12},{8,0},{12,4},{16,24},{20,28},{24,16},{28,20},{1,9},{5... | collective-permute-start | bytes 958472 | tf_op jit(solution)/shard_map/ppermute | solution.py:510
  129.6 13.9 %collective-permute-start.30 = (bf16[80,768]{1,0:T(8,128)(2,1)S(1)}, bf16[80,768]{1,0:T(8,128)(2,1)S(1)}, u32[]{:S(2)}, u32[]{:S(2)}) collective-permute-start(bf16[80,768]{1,0:T(8,128)(2,1)S(1)} %get-tuple-element.261), channel_id=1, source_target_pairs={{0,8},{4,12},{8,0},{12,4},{16,24},{20,28},{24,16},{28,20},{1,9},{5... | collective-permute-start | bytes 368648 | tf_op jit(solution)/shard_map/ppermute | solution.py:510
  130.2 13.3 %collective-permute-start.31 = (bf16[80,768]{1,0:T(8,128)(2,1)S(1)}, bf16[80,768]{1,0:T(8,128)(2,1)S(1)}, u32[]{:S(2)}, u32[]{:S(2)}) collective-permute-start(bf16[80,768]{1,0:T(8,128)(2,1)S(1)} %get-tuple-element.260), channel_id=1, source_target_pairs={{0,16},{4,20},{8,24},{12,28},{16,0},{20,4},{24,8},{28,12},{1,17},{... | collective-permute-start | bytes 368648 | tf_op jit(solution)/shard_map/ppermute | solution.py:510
  130.7 12.8 %collective-permute-start.32 = (bf16[80,768]{1,0:T(8,128)(2,1)S(1)}, bf16[80,768]{1,0:T(8,128)(2,1)S(1)}, u32[]{:S(2)}, u32[]{:S(2)}) collective-permute-start(bf16[80,768]{1,0:T(8,128)(2,1)S(1)} %get-tuple-element.259), channel_id=1, source_target_pairs={{0,24},{4,28},{8,16},{12,20},{16,8},{20,12},{24,0},{28,4},{1,25},{... | collective-permute-start | bytes 368648 | tf_op jit(solution)/shard_map/ppermute | solution.py:510
  144.3 15.8 %collective-permute-start.33 = (bf16[416,768]{1,0:T(8,128)(2,1)}, bf16[416,768]{1,0:T(8,128)(2,1)S(1)}, u32[]{:S(2)}, u32[]{:S(2)}) collective-permute-start(bf16[416,768]{1,0:T(8,128)(2,1)} %shard_map.390), channel_id=1, source_target_pairs={{0,8},{4,12},{8,0},{12,4},{16,24},{20,28},{24,16},{28,20},{1,9},{5... | collective-permute-start | bytes 1916936 | tf_op jit(solution)/shard_map/ppermute | solution.py:510
  160.9 3.1 collective-permute-start.34
  160.9 5.3 %collective-permute-start.35 = (bf16[4,96,1536]{2,1,0:T(8,128)(2,1)}, bf16[4,96,1536]{2,1,0:T(8,128)(2,1)S(1)}, u32[]{:S(2)}, u32[]{:S(2)}) collective-permute-start(bf16[4,96,1536]{2,1,0:T(8,128)(2,1)} %get-tuple-element.199), channel_id=1, source_target_pairs={{0,4},{4,0},{8,12},{12,8},{16,20},{20,16},{24,28},{28,24},{1,5},{5... | collective-permute-start | bytes 3538952 | tf_op jit(solution)/shard_map/ppermute | solution.py:510
  161.4 25.6 %collective-permute-start.38 = (bf16[416,768]{1,0:T(8,128)(2,1)}, bf16[416,768]{1,0:T(8,128)(2,1)S(1)}, u32[]{:S(2)}, u32[]{:S(2)}) collective-permute-start(bf16[416,768]{1,0:T(8,128)(2,1)} %get-tuple-element.201), channel_id=1, source_target_pairs={{0,8},{4,12},{8,0},{12,4},{16,24},{20,28},{24,16},{28,20},{1,9},{5... | collective-permute-start | bytes 1916936 | tf_op jit(solution)/shard_map/ppermute | solution.py:510
  162.0 25.0 %collective-permute-start.39 = (bf16[4,80,768]{2,1,0:T(8,128)(2,1)}, bf16[4,80,768]{2,1,0:T(8,128)(2,1)S(1)}, u32[]{:S(2)}, u32[]{:S(2)}) collective-permute-start(bf16[4,80,768]{2,1,0:T(8,128)(2,1)} %get-tuple-element.202), channel_id=1, source_target_pairs={{0,4},{4,0},{8,12},{12,8},{16,20},{20,16},{24,28},{28,24},{1,5},{5... | collective-permute-start | bytes 1474568 | tf_op jit(solution)/shard_map/ppermute | solution.py:510
  165.6 21.8 %collective-permute-start.36 = (bf16[384,768]{1,0:T(8,128)(2,1)S(1)}, bf16[384,768]{1,0:T(8,128)(2,1)S(1)}, u32[]{:S(2)}, u32[]{:S(2)}) collective-permute-start(bf16[384,768]{1,0:T(8,128)(2,1)S(1)} %fusion.3.refs_0_), channel_id=1, source_target_pairs={{0,16},{4,20},{8,24},{12,28},{16,0},{20,4},{24,8},{28,12},{1,17},{... | collective-permute-start | bytes 1769480 | tf_op jit(solution)/shard_map/ppermute | solution.py:510
  167.3 20.0 %collective-permute-start.37 = (bf16[96,1536]{1,0:T(8,128)(2,1)S(1)}, bf16[96,1536]{1,0:T(8,128)(2,1)S(1)}, u32[]{:S(2)}, u32[]{:S(2)}) collective-permute-start(bf16[96,1536]{1,0:T(8,128)(2,1)S(1)} %get-tuple-element.241.refs_2_), channel_id=1, source_target_pairs={{0,16},{4,20},{8,24},{12,28},{16,0},{20,4},{24,8},{28,12},{1,17},{... | collective-permute-start | bytes 884744 | tf_op jit(solution)/shard_map/ppermute | solution.py:510
  189.5 8.6 %collective-permute-start.40 = (bf16[96,1536]{1,0:T(8,128)(2,1)S(1)}, bf16[96,1536]{1,0:T(8,128)(2,1)S(1)}, u32[]{:S(2)}, u32[]{:S(2)}) collective-permute-start(bf16[96,1536]{1,0:T(8,128)(2,1)S(1)} %fusion.8), channel_id=1, source_target_pairs={{0,8},{4,12},{8,0},{12,4},{16,24},{20,28},{24,16},{28,20},{1,9},{5... | collective-permute-start | bytes 884744 | tf_op jit(solution)/shard_map/ppermute | solution.py:510
  190.1 8.2 %collective-permute-start.41 = (bf16[96,1536]{1,0:T(8,128)(2,1)S(1)}, bf16[96,1536]{1,0:T(8,128)(2,1)S(1)}, u32[]{:S(2)}, u32[]{:S(2)}) collective-permute-start(bf16[96,1536]{1,0:T(8,128)(2,1)S(1)} %copy-done.43), channel_id=1, source_target_pairs={{0,16},{4,20},{8,24},{12,28},{16,0},{20,4},{24,8},{28,12},{1,17},{... | collective-permute-start | bytes 884744 | tf_op jit(solution)/shard_map/ppermute | solution.py:510
  199.0 11.4 %collective-permute-start.42 = (bf16[4,96,1536]{2,1,0:T(8,128)(2,1)}, bf16[4,96,1536]{2,1,0:T(8,128)(2,1)S(1)}, u32[]{:S(2)}, u32[]{:S(2)}) collective-permute-start(bf16[4,96,1536]{2,1,0:T(8,128)(2,1)} %get-tuple-element.207), channel_id=1, source_target_pairs={{0,4},{4,0},{8,12},{12,8},{16,20},{20,16},{24,28},{28,24},{1,5},{5... | collective-permute-start | bytes 3538952 | tf_op jit(solution)/shard_map/ppermute | solution.py:510
  211.5 4.6 %collective-permute-start.44 = (bf16[4,96,1536]{2,1,0:T(8,128)(2,1)}, bf16[4,96,1536]{2,1,0:T(8,128)(2,1)S(1)}, u32[]{:S(2)}, u32[]{:S(2)}) collective-permute-start(bf16[4,96,1536]{2,1,0:T(8,128)(2,1)} %get-tuple-element.215), channel_id=1, source_target_pairs={{0,4},{4,0},{8,12},{12,8},{16,20},{20,16},{24,28},{28,24},{1,5},{5... | collective-permute-start | bytes 3538952 | tf_op jit(solution)/shard_map/ppermute | solution.py:510
  214.6 16.8 %collective-permute-start.43 = (bf16[2,96,1536]{2,1,0:T(8,128)(2,1)}, bf16[2,96,1536]{2,1,0:T(8,128)(2,1)S(1)}, u32[]{:S(2)}, u32[]{:S(2)}) collective-permute-start(bf16[2,96,1536]{2,1,0:T(8,128)(2,1)} %add_convert_fusion.2.refs_10_), channel_id=1, source_target_pairs={{0,8},{4,12},{8,0},{12,4},{16,24},{20,28},{24,16},{28,20},{1,9},{5... | collective-permute-start | bytes 1769480 | tf_op jit(solution)/shard_map/ppermute | solution.py:510
  218.1 14.8 %collective-permute-start.45 = (bf16[2,96,1536]{2,1,0:T(8,128)(2,1)}, bf16[2,96,1536]{2,1,0:T(8,128)(2,1)S(1)}, u32[]{:S(2)}, u32[]{:S(2)}) collective-permute-start(bf16[2,96,1536]{2,1,0:T(8,128)(2,1)} %add_convert_fusion.1.refs_11_), channel_id=1, source_target_pairs={{0,16},{4,20},{8,24},{12,28},{16,0},{20,4},{24,8},{28,12},{1,17},{... | collective-permute-start | bytes 1769480 | tf_op jit(solution)/shard_map/ppermute | solution.py:510
  231.4 99.6 %all-reduce.12.cloned.1.call-start = ((), (), s32[]{:S(2)}) async-start(), calls=%async_computation.3 | async-start | bytes 2359296 | tf_op jit(solution)/shard_map/psum | solution.py:825
  238.4 4.3 %collective-permute-start.51 = (f32[14,768]{1,0:T(8,128)S(1)}, f32[14,768]{1,0:T(8,128)S(1)}, u32[]{:S(2)}, u32[]{:S(2)}) collective-permute-start(f32[14,768]{1,0:T(8,128)S(1)} %concatenate.57), channel_id=1, source_target_pairs={{0,4},{4,0},{8,12},{12,8},{16,20},{20,16},{24,28},{28,24},{1,5},{5... | collective-permute-start | bytes 129032 | tf_op jit(solution)/shard_map/ppermute | solution.py:510
  243.3 6.3 %collective-permute-start.52 = (f32[14,768]{1,0:T(8,128)}, f32[14,768]{1,0:T(8,128)}, u32[]{:S(2)}, u32[]{:S(2)}) collective-permute-start(f32[14,768]{1,0:T(8,128)} %add.222), channel_id=1, source_target_pairs={{0,8},{4,12},{8,0},{12,4},{16,24},{20,28},{24,16},{28,20},{1,9},{5... | collective-permute-start | bytes 129032 | tf_op jit(solution)/shard_map/ppermute | solution.py:510
  248.3 9.3 %collective-permute-start.47 = (bf16[96,1536]{1,0:T(8,128)(2,1)S(1)}, bf16[96,1536]{1,0:T(8,128)(2,1)}, u32[]{:S(2)}, u32[]{:S(2)}) collective-permute-start(bf16[96,1536]{1,0:T(8,128)(2,1)S(1)} %copy-done.52), channel_id=1, source_target_pairs={{0,8},{4,12},{8,0},{12,4},{16,24},{20,28},{24,16},{28,20},{1,9},{5... | collective-permute-start | bytes 884744 | tf_op jit(solution)/shard_map/ppermute | solution.py:510
  250.5 4.2 %collective-permute-start.53 = (f32[14,768]{1,0:T(8,128)S(1)}, f32[14,768]{1,0:T(8,128)S(1)}, u32[]{:S(2)}, u32[]{:S(2)}) collective-permute-start(f32[14,768]{1,0:T(8,128)S(1)} %add.223), channel_id=1, source_target_pairs={{0,16},{4,20},{8,24},{12,28},{16,0},{20,4},{24,8},{28,12},{1,17},{... | collective-permute-start | bytes 129032 | tf_op jit(solution)/shard_map/ppermute | solution.py:510
  253.3 9.2 %collective-permute-start.46 = (bf16[96,1536]{1,0:T(8,128)(2,1)S(1)}, bf16[96,1536]{1,0:T(8,128)(2,1)}, u32[]{:S(2)}, u32[]{:S(2)}) collective-permute-start(bf16[96,1536]{1,0:T(8,128)(2,1)S(1)} %copy-done.51), channel_id=1, source_target_pairs={{0,16},{4,20},{8,24},{12,28},{16,0},{20,4},{24,8},{28,12},{1,17},{... | collective-permute-start | bytes 884744 | tf_op jit(solution)/shard_map/ppermute | solution.py:510
  258.9 24.0 %collective-permute-start.57 = (bf16[96,1536]{1,0:T(8,128)(2,1)S(1)}, bf16[96,1536]{1,0:T(8,128)(2,1)S(1)}, u32[]{:S(2)}, u32[]{:S(2)}) collective-permute-start(bf16[96,1536]{1,0:T(8,128)(2,1)S(1)} %fusion.5.refs_6_), channel_id=1, source_target_pairs={{0,1},{3,2},{4,5},{7,6},{8,9},{11,10},{12,13},{15,14},{16,17},{19,... | collective-permute-start | bytes 884744 | tf_op jit(solution)/shard_map/ppermute | solution.py:514
  264.5 14.7 %collective-permute-start.60 = (bf16[4,96,384]{2,1,0:T(8,128)(2,1)}, bf16[4,96,384]{2,1,0:T(8,128)(2,1)S(1)}, u32[]{:S(2)}, u32[]{:S(2)}) collective-permute-start(bf16[4,96,384]{2,1,0:T(8,128)(2,1)} %get-tuple-element.232), channel_id=1, source_target_pairs={{0,4},{4,0},{8,12},{12,8},{16,20},{20,16},{24,28},{28,24},{1,5},{5... | collective-permute-start | bytes 884744 | tf_op jit(solution)/shard_map/ppermute | solution.py:510
  268.1 5.8 %collective-permute-start.48 = (bf16[80,768]{1,0:T(8,128)(2,1)S(1)}, bf16[80,768]{1,0:T(8,128)(2,1)S(1)}, u32[]{:S(2)}, u32[]{:S(2)}) collective-permute-start(bf16[80,768]{1,0:T(8,128)(2,1)S(1)} %get-tuple-element.256), channel_id=1, source_target_pairs={{0,8},{4,12},{8,0},{12,4},{16,24},{20,28},{24,16},{28,20},{1,9},{5... | collective-permute-start | bytes 368648 | tf_op jit(solution)/shard_map/ppermute | solution.py:510
  269.5 7.6 %collective-permute-start.49 = (bf16[80,768]{1,0:T(8,128)(2,1)S(1)}, bf16[80,768]{1,0:T(8,128)(2,1)S(1)}, u32[]{:S(2)}, u32[]{:S(2)}) collective-permute-start(bf16[80,768]{1,0:T(8,128)(2,1)S(1)} %get-tuple-element.258), channel_id=1, source_target_pairs={{0,16},{4,20},{8,24},{12,28},{16,0},{20,4},{24,8},{28,12},{1,17},{... | collective-permute-start | bytes 368648 | tf_op jit(solution)/shard_map/ppermute | solution.py:510
  270.5 6.6 %collective-permute-start.50 = (bf16[80,768]{1,0:T(8,128)(2,1)S(1)}, bf16[80,768]{1,0:T(8,128)(2,1)S(1)}, u32[]{:S(2)}, u32[]{:S(2)}) collective-permute-start(bf16[80,768]{1,0:T(8,128)(2,1)S(1)} %get-tuple-element.257), channel_id=1, source_target_pairs={{0,24},{4,28},{8,16},{12,20},{16,8},{20,12},{24,0},{28,4},{1,25},{... | collective-permute-start | bytes 368648 | tf_op jit(solution)/shard_map/ppermute | solution.py:510
  273.8 13.9 %collective-permute-start.54 = (bf16[104,1536]{1,0:T(8,128)(2,1)S(1)}, bf16[104,1536]{1,0:T(8,128)(2,1)S(1)}, u32[]{:S(2)}, u32[]{:S(2)}) collective-permute-start(bf16[104,1536]{1,0:T(8,128)(2,1)S(1)} %pad_maximum_fusion.7), channel_id=1, source_target_pairs={{0,1},{3,2},{4,5},{7,6},{8,9},{11,10},{12,13},{15,14},{16,17},{19,... | collective-permute-start | bytes 958472 | tf_op jit(solution)/shard_map/ppermute | solution.py:514
  279.4 9.1 %collective-permute-start.61 = (bf16[96,768]{1,0:T(8,128)(2,1)S(1)}, bf16[96,768]{1,0:T(8,128)(2,1)S(1)}, u32[]{:S(2)}, u32[]{:S(2)}) collective-permute-start(bf16[96,768]{1,0:T(8,128)(2,1)S(1)} %get-tuple-element.251), channel_id=1, source_target_pairs={{0,8},{4,12},{8,0},{12,4},{16,24},{20,28},{24,16},{28,20},{1,9},{5... | collective-permute-start | bytes 442376 | tf_op jit(solution)/shard_map/ppermute | solution.py:510
  279.8 8.7 %collective-permute-start.62 = (bf16[96,768]{1,0:T(8,128)(2,1)S(1)}, bf16[96,768]{1,0:T(8,128)(2,1)S(1)}, u32[]{:S(2)}, u32[]{:S(2)}) collective-permute-start(bf16[96,768]{1,0:T(8,128)(2,1)S(1)} %get-tuple-element.253), channel_id=1, source_target_pairs={{0,16},{4,20},{8,24},{12,28},{16,0},{20,4},{24,8},{28,12},{1,17},{... | collective-permute-start | bytes 442376 | tf_op jit(solution)/shard_map/ppermute | solution.py:510
  280.8 7.7 %collective-permute-start.63 = (bf16[96,768]{1,0:T(8,128)(2,1)S(1)}, bf16[96,768]{1,0:T(8,128)(2,1)S(1)}, u32[]{:S(2)}, u32[]{:S(2)}) collective-permute-start(bf16[96,768]{1,0:T(8,128)(2,1)S(1)} %get-tuple-element.252), channel_id=1, source_target_pairs={{0,24},{4,28},{8,16},{12,20},{16,8},{20,12},{24,0},{28,4},{1,25},{... | collective-permute-start | bytes 442376 | tf_op jit(solution)/shard_map/ppermute | solution.py:510
  283.0 6.7 %collective-permute-start.58 = (bf16[96,1536]{1,0:T(8,128)(2,1)S(1)}, bf16[96,1536]{1,0:T(8,128)(2,1)S(1)}, u32[]{:S(2)}, u32[]{:S(2)}) collective-permute-start(bf16[96,1536]{1,0:T(8,128)(2,1)S(1)} %add_convert_fusion.9), channel_id=1, source_target_pairs={{1,2},{2,1},{5,6},{6,5},{9,10},{10,9},{13,14},{14,13},{17,18},{18,... | collective-permute-start | bytes 884744 | tf_op jit(solution)/shard_map/ppermute | solution.py:514
  287.8 3.3 collective-permute-start.55
  289.8 31.1 %collective-permute-start.59 = (bf16[96,1536]{1,0:T(8,128)(2,1)S(1)}, bf16[96,1536]{1,0:T(8,128)(2,1)S(1)}, u32[]{:S(2)}, u32[]{:S(2)}) collective-permute-start(bf16[96,1536]{1,0:T(8,128)(2,1)S(1)} %add_convert_fusion.8), channel_id=1, source_target_pairs={{1,0},{2,3},{5,4},{6,7},{9,8},{10,11},{13,12},{14,15},{17,16},{18,... | collective-permute-start | bytes 884744 | tf_op jit(solution)/shard_map/ppermute | solution.py:514
  291.2 38.4 %collective-permute-start.56 = (bf16[104,1536]{1,0:T(8,128)(2,1)S(1)}, bf16[104,1536]{1,0:T(8,128)(2,1)S(1)}, u32[]{:S(2)}, u32[]{:S(2)}) collective-permute-start(bf16[104,1536]{1,0:T(8,128)(2,1)S(1)} %add_convert_fusion.6), channel_id=1, source_target_pairs={{1,0},{2,3},{5,4},{6,7},{9,8},{10,11},{13,12},{14,15},{17,16},{18,... | collective-permute-start | bytes 958472 | tf_op jit(solution)/shard_map/ppermute | solution.py:514
  (97 other events, 274.8 us)
Sparse Core Ops, SparseCore 0:
  38.4 30.7 all-gather.3
  71.4 22.6 all-gather.5
  191.0 57.3 all-reduce.9
  250.6 77.6 all-reduce.11

commit v2 on v1

--- a/solution.py
+++ b/solution.py
@@ -15,7 +15,7 @@
 VMEM_LIMIT = 58 * 1024 * 1024
 
 ITEM = 256
-SCALE = 0.3
+SCALE = 0.35
 TEXT_AT = 208
 
 

time: 348 us -> 347 us (level)
    unnamed x193 -> x187, local copies, waits for them, and re-layouts: 25.8 us -> 26.3 us
  transfers between devices with their start and end apart: 68 -> 68, of which waited for: 21 -> 20; matrix products, arithmetic and copies ran while one was open for 15% -> 15% of each run, Pallas kernels for 33% -> 33%
where the time goes in v2:
time: 347 us; the launch traced here: 342 us
  Pallas kernels  114 us (33%)
  waiting for transfers between devices  75.7 us (22%)
  starting transfers between devices  56 us (16%)
  local copies, waits for them, and re-layouts  40.7 us (12%)
  other arithmetic  39.7 us (11%)
  between operations  15.2 us (4%)
    pallas_call x14, Pallas kernels, call(): pl.pallas_call(kernel, out_shape=[jax.ShapeDtypeStruct(s, d) for s, d in...  114 us
    ppermute x58, starting transfers between devices, swap(): return lax.ppermute(array, 'fsdp', [(i, i ^ mask) for i in range(8)])  45.4 us
    ppermute x6, waiting for transfers between devices, along_rep(): return lax.ppermute(array, 'rep', pairs)  40.5 us
    ppermute x58, waiting for transfers between devices, swap(): return lax.ppermute(array, 'fsdp', [(i, i ^ mask) for i in range(8)])  29 us
    unnamed x187, local copies, waits for them, and re-layouts  26.3 us
    convert_element_type x16, other arithmetic, add(): return out.astype(BF)  18.1 us
    ppermute x6, starting transfers between devices, along_rep(): return lax.ppermute(array, 'rep', pairs)  10.5 us
  transfers between devices with their start and end apart: 68, of which 20 were waited for; matrix products, arithmetic and copies ran while one was open for 15% of the time, Pallas kernels for 33%

profile of v2, /device:TPU:0, one launch (start us, length us, event | category | flops | bytes accessed | tf_op | source)
XLA Modules:
  0.0 341.8 jit_solution(3790193079632895050)
XLA Ops:
  7.3 3.0 collective-permute-start.4
  10.3 1.5 collective-permute-start.5
  11.8 1.5 stack.97
  14.6 2.9 collective-permute-start.2
  17.5 2.1 copy.119.tokens
  21.1 4.3 %shard_map.365 = (bf16[512,768]{1,0:T(8,128)(2,1)}, bf16[512,768]{1,0:T(8,128)(2,1)}, bf16[416,768]{1,0:T(8,128)(2,1)}, bf16[80,768]{1,0:T(8,128)(2,1)}, f32[2,7...) custom-call(s32[4]{0:T(128)} %pad_add_fusion.info, ...), custom_call_target="tpu_custom_call" | custom-call | flops 1924999936 | bytes 1750000 | tf_op jit(solution)/shard_map/pallas_call | solution.py:498
  30.9 4.7 %shard_map.368 = (bf16[512,768]{1,0:T(8,128)(2,1)}, f32[16,768]{1,0:T(8,128)}, f32[1,1536]{1,0:T(1,128)}) custom-call(s32[4]{0:T(128)} %pad_add_fusion.info, bf16[512,768]{1,0:T(8,128)(2,1)} %get-tuple-element.127.refs_2_.tok, f32[512,1]{1,0:T(8,128)} %bitcast.127, bf16[4,16,128]{2,1,0:T(8,128)(2,1)} %shard_map.366.even, bf16[4,16,128]{2,1,0:T(8,128)(2,1)} %copy-done.79, ...), custom_call_target="tpu_custom_call" | custom-call | flops 1924999936 | bytes 1750000 | tf_op jit(solution)/shard_map/pallas_call | solution.py:498
  35.6 1.4 collective-permute-done.6.refs_0_
  39.4 1.6 collective-permute-start.18
  41.8 8.0 %shard_map.370.refs_1_.qkv = bf16[512,2304]{1,0:T(8,128)(2,1)} custom-call(s32[4]{0:T(128)} %pad_add_fusion.info, bf16[512,768]{1,0:T(8,128)(2,1)} %get-tuple-element.131.refs_5_.n1.left, f32[16,768]{1,0:T(8,128)} %get-tuple-element.130.vec, bf16[96,2304]{1,0:T(8,128)(2,1)} %refs_0_.3, bf16[96,2304]{1,0:T(8,128)(2,1)} %copy-done.76, ...), custom_call_target="tpu_custom_call" | custom-call | flops 3080000000 | bytes 2800000 | tf_op jit(solution)/shard_map/pallas_call | solution.py:498
  54.7 1.5 collective-permute-start.17
  56.2 11.4 %shard_map.372 = (bf16[12,512,256]{2,1,0:T(8,128)(2,1)}, bf16[512,768]{1,0:T(8,128)(2,1)}) custom-call(s32[4]{0:T(128)} %pad_add_fusion.info, bf16[512,2304]{1,0:T(8,128)(2,1)} %shard_map.370.refs_1_.qkv, f32[8,128]{1,0:T(8,128)} %shard_map.371.refs_0_.refs_4_), custom_call_target="tpu_custom_call" | custom-call | flops 3849999872 | bytes 3500000 | tf_op jit(solution)/shard_map/pallas_call | solution.py:498
  67.6 4.5 %collective-permute-done.17.refs_5_.refs_3_ = bf16[176,768]{1,0:T(8,128)(2,1)S(1)} collective-permute-done((bf16[176,768]{1,0:T(8,128)(2,1)S(1)}, bf16[176,768]{1,0:T(8,128)(2,1)S(1)}, u32[]{:S(2)}, u32[]{:S(2)}) %collective-permute-start.17) | collective-permute-done | bytes 270368 | tf_op jit(solution)/shard_map/ppermute | solution.py:510
  72.1 5.8 %collective-permute-done.14.refs_2_.refs_0_ = bf16[2,96,1536]{2,1,0:T(8,128)(2,1)S(1)} collective-permute-done((bf16[2,96,1536]{2,1,0:T(8,128)(2,1)S(1)}, bf16[2,96,1536]{2,1,0:T(8,128)(2,1)S(1)}, u32[]{:S(2)}, u32[]{:S(2)}) %collective-permute-start.14) | collective-permute-done | bytes 589856 | tf_op jit(solution)/shard_map/ppermute | solution.py:510
  80.0 1.2 pad_maximum_fusion.1.refs_6_
  81.8 1.6 collective-permute-start.19
  83.4 4.5 %shard_map.375 = (f32[512,768]{1,0:T(8,128)}, bf16[80,768]{1,0:T(8,128)(2,1)}, bf16[208,768]{1,0:T(8,128)(2,1)}, bf16[208,768]{1,0:T(8,128)(2,1)}) custom-call(s32[4]{0:T(128)} %pad_add_fusion.info, bf16[512,768]{1,0:T(8,128)(2,1)} %get-tuple-element.127.refs_2_.tok, f32[512,1]{1,0:T(8,128)} %bitcast.128, f32[16,768]{1,0:T(8,128)} %get-tuple-element.130.vec, ...), custom_call_target="tpu_custom_call" | custom-call | flops 1924999936 | bytes 1750000 | tf_op jit(solution)/shard_map/pallas_call | solution.py:498
  87.9 6.2 %all-gather.6.cloned.1.call-done = bf16[832,768]{1,0:T(8,128)(2,1)} async-done(((bf16[416,768]{1,0:T(8,128)(2,1)}), bf16[832,768]{1,0:T(8,128)(2,1)}) %all-gather.6.cloned.1.call-update) | async-done | bytes 1277968 | tf_op jit(solution)/shard_map/all_gather | solution.py:631
  95.1 2.2 shard_map.379.refs_8_
  97.7 1.7 collective-permute-start.24
  99.4 1.5 collective-permute-start.25
  101.2 10.0 %shard_map.380 = (f32[416,768]{1,0:T(8,128)}, f32[416,768]{1,0:T(8,128)}, bf16[416,1536]{1,0:T(8,128)(2,1)}, bf16[416,1536]{1,0:T(8,128)(2,1)}) custom-call(s32[4]{0:T(128)} %pad_add_fusion.info, bf16[416,768]{1,0:T(8,128)(2,1)} %get-tuple-element.150.grad, f32[1,1536]{1,0:T(1,128)} %get-tuple-element.151.up_bias, ...), custom_call_target="tpu_custom_call" | custom-call | flops 3464999936 | bytes 3150000 | tf_op jit(solution)/shard_map/pallas_call | solution.py:498
  111.3 1.3 collective-permute-done.26.refs_5_.refs_2_.refs_1_
  117.5 6.3 %shard_map.383 = (bf16[4,80,768]{2,1,0:T(8,128)(2,1)}, bf16[4,80,768]{2,1,0:T(8,128)(2,1)}, bf16[4,80,768]{2,1,0:T(8,128)(2,1)}, bf16[4,80,768]{2,1,0:T(8,128)(2...) custom-call(s32[4]{0:T(128)} %pad_add_fusion.info, ...), custom_call_target="tpu_custom_call" | custom-call | flops 2309999872 | bytes 2099999 | tf_op jit(solution)/shard_map/pallas_call | solution.py:498
  123.8 1.9 collective-permute-done.28.refs_3_.refs_2_
  126.5 2.1 collective-permute-done.29
  129.2 1.6 collective-permute-start.31
  130.8 1.5 collective-permute-start.32
  132.2 10.3 %shard_map.387 = (bf16[416,768]{1,0:T(8,128)(2,1)}, bf16[416,768]{1,0:T(8,128)(2,1)}, bf16[416,1536]{1,0:T(8,128)(2,1)}, bf16[416,1536]{1,0:T(8,128)(2,1)}) custom-call(s32[4]{0:T(128)} %pad_add_fusion.info, bf16[2,416,768]{2,1,0:T(8,128)(2,1)} %bitcast.119, f32[1,1536]{1,0:T(1,128)} %get-tuple-element.151.up_bias, ...), custom_call_target="tpu_custom_call" | custom-call | flops 3464999936 | bytes 3150000 | tf_op jit(solution)/shard_map/pallas_call | solution.py:498
  143.8 12.3 %shard_map.389 = (bf16[4,96,1536]{2,1,0:T(8,128)(2,1)}, bf16[4,96,1536]{2,1,0:T(8,128)(2,1)}, bf16[2,384,768]{2,1,0:T(8,128)(2,1)}, bf16[2,384,768]{2,1,0:T(8,128)(2,1)}, f32[1,1536]{1,0:T(1,128)}) custom-call(s32[4]{0:T(128)} %pad_add_fusion.info, bf16[208,768]{1,0:T(8,128)(2,1)} %get-tuple-element.161.refs_0_, ...), custom_call_target="tpu_custom_call" | custom-call | flops 4619999744 | bytes 4199999 | tf_op jit(solution)/shard_map/pallas_call | solution.py:498
  156.2 3.0 collective-permute-done.33.refs_2_.refs_4_
  161.0 2.2 collective-permute-done.35
  163.2 1.9 fusion.10
  165.1 1.4 collective-permute-start.37
  166.5 1.4 fusion.3.refs_0_
  168.7 18.1 %shard_map.393 = (f32[512,768]{1,0:T(8,128)}, bf16[512,768]{1,0:T(8,128)(2,1)}, bf16[512,2304]{1,0:T(8,128)(2,1)}, f32[8,768]{1,0:T(8,128)}) custom-call(s32[4]{0:T(128)} %pad_add_fusion.info, f32[416,768]{1,0:T(8,128)} %get-tuple-element.170.refs_1_.gn2v, bf16[416,768]{1,0:T(8,128)(2,1)} %get-tuple-element.193.gn2x, bf16[4,80,768]{2,1,0:T(8,128)(2,1)} %copy-done.39, ...), custom_call_target="tpu_custom_call" | custom-call | flops 6929999872 | bytes 6300000 | tf_op jit(solution)/shard_map/pallas_call | solution.py:498
  190.0 1.3 collective-permute-start.41
  191.5 5.3 %shard_map.395 = (bf16[4,96,1536]{2,1,0:T(8,128)(2,1)}, bf16[4,96,1536]{2,1,0:T(8,128)(2,1)}) custom-call(s32[4]{0:T(128)} %pad_add_fusion.info, bf16[512,768]{1,0:T(8,128)(2,1)} %get-tuple-element.131.refs_5_.n1.left, bf16[512,2304]{1,0:T(8,128)(2,1)} %get-tuple-element.200.refs_1_.refs_0_.refs_2_.stacked, f32[8,128]{1,0:T(8,128)} %shard_map.394.refs_1_.refs_4_.refs_0_), custom_call_target="tpu_custom_call" | custom-call | flops 1924999936 | bytes 1750000 | tf_op jit(solution)/shard_map/pallas_call | solution.py:498
  196.8 1.4 collective-permute-done.40.refs_2_.refs_1_
  200.2 1.9 add_convert_fusion.4.refs_2_
  202.2 2.4 fusion.2.refs_13_
  204.6 5.3 %shard_map.399 = (bf16[4,96,1536]{2,1,0:T(8,128)(2,1)}, bf16[4,96,1536]{2,1,0:T(8,128)(2,1)}) custom-call(s32[4]{0:T(128)} %pad_add_fusion.info, bf16[512,768]{1,0:T(8,128)(2,1)} %get-tuple-element.131.refs_5_.n1.left, bf16[512,768]{1,0:T(8,128)(2,1)} %get-tuple-element.139.refs_1_.ctx.refs_0_, bf16[512,768]{1,0:T(8,128)(2,1)} %get-tuple-element.208.refs_1_, ...), custom_call_target="tpu_custom_call" | custom-call | flops 1924999936 | bytes 1750000 | tf_op jit(solution)/shard_map/pallas_call | solution.py:498
  214.0 1.4 collective-permute-start.43
  219.3 11.5 %shard_map.402 = (f32[512,768]{1,0:T(8,128)}, f32[8,768]{1,0:T(8,128)}) custom-call(s32[4]{0:T(128)} %pad_add_fusion.info, bf16[512,2304]{1,0:T(8,128)(2,1)} %get-tuple-element.200.refs_1_.refs_0_.refs_2_.stacked, f32[512,768]{1,0:T(8,128)} %get-tuple-element.216.gh1, bf16[512,768]{1,0:T(8,128)(2,1)} %get-tuple-element.127.refs_2_.tok, f32[512,1]{1,0:T(8,128)} %bitcast.129, ...), custom_call_target="tpu_custom_call" | custom-call | flops 4619999744 | bytes 4199999 | tf_op jit(solution)/shard_map/pallas_call | solution.py:498
  233.0 1.9 fusion.11.refs_1_
  235.0 1.8 fusion.12.refs_2_
  238.5 2.4 slice.331
  243.5 1.4 slice.345
  244.9 1.7 slice.346
  250.8 1.7 pad_maximum_fusion
  254.2 2.8 collective-permute-done.47
  257.0 1.3 fusion.5.refs_6_
  258.3 3.7 %collective-permute-start.57 = (bf16[96,1536]{1,0:T(8,128)(2,1)S(1)}, bf16[96,1536]{1,0:T(8,128)(2,1)S(1)}, u32[]{:S(2)}, u32[]{:S(2)}) collective-permute-start(bf16[96,1536]{1,0:T(8,128)(2,1)S(1)} %fusion.5.refs_6_), channel_id=1, source_target_pairs={{0,1},{3,2},{4,5},{7,6},{8,9},{11,10},{12,13},{15,14},{16,17},{19,... | collective-permute-start | bytes 884744 | tf_op jit(solution)/shard_map/ppermute | solution.py:514
  262.0 1.9 fusion.6.refs_5_
  267.5 1.2 collective-permute-start.48
  269.7 1.3 collective-permute-start.50
  273.4 2.9 collective-permute-start.54
  276.6 1.8 pad_maximum_fusion.3
  280.4 1.8 collective-permute-start.63
  282.9 4.6 %collective-permute-done.54 = bf16[104,1536]{1,0:T(8,128)(2,1)S(1)} collective-permute-done((bf16[104,1536]{1,0:T(8,128)(2,1)S(1)}, bf16[104,1536]{1,0:T(8,128)(2,1)S(1)}, u32[]{:S(2)}, u32[]{:S(2)}) %collective-permute-start.54) | collective-permute-done | bytes 319520 | tf_op jit(solution)/shard_map/ppermute | solution.py:514
  289.6 1.3 collective-permute-start.59
  291.0 1.3 collective-permute-start.56
  292.3 28.3 %collective-permute-done.59 = bf16[96,1536]{1,0:T(8,128)(2,1)S(1)} collective-permute-done((bf16[96,1536]{1,0:T(8,128)(2,1)S(1)}, bf16[96,1536]{1,0:T(8,128)(2,1)S(1)}, u32[]{:S(2)}, u32[]{:S(2)}) %collective-permute-start.59) | collective-permute-done | bytes 294944 | tf_op jit(solution)/shard_map/ppermute | solution.py:514
  321.4 7.7 %collective-permute-done.56 = bf16[104,1536]{1,0:T(8,128)(2,1)S(1)} collective-permute-done((bf16[104,1536]{1,0:T(8,128)(2,1)S(1)}, bf16[104,1536]{1,0:T(8,128)(2,1)S(1)}, u32[]{:S(2)}, u32[]{:S(2)}) %collective-permute-start.56) | collective-permute-done | bytes 319520 | tf_op jit(solution)/shard_map/ppermute | solution.py:514
  (394 shorter events, 75.1 us)
Async XLA Ops:
  7.2 76.1 %all-gather.4.cloned.1.call-start = ((), (), s32[]{:S(2)}) async-start(), calls=%async_computation | async-start | bytes 1327104 | tf_op jit(solution)/shard_map/all_gather | solution.py:629
  7.3 18.7 %collective-permute-start.4 = (bf16[96,2304]{1,0:T(8,128)(2,1)}, bf16[96,2304]{1,0:T(8,128)(2,1)S(1)}, u32[]{:S(2)}, u32[]{:S(2)}) collective-permute-start(bf16[96,2304]{1,0:T(8,128)(2,1)} %refs_0_.3), channel_id=1, source_target_pairs={{0,8},{4,12},{8,0},{12,4},{16,24},{20,28},{24,16},{28,20},{1,9},{5... | collective-permute-start | bytes 1327112 | tf_op jit(solution)/shard_map/ppermute | solution.py:510
  10.3 15.2 %collective-permute-start.5 = (bf16[96,2304]{1,0:T(8,128)(2,1)}, bf16[96,2304]{1,0:T(8,128)(2,1)S(1)}, u32[]{:S(2)}, u32[]{:S(2)}) collective-permute-start(bf16[96,2304]{1,0:T(8,128)(2,1)} %refs_0_.3), channel_id=1, source_target_pairs={{0,16},{4,20},{8,24},{12,28},{16,0},{20,4},{24,8},{28,12},{1,17},{... | collective-permute-start | bytes 1327112 | tf_op jit(solution)/shard_map/ppermute | solution.py:510
  14.0 11.4 %collective-permute-start = (bf16[1,16,128]{2,1,0:T(8,128)(2,1)S(1)}, bf16[1,16,128]{2,1,0:T(8,128)(2,1)S(1)}, u32[]{:S(2)}, u32[]{:S(2)}) collective-permute-start(bf16[1,16,128]{2,1,0:T(8,128)(2,1)S(1)} %pad_bitcast_fusion), channel_id=1, source_target_pairs={{0,8},{4,12},{8,0},{12,4},{16,24},{20,28},{24,16},{28,20},{1,9},{5... | collective-permute-start | bytes 12296 | tf_op jit(solution)/shard_map/ppermute | solution.py:510
  14.6 11.5 %collective-permute-start.1 = (bf16[1,16,128]{2,1,0:T(8,128)(2,1)S(1)}, bf16[1,16,128]{2,1,0:T(8,128)(2,1)S(1)}, u32[]{:S(2)}, u32[]{:S(2)}) collective-permute-start(bf16[1,16,128]{2,1,0:T(8,128)(2,1)S(1)} %pad_bitcast_fusion), channel_id=1, source_target_pairs={{0,16},{4,20},{8,24},{12,28},{16,0},{20,4},{24,8},{28,12},{1,17},{... | collective-permute-start | bytes 12296 | tf_op jit(solution)/shard_map/ppermute | solution.py:510
  14.6 11.5 %collective-permute-start.2 = (bf16[1,16,128]{2,1,0:T(8,128)(2,1)S(1)}, bf16[1,16,128]{2,1,0:T(8,128)(2,1)S(1)}, u32[]{:S(2)}, u32[]{:S(2)}) collective-permute-start(bf16[1,16,128]{2,1,0:T(8,128)(2,1)S(1)} %pad_bitcast_fusion), channel_id=1, source_target_pairs={{0,24},{4,28},{8,16},{12,20},{16,8},{20,12},{24,0},{28,4},{1,25},{... | collective-permute-start | bytes 12296 | tf_op jit(solution)/shard_map/ppermute | solution.py:510
  25.4 10.2 %collective-permute-start.8 = (bf16[96,2304]{1,0:T(8,128)(2,1)S(1)}, bf16[96,2304]{1,0:T(8,128)(2,1)S(1)}, u32[]{:S(2)}, u32[]{:S(2)}) collective-permute-start(bf16[96,2304]{1,0:T(8,128)(2,1)S(1)} %copy-done.87), channel_id=1, source_target_pairs={{0,4},{4,0},{8,12},{12,8},{16,20},{20,16},{24,28},{28,24},{1,5},{5... | collective-permute-start | bytes 1327112 | tf_op jit(solution)/shard_map/ppermute | solution.py:510
  25.5 11.8 %collective-permute-start.10 = (bf16[96,2304]{1,0:T(8,128)(2,1)S(1)}, bf16[96,2304]{1,0:T(8,128)(2,1)S(1)}, u32[]{:S(2)}, u32[]{:S(2)}) collective-permute-start(bf16[96,2304]{1,0:T(8,128)(2,1)S(1)} %collective-permute-done.5.refs_2_), channel_id=1, source_target_pairs={{0,4},{4,0},{8,12},{12,8},{16,20},{20,16},{24,28},{28,24},{1,5},{5... | collective-permute-start | bytes 1327112 | tf_op jit(solution)/shard_map/ppermute | solution.py:510
  26.0 11.3 %collective-permute-start.9 = (bf16[96,2304]{1,0:T(8,128)(2,1)S(1)}, bf16[96,2304]{1,0:T(8,128)(2,1)S(1)}, u32[]{:S(2)}, u32[]{:S(2)}) collective-permute-start(bf16[96,2304]{1,0:T(8,128)(2,1)S(1)} %collective-permute-done.4.refs_1_), channel_id=1, source_target_pairs={{0,4},{4,0},{8,12},{12,8},{16,20},{20,16},{24,28},{28,24},{1,5},{5... | collective-permute-start | bytes 1327112 | tf_op jit(solution)/shard_map/ppermute | solution.py:510
  29.4 7.7 %collective-permute-start.6 = (bf16[48,2304]{1,0:T(8,128)(2,1)}, bf16[48,2304]{1,0:T(8,128)(2,1)S(1)}, u32[]{:S(2)}, u32[]{:S(2)}) collective-permute-start(bf16[48,2304]{1,0:T(8,128)(2,1)} %get-tuple-element.129.refs_0_), channel_id=1, source_target_pairs={{0,16},{4,20},{8,24},{12,28},{16,0},{20,4},{24,8},{28,12},{1,17},{... | collective-permute-start | bytes 663560 | tf_op jit(solution)/shard_map/ppermute | solution.py:510
  29.9 7.4 %collective-permute-start.7 = (bf16[48,2304]{1,0:T(8,128)(2,1)}, bf16[48,2304]{1,0:T(8,128)(2,1)S(1)}, u32[]{:S(2)}, u32[]{:S(2)}) collective-permute-start(bf16[48,2304]{1,0:T(8,128)(2,1)} %get-tuple-element.132), channel_id=1, source_target_pairs={{0,8},{4,12},{8,0},{12,4},{16,24},{20,28},{24,16},{28,20},{1,9},{5... | collective-permute-start | bytes 663560 | tf_op jit(solution)/shard_map/ppermute | solution.py:510
  38.3 55.7 %all-gather.6.cloned.1.call-start = ((), (), s32[]{:S(2)}) async-start(), calls=%async_computation.1 | async-start | bytes 1916928 | tf_op jit(solution)/shard_map/all_gather | solution.py:631
  38.4 2.6 collective-permute-start.11
  38.9 10.8 %collective-permute-start.13 = (bf16[96,1536]{1,0:T(8,128)(2,1)}, bf16[96,1536]{1,0:T(8,128)(2,1)S(1)}, u32[]{:S(2)}, u32[]{:S(2)}) collective-permute-start(bf16[96,1536]{1,0:T(8,128)(2,1)} %get-tuple-element.138), channel_id=1, source_target_pairs={{0,8},{4,12},{8,0},{12,4},{16,24},{20,28},{24,16},{28,20},{1,9},{5... | collective-permute-start | bytes 884744 | tf_op jit(solution)/shard_map/ppermute | solution.py:510
  39.4 32.6 %collective-permute-start.18 = (bf16[384,768]{1,0:T(8,128)(2,1)}, bf16[384,768]{1,0:T(8,128)(2,1)S(1)}, u32[]{:S(2)}, u32[]{:S(2)}) collective-permute-start(bf16[384,768]{1,0:T(8,128)(2,1)} %get-tuple-element.148), channel_id=1, source_target_pairs={{0,16},{4,20},{8,24},{12,28},{16,0},{20,4},{24,8},{28,12},{1,17},{... | collective-permute-start | bytes 1769480 | tf_op jit(solution)/shard_map/ppermute | solution.py:510
  52.5 25.4 %collective-permute-start.14 = (bf16[2,96,1536]{2,1,0:T(8,128)(2,1)S(1)}, bf16[2,96,1536]{2,1,0:T(8,128)(2,1)S(1)}, u32[]{:S(2)}, u32[]{:S(2)}) collective-permute-start(bf16[2,96,1536]{2,1,0:T(8,128)(2,1)S(1)} %pad_maximum_fusion.4.refs_2_), channel_id=1, source_target_pairs={{0,16},{4,20},{8,24},{12,28},{16,0},{20,4},{24,8},{28,12},{1,17},{... | collective-permute-start | bytes 1769480 | tf_op jit(solution)/shard_map/ppermute | solution.py:510
  53.4 24.5 %collective-permute-start.15 = (bf16[2,96,1536]{2,1,0:T(8,128)(2,1)S(1)}, bf16[2,96,1536]{2,1,0:T(8,128)(2,1)S(1)}, u32[]{:S(2)}, u32[]{:S(2)}) collective-permute-start(bf16[2,96,1536]{2,1,0:T(8,128)(2,1)S(1)} %pad_maximum_fusion.4.refs_2_), channel_id=1, source_target_pairs={{0,4},{4,0},{8,12},{12,8},{16,20},{20,16},{24,28},{28,24},{1,5},{5... | collective-permute-start | bytes 1769480 | tf_op jit(solution)/shard_map/ppermute | solution.py:510
  53.4 210.5 %all-reduce.10.cloned.1.call-start = ((), (), s32[]{:S(2)}) async-start(), calls=%async_computation.2 | async-start | bytes 2359296 | tf_op jit(solution)/shard_map/psum | solution.py:749
  53.5 14.1 %collective-permute-start.16 = (bf16[176,768]{1,0:T(8,128)(2,1)S(1)}, bf16[176,768]{1,0:T(8,128)(2,1)S(1)}, u32[]{:S(2)}, u32[]{:S(2)}) collective-permute-start(bf16[176,768]{1,0:T(8,128)(2,1)S(1)} %copy-done.67), channel_id=1, source_target_pairs={{0,8},{4,12},{8,0},{12,4},{16,24},{20,28},{24,16},{28,20},{1,9},{5... | collective-permute-start | bytes 811016 | tf_op jit(solution)/shard_map/ppermute | solution.py:510
  54.7 17.4 %collective-permute-start.17 = (bf16[176,768]{1,0:T(8,128)(2,1)S(1)}, bf16[176,768]{1,0:T(8,128)(2,1)S(1)}, u32[]{:S(2)}, u32[]{:S(2)}) collective-permute-start(bf16[176,768]{1,0:T(8,128)(2,1)S(1)} %copy-done.68), channel_id=1, source_target_pairs={{0,24},{4,28},{8,16},{12,20},{16,8},{20,12},{24,0},{28,4},{1,25},{... | collective-permute-start | bytes 811016 | tf_op jit(solution)/shard_map/ppermute | solution.py:510
  81.2 12.8 %collective-permute-start.21 = (bf16[2,384,768]{2,1,0:T(8,128)(2,1)S(1)}, bf16[2,384,768]{2,1,0:T(8,128)(2,1)S(1)}, u32[]{:S(2)}, u32[]{:S(2)}) collective-permute-start(bf16[2,384,768]{2,1,0:T(8,128)(2,1)S(1)} %pad_maximum_fusion.1.refs_6_), channel_id=1, source_target_pairs={{0,4},{4,0},{8,12},{12,8},{16,20},{20,16},{24,28},{28,24},{1,5},{5... | collective-permute-start | bytes 3538952 | tf_op jit(solution)/shard_map/ppermute | solution.py:510
  81.3 12.7 %collective-permute-start.20 = (bf16[2,96,1536]{2,1,0:T(8,128)(2,1)S(1)}, bf16[2,96,1536]{2,1,0:T(8,128)(2,1)}, u32[]{:S(2)}, u32[]{:S(2)}) collective-permute-start(bf16[2,96,1536]{2,1,0:T(8,128)(2,1)S(1)} %copy-done.37), channel_id=1, source_target_pairs={{0,4},{4,0},{8,12},{12,8},{16,20},{20,16},{24,28},{28,24},{1,5},{5... | collective-permute-start | bytes 1769480 | tf_op jit(solution)/shard_map/ppermute | solution.py:510
  81.8 12.2 %collective-permute-start.19 = (bf16[176,768]{1,0:T(8,128)(2,1)}, bf16[176,768]{1,0:T(8,128)(2,1)S(1)}, u32[]{:S(2)}, u32[]{:S(2)}) collective-permute-start(bf16[176,768]{1,0:T(8,128)(2,1)} %get-tuple-element.154), channel_id=1, source_target_pairs={{0,16},{4,20},{8,24},{12,28},{16,0},{20,4},{24,8},{28,12},{1,17},{... | collective-permute-start | bytes 811016 | tf_op jit(solution)/shard_map/ppermute | solution.py:510
  97.3 15.3 %collective-permute-start.22 = (bf16[512,768]{1,0:T(8,128)(2,1)}, bf16[512,768]{1,0:T(8,128)(2,1)S(1)}, u32[]{:S(2)}, u32[]{:S(2)}) collective-permute-start(bf16[512,768]{1,0:T(8,128)(2,1)} %shard_map.379.refs_8_), channel_id=1, source_target_pairs={{0,4},{4,0},{8,12},{12,8},{16,20},{20,16},{24,28},{28,24},{1,5},{5... | collective-permute-start | bytes 2359304 | tf_op jit(solution)/shard_map/ppermute | solution.py:510
  97.3 13.9 %collective-permute-start.23 = (bf16[80,768]{1,0:T(8,128)(2,1)S(1)}, bf16[80,768]{1,0:T(8,128)(2,1)S(1)}, u32[]{:S(2)}, u32[]{:S(2)}) collective-permute-start(bf16[80,768]{1,0:T(8,128)(2,1)S(1)} %copy-done.54), channel_id=1, source_target_pairs={{0,8},{4,12},{8,0},{12,4},{16,24},{20,28},{24,16},{28,20},{1,9},{5... | collective-permute-start | bytes 368648 | tf_op jit(solution)/shard_map/ppermute | solution.py:510
  97.7 13.5 %collective-permute-start.24 = (bf16[80,768]{1,0:T(8,128)(2,1)S(1)}, bf16[80,768]{1,0:T(8,128)(2,1)S(1)}, u32[]{:S(2)}, u32[]{:S(2)}) collective-permute-start(bf16[80,768]{1,0:T(8,128)(2,1)S(1)} %copy-done.54), channel_id=1, source_target_pairs={{0,16},{4,20},{8,24},{12,28},{16,0},{20,4},{24,8},{28,12},{1,17},{... | collective-permute-start | bytes 368648 | tf_op jit(solution)/shard_map/ppermute | solution.py:510
  99.4 11.8 %collective-permute-start.25 = (bf16[80,768]{1,0:T(8,128)(2,1)S(1)}, bf16[80,768]{1,0:T(8,128)(2,1)S(1)}, u32[]{:S(2)}, u32[]{:S(2)}) collective-permute-start(bf16[80,768]{1,0:T(8,128)(2,1)S(1)} %copy-done.54), channel_id=1, source_target_pairs={{0,24},{4,28},{8,16},{12,20},{16,8},{20,12},{24,0},{28,4},{1,25},{... | collective-permute-start | bytes 368648 | tf_op jit(solution)/shard_map/ppermute | solution.py:510
  100.9 11.7 %collective-permute-start.26 = (bf16[208,768]{1,0:T(8,128)(2,1)S(1)}, bf16[208,768]{1,0:T(8,128)(2,1)S(1)}, u32[]{:S(2)}, u32[]{:S(2)}) collective-permute-start(bf16[208,768]{1,0:T(8,128)(2,1)S(1)} %copy-done.64), channel_id=1, source_target_pairs={{0,8},{4,12},{8,0},{12,4},{16,24},{20,28},{24,16},{28,20},{1,9},{5... | collective-permute-start | bytes 958472 | tf_op jit(solution)/shard_map/ppermute | solution.py:510
  115.6 10.1 %collective-permute-start.28 = (bf16[208,768]{1,0:T(8,128)(2,1)}, bf16[208,768]{1,0:T(8,128)(2,1)S(1)}, u32[]{:S(2)}, u32[]{:S(2)}) collective-permute-start(bf16[208,768]{1,0:T(8,128)(2,1)} %shard_map.384), channel_id=1, source_target_pairs={{0,8},{4,12},{8,0},{12,4},{16,24},{20,28},{24,16},{28,20},{1,9},{5... | collective-permute-start | bytes 958472 | tf_op jit(solution)/shard_map/ppermute | solution.py:510
  128.7 13.9 %collective-permute-start.30 = (bf16[80,768]{1,0:T(8,128)(2,1)S(1)}, bf16[80,768]{1,0:T(8,128)(2,1)S(1)}, u32[]{:S(2)}, u32[]{:S(2)}) collective-permute-start(bf16[80,768]{1,0:T(8,128)(2,1)S(1)} %get-tuple-element.261), channel_id=1, source_target_pairs={{0,8},{4,12},{8,0},{12,4},{16,24},{20,28},{24,16},{28,20},{1,9},{5... | collective-permute-start | bytes 368648 | tf_op jit(solution)/shard_map/ppermute | solution.py:510
  129.2 13.4 %collective-permute-start.31 = (bf16[80,768]{1,0:T(8,128)(2,1)S(1)}, bf16[80,768]{1,0:T(8,128)(2,1)S(1)}, u32[]{:S(2)}, u32[]{:S(2)}) collective-permute-start(bf16[80,768]{1,0:T(8,128)(2,1)S(1)} %get-tuple-element.260), channel_id=1, source_target_pairs={{0,16},{4,20},{8,24},{12,28},{16,0},{20,4},{24,8},{28,12},{1,17},{... | collective-permute-start | bytes 368648 | tf_op jit(solution)/shard_map/ppermute | solution.py:510
  130.8 11.8 %collective-permute-start.32 = (bf16[80,768]{1,0:T(8,128)(2,1)S(1)}, bf16[80,768]{1,0:T(8,128)(2,1)S(1)}, u32[]{:S(2)}, u32[]{:S(2)}) collective-permute-start(bf16[80,768]{1,0:T(8,128)(2,1)S(1)} %get-tuple-element.259), channel_id=1, source_target_pairs={{0,24},{4,28},{8,16},{12,20},{16,8},{20,12},{24,0},{28,4},{1,25},{... | collective-permute-start | bytes 368648 | tf_op jit(solution)/shard_map/ppermute | solution.py:510
  143.3 15.8 %collective-permute-start.33 = (bf16[416,768]{1,0:T(8,128)(2,1)}, bf16[416,768]{1,0:T(8,128)(2,1)S(1)}, u32[]{:S(2)}, u32[]{:S(2)}) collective-permute-start(bf16[416,768]{1,0:T(8,128)(2,1)} %shard_map.390), channel_id=1, source_target_pairs={{0,8},{4,12},{8,0},{12,4},{16,24},{20,28},{24,16},{28,20},{1,9},{5... | collective-permute-start | bytes 1916936 | tf_op jit(solution)/shard_map/ppermute | solution.py:510
  160.0 3.2 collective-permute-start.35
  160.0 6.5 %collective-permute-start.34 = (bf16[2,384,768]{2,1,0:T(8,128)(2,1)}, bf16[2,384,768]{2,1,0:T(8,128)(2,1)}, u32[]{:S(2)}, u32[]{:S(2)}) collective-permute-start(bf16[2,384,768]{2,1,0:T(8,128)(2,1)} %get-tuple-element.197), channel_id=1, source_target_pairs={{0,4},{4,0},{8,12},{12,8},{16,20},{20,16},{24,28},{28,24},{1,5},{5... | collective-permute-start | bytes 3538952 | tf_op jit(solution)/shard_map/ppermute | solution.py:510
  160.5 26.3 %collective-permute-start.38 = (bf16[416,768]{1,0:T(8,128)(2,1)}, bf16[416,768]{1,0:T(8,128)(2,1)S(1)}, u32[]{:S(2)}, u32[]{:S(2)}) collective-permute-start(bf16[416,768]{1,0:T(8,128)(2,1)} %get-tuple-element.201), channel_id=1, source_target_pairs={{0,8},{4,12},{8,0},{12,4},{16,24},{20,28},{24,16},{28,20},{1,9},{5... | collective-permute-start | bytes 1916936 | tf_op jit(solution)/shard_map/ppermute | solution.py:510
  161.0 25.9 %collective-permute-start.39 = (bf16[4,80,768]{2,1,0:T(8,128)(2,1)}, bf16[4,80,768]{2,1,0:T(8,128)(2,1)S(1)}, u32[]{:S(2)}, u32[]{:S(2)}) collective-permute-start(bf16[4,80,768]{2,1,0:T(8,128)(2,1)} %get-tuple-element.202), channel_id=1, source_target_pairs={{0,4},{4,0},{8,12},{12,8},{16,20},{20,16},{24,28},{28,24},{1,5},{5... | collective-permute-start | bytes 1474568 | tf_op jit(solution)/shard_map/ppermute | solution.py:510
  165.1 21.8 %collective-permute-start.37 = (bf16[96,1536]{1,0:T(8,128)(2,1)S(1)}, bf16[96,1536]{1,0:T(8,128)(2,1)S(1)}, u32[]{:S(2)}, u32[]{:S(2)}) collective-permute-start(bf16[96,1536]{1,0:T(8,128)(2,1)S(1)} %get-tuple-element.241.refs_2_), channel_id=1, source_target_pairs={{0,16},{4,20},{8,24},{12,28},{16,0},{20,4},{24,8},{28,12},{1,17},{... | collective-permute-start | bytes 884744 | tf_op jit(solution)/shard_map/ppermute | solution.py:510
  167.9 19.0 %collective-permute-start.36 = (bf16[384,768]{1,0:T(8,128)(2,1)S(1)}, bf16[384,768]{1,0:T(8,128)(2,1)S(1)}, u32[]{:S(2)}, u32[]{:S(2)}) collective-permute-start(bf16[384,768]{1,0:T(8,128)(2,1)S(1)} %fusion.3.refs_0_), channel_id=1, source_target_pairs={{0,16},{4,20},{8,24},{12,28},{16,0},{20,4},{24,8},{28,12},{1,17},{... | collective-permute-start | bytes 1769480 | tf_op jit(solution)/shard_map/ppermute | solution.py:510
  189.3 8.8 %collective-permute-start.40 = (bf16[96,1536]{1,0:T(8,128)(2,1)S(1)}, bf16[96,1536]{1,0:T(8,128)(2,1)S(1)}, u32[]{:S(2)}, u32[]{:S(2)}) collective-permute-start(bf16[96,1536]{1,0:T(8,128)(2,1)S(1)} %fusion.8), channel_id=1, source_target_pairs={{0,8},{4,12},{8,0},{12,4},{16,24},{20,28},{24,16},{28,20},{1,9},{5... | collective-permute-start | bytes 884744 | tf_op jit(solution)/shard_map/ppermute | solution.py:510
  190.0 8.5 %collective-permute-start.41 = (bf16[96,1536]{1,0:T(8,128)(2,1)S(1)}, bf16[96,1536]{1,0:T(8,128)(2,1)S(1)}, u32[]{:S(2)}, u32[]{:S(2)}) collective-permute-start(bf16[96,1536]{1,0:T(8,128)(2,1)S(1)} %copy-done.43), channel_id=1, source_target_pairs={{0,16},{4,20},{8,24},{12,28},{16,0},{20,4},{24,8},{28,12},{1,17},{... | collective-permute-start | bytes 884744 | tf_op jit(solution)/shard_map/ppermute | solution.py:510
  199.2 10.7 %collective-permute-start.42 = (bf16[4,96,1536]{2,1,0:T(8,128)(2,1)}, bf16[4,96,1536]{2,1,0:T(8,128)(2,1)S(1)}, u32[]{:S(2)}, u32[]{:S(2)}) collective-permute-start(bf16[4,96,1536]{2,1,0:T(8,128)(2,1)} %get-tuple-element.207), channel_id=1, source_target_pairs={{0,4},{4,0},{8,12},{12,8},{16,20},{20,16},{24,28},{28,24},{1,5},{5... | collective-permute-start | bytes 3538952 | tf_op jit(solution)/shard_map/ppermute | solution.py:510
  210.9 4.5 %collective-permute-start.44 = (bf16[4,96,1536]{2,1,0:T(8,128)(2,1)}, bf16[4,96,1536]{2,1,0:T(8,128)(2,1)S(1)}, u32[]{:S(2)}, u32[]{:S(2)}) collective-permute-start(bf16[4,96,1536]{2,1,0:T(8,128)(2,1)} %get-tuple-element.215), channel_id=1, source_target_pairs={{0,4},{4,0},{8,12},{12,8},{16,20},{20,16},{24,28},{28,24},{1,5},{5... | collective-permute-start | bytes 3538952 | tf_op jit(solution)/shard_map/ppermute | solution.py:510
  214.0 16.9 %collective-permute-start.43 = (bf16[2,96,1536]{2,1,0:T(8,128)(2,1)}, bf16[2,96,1536]{2,1,0:T(8,128)(2,1)S(1)}, u32[]{:S(2)}, u32[]{:S(2)}) collective-permute-start(bf16[2,96,1536]{2,1,0:T(8,128)(2,1)} %add_convert_fusion.2.refs_10_), channel_id=1, source_target_pairs={{0,8},{4,12},{8,0},{12,4},{16,24},{20,28},{24,16},{28,20},{1,9},{5... | collective-permute-start | bytes 1769480 | tf_op jit(solution)/shard_map/ppermute | solution.py:510
  217.4 14.7 %collective-permute-start.45 = (bf16[2,96,1536]{2,1,0:T(8,128)(2,1)}, bf16[2,96,1536]{2,1,0:T(8,128)(2,1)S(1)}, u32[]{:S(2)}, u32[]{:S(2)}) collective-permute-start(bf16[2,96,1536]{2,1,0:T(8,128)(2,1)} %add_convert_fusion.1.refs_11_), channel_id=1, source_target_pairs={{0,16},{4,20},{8,24},{12,28},{16,0},{20,4},{24,8},{28,12},{1,17},{... | collective-permute-start | bytes 1769480 | tf_op jit(solution)/shard_map/ppermute | solution.py:510
  230.8 99.7 %all-reduce.12.cloned.1.call-start = ((), (), s32[]{:S(2)}) async-start(), calls=%async_computation.3 | async-start | bytes 2359296 | tf_op jit(solution)/shard_map/psum | solution.py:825
  237.6 4.3 %collective-permute-start.51 = (f32[14,768]{1,0:T(8,128)S(1)}, f32[14,768]{1,0:T(8,128)S(1)}, u32[]{:S(2)}, u32[]{:S(2)}) collective-permute-start(f32[14,768]{1,0:T(8,128)S(1)} %concatenate.57), channel_id=1, source_target_pairs={{0,4},{4,0},{8,12},{12,8},{16,20},{20,16},{24,28},{28,24},{1,5},{5... | collective-permute-start | bytes 129032 | tf_op jit(solution)/shard_map/ppermute | solution.py:510
  242.6 6.3 %collective-permute-start.52 = (f32[14,768]{1,0:T(8,128)}, f32[14,768]{1,0:T(8,128)}, u32[]{:S(2)}, u32[]{:S(2)}) collective-permute-start(f32[14,768]{1,0:T(8,128)} %add.222), channel_id=1, source_target_pairs={{0,8},{4,12},{8,0},{12,4},{16,24},{20,28},{24,16},{28,20},{1,9},{5... | collective-permute-start | bytes 129032 | tf_op jit(solution)/shard_map/ppermute | solution.py:510
  247.7 9.3 %collective-permute-start.47 = (bf16[96,1536]{1,0:T(8,128)(2,1)S(1)}, bf16[96,1536]{1,0:T(8,128)(2,1)}, u32[]{:S(2)}, u32[]{:S(2)}) collective-permute-start(bf16[96,1536]{1,0:T(8,128)(2,1)S(1)} %copy-done.49), channel_id=1, source_target_pairs={{0,8},{4,12},{8,0},{12,4},{16,24},{20,28},{24,16},{28,20},{1,9},{5... | collective-permute-start | bytes 884744 | tf_op jit(solution)/shard_map/ppermute | solution.py:510
  249.7 4.2 %collective-permute-start.53 = (f32[14,768]{1,0:T(8,128)S(1)}, f32[14,768]{1,0:T(8,128)S(1)}, u32[]{:S(2)}, u32[]{:S(2)}) collective-permute-start(f32[14,768]{1,0:T(8,128)S(1)} %add.223), channel_id=1, source_target_pairs={{0,16},{4,20},{8,24},{12,28},{16,0},{20,4},{24,8},{28,12},{1,17},{... | collective-permute-start | bytes 129032 | tf_op jit(solution)/shard_map/ppermute | solution.py:510
  252.6 9.4 %collective-permute-start.46 = (bf16[96,1536]{1,0:T(8,128)(2,1)S(1)}, bf16[96,1536]{1,0:T(8,128)(2,1)}, u32[]{:S(2)}, u32[]{:S(2)}) collective-permute-start(bf16[96,1536]{1,0:T(8,128)(2,1)S(1)} %copy-done.48), channel_id=1, source_target_pairs={{0,16},{4,20},{8,24},{12,28},{16,0},{20,4},{24,8},{28,12},{1,17},{... | collective-permute-start | bytes 884744 | tf_op jit(solution)/shard_map/ppermute | solution.py:510
  258.3 23.9 %collective-permute-start.57 = (bf16[96,1536]{1,0:T(8,128)(2,1)S(1)}, bf16[96,1536]{1,0:T(8,128)(2,1)S(1)}, u32[]{:S(2)}, u32[]{:S(2)}) collective-permute-start(bf16[96,1536]{1,0:T(8,128)(2,1)S(1)} %fusion.5.refs_6_), channel_id=1, source_target_pairs={{0,1},{3,2},{4,5},{7,6},{8,9},{11,10},{12,13},{15,14},{16,17},{19,... | collective-permute-start | bytes 884744 | tf_op jit(solution)/shard_map/ppermute | solution.py:514
  263.9 14.5 %collective-permute-start.60 = (bf16[4,96,384]{2,1,0:T(8,128)(2,1)}, bf16[4,96,384]{2,1,0:T(8,128)(2,1)S(1)}, u32[]{:S(2)}, u32[]{:S(2)}) collective-permute-start(bf16[4,96,384]{2,1,0:T(8,128)(2,1)} %get-tuple-element.232), channel_id=1, source_target_pairs={{0,4},{4,0},{8,12},{12,8},{16,20},{20,16},{24,28},{28,24},{1,5},{5... | collective-permute-start | bytes 884744 | tf_op jit(solution)/shard_map/ppermute | solution.py:510
  267.5 6.0 %collective-permute-start.48 = (bf16[80,768]{1,0:T(8,128)(2,1)S(1)}, bf16[80,768]{1,0:T(8,128)(2,1)S(1)}, u32[]{:S(2)}, u32[]{:S(2)}) collective-permute-start(bf16[80,768]{1,0:T(8,128)(2,1)S(1)} %get-tuple-element.256), channel_id=1, source_target_pairs={{0,8},{4,12},{8,0},{12,4},{16,24},{20,28},{24,16},{28,20},{1,9},{5... | collective-permute-start | bytes 368648 | tf_op jit(solution)/shard_map/ppermute | solution.py:510
  268.7 7.6 %collective-permute-start.49 = (bf16[80,768]{1,0:T(8,128)(2,1)S(1)}, bf16[80,768]{1,0:T(8,128)(2,1)S(1)}, u32[]{:S(2)}, u32[]{:S(2)}) collective-permute-start(bf16[80,768]{1,0:T(8,128)(2,1)S(1)} %get-tuple-element.258), channel_id=1, source_target_pairs={{0,16},{4,20},{8,24},{12,28},{16,0},{20,4},{24,8},{28,12},{1,17},{... | collective-permute-start | bytes 368648 | tf_op jit(solution)/shard_map/ppermute | solution.py:510
  269.7 6.6 %collective-permute-start.50 = (bf16[80,768]{1,0:T(8,128)(2,1)S(1)}, bf16[80,768]{1,0:T(8,128)(2,1)S(1)}, u32[]{:S(2)}, u32[]{:S(2)}) collective-permute-start(bf16[80,768]{1,0:T(8,128)(2,1)S(1)} %get-tuple-element.257), channel_id=1, source_target_pairs={{0,24},{4,28},{8,16},{12,20},{16,8},{20,12},{24,0},{28,4},{1,25},{... | collective-permute-start | bytes 368648 | tf_op jit(solution)/shard_map/ppermute | solution.py:510
  273.4 14.0 %collective-permute-start.54 = (bf16[104,1536]{1,0:T(8,128)(2,1)S(1)}, bf16[104,1536]{1,0:T(8,128)(2,1)S(1)}, u32[]{:S(2)}, u32[]{:S(2)}) collective-permute-start(bf16[104,1536]{1,0:T(8,128)(2,1)S(1)} %pad_maximum_fusion.7), channel_id=1, source_target_pairs={{0,1},{3,2},{4,5},{7,6},{8,9},{11,10},{12,13},{15,14},{16,17},{19,... | collective-permute-start | bytes 958472 | tf_op jit(solution)/shard_map/ppermute | solution.py:514
  278.6 9.7 %collective-permute-start.61 = (bf16[96,768]{1,0:T(8,128)(2,1)S(1)}, bf16[96,768]{1,0:T(8,128)(2,1)S(1)}, u32[]{:S(2)}, u32[]{:S(2)}) collective-permute-start(bf16[96,768]{1,0:T(8,128)(2,1)S(1)} %get-tuple-element.251), channel_id=1, source_target_pairs={{0,8},{4,12},{8,0},{12,4},{16,24},{20,28},{24,16},{28,20},{1,9},{5... | collective-permute-start | bytes 442376 | tf_op jit(solution)/shard_map/ppermute | solution.py:510
  279.4 8.9 %collective-permute-start.62 = (bf16[96,768]{1,0:T(8,128)(2,1)S(1)}, bf16[96,768]{1,0:T(8,128)(2,1)S(1)}, u32[]{:S(2)}, u32[]{:S(2)}) collective-permute-start(bf16[96,768]{1,0:T(8,128)(2,1)S(1)} %get-tuple-element.253), channel_id=1, source_target_pairs={{0,16},{4,20},{8,24},{12,28},{16,0},{20,4},{24,8},{28,12},{1,17},{... | collective-permute-start | bytes 442376 | tf_op jit(solution)/shard_map/ppermute | solution.py:510
  280.4 8.0 %collective-permute-start.63 = (bf16[96,768]{1,0:T(8,128)(2,1)S(1)}, bf16[96,768]{1,0:T(8,128)(2,1)S(1)}, u32[]{:S(2)}, u32[]{:S(2)}) collective-permute-start(bf16[96,768]{1,0:T(8,128)(2,1)S(1)} %get-tuple-element.252), channel_id=1, source_target_pairs={{0,24},{4,28},{8,16},{12,20},{16,8},{20,12},{24,0},{28,4},{1,25},{... | collective-permute-start | bytes 442376 | tf_op jit(solution)/shard_map/ppermute | solution.py:510
  282.2 7.3 %collective-permute-start.58 = (bf16[96,1536]{1,0:T(8,128)(2,1)S(1)}, bf16[96,1536]{1,0:T(8,128)(2,1)S(1)}, u32[]{:S(2)}, u32[]{:S(2)}) collective-permute-start(bf16[96,1536]{1,0:T(8,128)(2,1)S(1)} %add_convert_fusion.9), channel_id=1, source_target_pairs={{1,2},{2,1},{5,6},{6,5},{9,10},{10,9},{13,14},{14,13},{17,18},{18,... | collective-permute-start | bytes 884744 | tf_op jit(solution)/shard_map/ppermute | solution.py:514
  287.6 3.3 collective-permute-start.55
  289.6 31.0 %collective-permute-start.59 = (bf16[96,1536]{1,0:T(8,128)(2,1)S(1)}, bf16[96,1536]{1,0:T(8,128)(2,1)S(1)}, u32[]{:S(2)}, u32[]{:S(2)}) collective-permute-start(bf16[96,1536]{1,0:T(8,128)(2,1)S(1)} %add_convert_fusion.8), channel_id=1, source_target_pairs={{1,0},{2,3},{5,4},{6,7},{9,8},{10,11},{13,12},{14,15},{17,16},{18,... | collective-permute-start | bytes 884744 | tf_op jit(solution)/shard_map/ppermute | solution.py:514
  291.0 38.1 %collective-permute-start.56 = (bf16[104,1536]{1,0:T(8,128)(2,1)S(1)}, bf16[104,1536]{1,0:T(8,128)(2,1)S(1)}, u32[]{:S(2)}, u32[]{:S(2)}) collective-permute-start(bf16[104,1536]{1,0:T(8,128)(2,1)S(1)} %add_convert_fusion.6), channel_id=1, source_target_pairs={{1,0},{2,3},{5,4},{6,7},{9,8},{10,11},{13,12},{14,15},{17,16},{18,... | collective-permute-start | bytes 958472 | tf_op jit(solution)/shard_map/ppermute | solution.py:514
  (94 other events, 272.3 us)
Sparse Core Ops, SparseCore 0:
  38.4 30.7 all-gather.3
  71.4 22.6 all-gather.5
  191.4 56.6 all-reduce.9
  250.5 77.4 all-reduce.11
